TPU v7x, 32 devices: a whole 2x2x4 slice. The times are simulated.
32 devices in a mesh: peer: 8 (over z, x), group: 4 (over y, core).
Axes of the slice: x: 2, y: 2, z: 4, core: 2. Of those that a mesh axis runs over, the one named last changes fastest.
Arguments:
- view_descriptors: bfloat16 [3072, 1536], P('peer'), may hold values from -6 to 6
- embedding_matrix: bfloat16 [1536, 1536], replicated, may hold values from -0.15625 to 0.15625
- picture_of_view: int32 [3072], P('peer'), may hold values from 0 to 6143
- filled_view_places: int32 [8], P('peer'), may hold values from 96 to 384, as said below
- companion_masks: int32 [4], P('group'), may hold values from 1 to 7, as said below
- score_scale: float32 [1], replicated, may hold values from 4 to 16
- score_shift: float32 [1], replicated, may hold values from -4 to -1
Outputs:
- projector_grad: float32 [12288, 1536], P('peer', 'group')
- block_loss: float32 [8, 4], P('peer', 'group')
Inputs may be any that keep to these rules, and one draw needn't show every extreme that they name: `companion_masks`: entries are distinct partner masks from 1 to 6 in random order, and one of them is replaced by the largest mask 7. `filled_view_places`: some block is full.
All inputs are finite; a program needn't handle non-finite values.
Results may differ from a plain program's by a relative error of at most 0.0049.
Values may be sent and summed in bfloat16 or wider, within the bound.
No kernel may reach another device: no remote copies, remote signals or barrier semaphores. Data moves between devices by JAX's collectives and lax.ppermute only.
A program may use at most 64 MiB of HBM per device.

v0:
```python
import jax
import jax.numpy as jnp
from jax import lax
from jax.sharding import PartitionSpec as P


def partner(block, axis, distance):
    count = lax.axis_size(axis)
    route = []
    for low in range(count):
        high = low | 1 << distance
        if high != low and high < count:
            route += [(low, high), (high, low)]
    return lax.ppermute(block, axis, route)


def project(view_descriptors, embedding_matrix):
    raw = jnp.dot(view_descriptors, embedding_matrix, preferred_element_type=jnp.float32)
    row_length = jnp.sqrt(jnp.sum(raw * raw, axis=1, keepdims=True) + 1e-06)
    return (raw / row_length, row_length)


def square_extent(
    self_reduced_vectors,
    self_identities,
    views_per_device,
    companion_normed_part,
    remote_identities,
    companion_views,
    scale_scalar,
    shift_scalar,
):
    similarity_matrix = lax.dot_general(
        self_reduced_vectors,
        companion_normed_part,
        (((1,), (1,)), ((), ())),
        preferred_element_type=jnp.float32,
    )
    row_image_index = jnp.arange(self_reduced_vectors.shape[0], dtype=jnp.int32)
    col_ids = jnp.arange(companion_normed_part.shape[0], dtype=jnp.int32)
    valid_flags = (row_image_index[:, None] < views_per_device) & (
        col_ids[None, :] < companion_views
    )
    target_signs = jnp.where(
        self_identities[:, None] == remote_identities[None, :], 1.0, -1.0
    ).astype(jnp.float32)
    multiplied_scores = scale_scalar * similarity_matrix + shift_scalar
    couple_penalty = jnp.sum(
        jnp.where(valid_flags, jax.nn.softplus(-target_signs * multiplied_scores), 0.0)
    )
    sigmoid_derivatives = jnp.where(
        valid_flags,
        -target_signs * jax.nn.sigmoid(-target_signs * multiplied_scores) * scale_scalar,
        0.0,
    ).astype(jnp.bfloat16)
    return (
        couple_penalty,
        jnp.dot(sigmoid_derivatives, companion_normed_part, preferred_element_type=jnp.float32),
    )


def on_device(
    view_descriptors,
    embedding_matrix,
    picture_of_view,
    filled_view_places,
    companion_masks,
    score_scale,
    score_shift,
):
    unit_rows, row_length = project(view_descriptors, embedding_matrix)
    self_reduced_vectors = unit_rows.astype(jnp.bfloat16)
    scale_scalar = score_scale[0]
    shift_scalar = score_shift[0]
    levels = lax.axis_size("peer").bit_length() - 1
    bit_list = list(range(levels))
    current = (self_reduced_vectors, picture_of_view, filled_view_places)
    for bit_pos in bit_list:
        arrived = partner((current[0], current[1], current[2]), "peer", bit_pos)
        chosen = jnp.bitwise_and(jnp.right_shift(companion_masks[0], bit_pos), 1) == 1
        current = (
            jnp.where(chosen, arrived[0], current[0]),
            jnp.where(chosen, arrived[1], current[1]),
            jnp.where(chosen, arrived[2], current[2]),
        )
    fetched = (current[0], current[1], current[2][0])
    couple_penalty, derivative_matrix = square_extent(
        self_reduced_vectors,
        picture_of_view,
        filled_view_places[0],
        fetched[0],
        fetched[1],
        fetched[2],
        scale_scalar,
        shift_scalar,
    )
    rows_here = self_reduced_vectors.shape[0]
    block_loss = (couple_penalty / (rows_here * rows_here)).reshape(1, 1)
    tangent = (
        derivative_matrix
        - unit_rows * jnp.sum(unit_rows * derivative_matrix, axis=1, keepdims=True)
    ) / row_length
    summed = lax.psum_scatter(tangent, "group", scatter_dimension=1, tiled=True)
    projector_grad = lax.dot_general(
        view_descriptors,
        summed.astype(jnp.bfloat16),
        (((0,), (0,)), ((), ())),
        preferred_element_type=jnp.float32,
    )
    return (projector_grad, block_loss)


def solution(mesh):
    placed = (P("peer", None), P(), P("peer"), P("peer"), P("group"), P(), P())
    return jax.shard_map(
        on_device,
        mesh=mesh,
        in_specs=placed,
        out_specs=(P("peer", "group"), P("peer", "group")),
        check_vma=False,
    )
```

profile of v0, /device:TPU:0, one launch (start us, length us, event | category | flops | bytes accessed | tf_op | source)
XLA Modules:
  0.0 178.3 jit_solution(13202257988445417675)
XLA Ops:
  7.2 0.0 copy-start
  7.2 0.0 reduce-scatter.2.cloned.1.call-start
  7.2 1.2 copy-done
  8.4 4.4 %multiply_reduce_fusion.1 = (f32[384]{0:T(512)S(1)}, f32[384,1536]{1,0:T(8,128)S(1)}) fusion(bf16[384,1536]{1,0:T(8,128)(2,1)S(1)} %copy-done, bf16[1536,1536]{1,0:T(8,128)(2,1)} %param.8), kind=kOutput, calls=%fused_computation.3 | convolution fusion | flops 1813118592 | bytes 8259072 | tf_op jit(solution)/shard_map/dot_general | solution.py:18
  12.9 0.3 fusion.18
  13.2 3.0 %collective-permute-start.6 = (bf16[384,1536]{1,0:T(8,128)(2,1)S(1)}, bf16[384,1536]{1,0:T(8,128)(2,1)S(1)}, u32[]{:S(2)}, u32[]{:S(2)}) collective-permute-start(bf16[384,1536]{1,0:T(8,128)(2,1)S(1)} %fusion.18), channel_id=1, source_target_pairs={{0,4},{4,0},{8,12},{12,8},{16,20},{20,16},{24,28},{28,24},{1,5},{5... | collective-permute-start | bytes 3538952 | tf_op jit(solution)/shard_map/ppermute | solution.py:14
  16.9 25.3 %collective-permute-done.6 = bf16[384,1536]{1,0:T(8,128)(2,1)S(1)} collective-permute-done((bf16[384,1536]{1,0:T(8,128)(2,1)S(1)}, bf16[384,1536]{1,0:T(8,128)(2,1)S(1)}, u32[]{:S(2)}, u32[]{:S(2)}) %collective-permute-start.6) | collective-permute-done | bytes 1179680 | tf_op jit(solution)/shard_map/ppermute | solution.py:14
  42.2 0.5 broadcast_select_fusion
  42.7 1.9 %collective-permute-start.7 = (bf16[384,1536]{1,0:T(8,128)(2,1)S(1)}, bf16[384,1536]{1,0:T(8,128)(2,1)S(1)}, u32[]{:S(2)}, u32[]{:S(2)}) collective-permute-start(bf16[384,1536]{1,0:T(8,128)(2,1)S(1)} %broadcast_select_fusion), channel_id=1, source_target_pairs={{0,8},{8,0},{4,12},{12,4},{16,24},{24,16},{20,28},{28,20},{1,9},{9... | collective-permute-start | bytes 3538952 | tf_op jit(solution)/shard_map/ppermute | solution.py:14
  44.6 25.3 %collective-permute-done.7 = bf16[384,1536]{1,0:T(8,128)(2,1)S(1)} collective-permute-done((bf16[384,1536]{1,0:T(8,128)(2,1)S(1)}, bf16[384,1536]{1,0:T(8,128)(2,1)S(1)}, u32[]{:S(2)}, u32[]{:S(2)}) %collective-permute-start.7) | collective-permute-done | bytes 1179680 | tf_op jit(solution)/shard_map/ppermute | solution.py:14
  69.9 0.0 copy-start.1
  69.9 0.1 broadcast_select_fusion.1
  70.0 2.6 %collective-permute-start.8 = (bf16[384,1536]{1,0:T(8,128)(2,1)S(1)}, bf16[384,1536]{1,0:T(8,128)(2,1)S(1)}, u32[]{:S(2)}, u32[]{:S(2)}) collective-permute-start(bf16[384,1536]{1,0:T(8,128)(2,1)S(1)} %broadcast_select_fusion.1), channel_id=1, source_target_pairs={{0,16},{16,0},{4,20},{20,4},{8,24},{24,8},{12,28},{28,12},{1,17},{... | collective-permute-start | bytes 3538952 | tf_op jit(solution)/shard_map/ppermute | solution.py:14
  72.6 0.0 copy-done.1
  72.6 1.5 collective-permute-start.3
  74.1 0.5 collective-permute-start
  75.3 0.9 collective-permute-done.3
  76.2 1.6 collective-permute-start.4
  79.1 0.0 collective-permute-done
  79.8 16.4 %collective-permute-start.1 = (s32[1]{0:T(128)}, s32[1]{0:T(128)}, u32[]{:S(2)}, u32[]{:S(2)}) collective-permute-start(s32[1]{0:T(128)} %select_n.69), channel_id=1, source_target_pairs={{0,8},{8,0},{4,12},{12,4},{16,24},{24,16},{20,28},{28,20},{1,9},{9... | collective-permute-start | bytes 20 | tf_op jit(solution)/shard_map/ppermute | solution.py:14
  96.2 0.0 collective-permute-done.1
  96.9 3.7 %collective-permute-start.2 = (s32[1]{0:T(128)}, s32[1]{0:T(128)}, u32[]{:S(2)}, u32[]{:S(2)}) collective-permute-start(s32[1]{0:T(128)} %select_n.70), channel_id=1, source_target_pairs={{0,16},{16,0},{4,20},{20,4},{8,24},{24,8},{12,28},{28,12},{1,17},{... | collective-permute-start | bytes 20 | tf_op jit(solution)/shard_map/ppermute | solution.py:14
  100.6 22.0 %collective-permute-done.2 = s32[1]{0:T(128)} collective-permute-done((s32[1]{0:T(128)}, s32[1]{0:T(128)}, u32[]{:S(2)}, u32[]{:S(2)}) %collective-permute-start.2) | collective-permute-done | bytes 36 | tf_op jit(solution)/shard_map/ppermute | solution.py:14
  123.2 0.0 collective-permute-done.4
  123.3 0.1 collective-permute-start.5
  123.3 4.5 %collective-permute-done.5 = s32[384]{0:T(512)S(1)} collective-permute-done((s32[384]{0:T(512)S(1)}, s32[384]{0:T(512)S(1)}, u32[]{:S(2)}, u32[]{:S(2)}) %collective-permute-start.5) | collective-permute-done | bytes 1568 | tf_op jit(solution)/shard_map/ppermute | solution.py:14
  127.8 0.0 collective-permute-done.8
  127.8 1.8 %fusion.3 = (f32[]{:T(128)}, f32[384,384]{1,0:T(8,128)S(1)}) fusion(pred[384]{0:T(512)(128)(4,1)S(1)} %iota_compare_fusion, pred[384]{0:T(512)(128)(4,1)S(1)} %iota_compare_fusion.1, f32[]{:T(128)} %bitcast.17, bf16[384,1536]{1,0:T(8,128)(2,1)S(1)} %fusion.18, bf16[384,1536]{1,0:T(8,128)(2,1)S(1)} %collective-permute-done.8, ...), kind=kOutput, calls=%fused_computation.15 | convolution fusion | flops 455786496 | bytes 4132621 | tf_op jit(solution)/shard_map/dot_general | solution.py:33
  129.6 1.1 multiply_reduce_fusion
  130.7 1.8 %subtract_divide_fusion = f32[384,1536]{1,0:T(8,128)} fusion(f32[384,1536]{1,0:T(8,128)S(1)} %get-tuple-element.7, f32[384]{0:T(512)S(1)} %get-tuple-element.6, f32[384]{0:T(512)S(1)} %add_sqrt_fusion, f32[384,1536]{1,0:T(8,128)S(1)} %get-tuple-element.5), kind=kLoop, calls=%fused_computation.1 | loop fusion | flops 2359296 | bytes 7080960 | tf_op jit(solution)/shard_map/div | solution.py:99
  132.5 0.0 reduce-scatter.2.cloned.1.call-update
  133.2 33.3 %reduce-scatter.2.cloned.1.call-done = f32[384,384]{1,0:T(8,128)} async-done(((f32[384,1536]{1,0:T(8,128)}), f32[384,384]{1,0:T(8,128)}) %reduce-scatter.2.cloned.1.call-update) | async-done | bytes 589840 | tf_op jit(solution)/shard_map/reduce_scatter | solution.py:103
  166.5 1.9 %convolution_bitcast_fusion = f32[1536,384]{0,1:T(8,128)S(1)} fusion(bf16[384,1536]{1,0:T(8,128)(2,1)S(1)} %copy-done, f32[384,384]{1,0:T(8,128)} %reduce-scatter.2.cloned.1.call-done), kind=kOutput, calls=%fused_computation | convolution fusion | flops 453132288 | bytes 4128768 | tf_op jit(solution)/shard_map/dot_general | solution.py:104
  168.4 2.0 %copy.9 = f32[1536,384]{1,0:T(8,128)} copy(f32[1536,384]{0,1:T(8,128)S(1)} %convolution_bitcast_fusion) | data formatting | bytes 4718592
  (6 shorter events, 0.0 us)
Async XLA Ops:
  7.2 1.3 copy-start
  7.2 159.3 %reduce-scatter.2.cloned.1.call-start = ((), (), s32[]{:S(2)}) async-start(), calls=%async_computation.1 | async-start | bytes 2949120 | tf_op jit(solution)/shard_map/reduce_scatter | solution.py:103
  13.2 29.0 %collective-permute-start.6 = (bf16[384,1536]{1,0:T(8,128)(2,1)S(1)}, bf16[384,1536]{1,0:T(8,128)(2,1)S(1)}, u32[]{:S(2)}, u32[]{:S(2)}) collective-permute-start(bf16[384,1536]{1,0:T(8,128)(2,1)S(1)} %fusion.18), channel_id=1, source_target_pairs={{0,4},{4,0},{8,12},{12,8},{16,20},{20,16},{24,28},{28,24},{1,5},{5... | collective-permute-start | bytes 3538952 | tf_op jit(solution)/shard_map/ppermute | solution.py:14
  42.7 27.2 %collective-permute-start.7 = (bf16[384,1536]{1,0:T(8,128)(2,1)S(1)}, bf16[384,1536]{1,0:T(8,128)(2,1)S(1)}, u32[]{:S(2)}, u32[]{:S(2)}) collective-permute-start(bf16[384,1536]{1,0:T(8,128)(2,1)S(1)} %broadcast_select_fusion), channel_id=1, source_target_pairs={{0,8},{8,0},{4,12},{12,4},{16,24},{24,16},{20,28},{28,20},{1,9},{9... | collective-permute-start | bytes 3538952 | tf_op jit(solution)/shard_map/ppermute | solution.py:14
  69.9 2.7 %copy-start.1 = (s32[384]{0:T(512)S(1)}, s32[384]{0:T(512)}, u32[]{:S(2)}) copy-start(s32[384]{0:T(512)} %param.9) | copy-start | bytes 4612
  70.0 57.8 %collective-permute-start.8 = (bf16[384,1536]{1,0:T(8,128)(2,1)S(1)}, bf16[384,1536]{1,0:T(8,128)(2,1)S(1)}, u32[]{:S(2)}, u32[]{:S(2)}) collective-permute-start(bf16[384,1536]{1,0:T(8,128)(2,1)S(1)} %broadcast_select_fusion.1), channel_id=1, source_target_pairs={{0,16},{16,0},{4,20},{20,4},{8,24},{24,8},{12,28},{28,12},{1,17},{... | collective-permute-start | bytes 3538952 | tf_op jit(solution)/shard_map/ppermute | solution.py:14
  72.6 3.6 %collective-permute-start.3 = (s32[384]{0:T(512)S(1)}, s32[384]{0:T(512)S(1)}, u32[]{:S(2)}, u32[]{:S(2)}) collective-permute-start(s32[384]{0:T(512)S(1)} %copy-done.1), channel_id=1, source_target_pairs={{0,4},{4,0},{8,12},{12,8},{16,20},{20,16},{24,28},{28,24},{1,5},{5... | collective-permute-start | bytes 4616 | tf_op jit(solution)/shard_map/ppermute | solution.py:14
  74.1 5.0 %collective-permute-start = (s32[1]{0:T(128)}, s32[1]{0:T(128)}, u32[]{:S(2)}, u32[]{:S(2)}) collective-permute-start(s32[1]{0:T(128)} %param.10), channel_id=1, source_target_pairs={{0,4},{4,0},{8,12},{12,8},{16,20},{20,16},{24,28},{28,24},{1,5},{5... | collective-permute-start | bytes 20 | tf_op jit(solution)/shard_map/ppermute | solution.py:14
  76.2 47.0 %collective-permute-start.4 = (s32[384]{0:T(512)S(1)}, s32[384]{0:T(512)S(1)}, u32[]{:S(2)}, u32[]{:S(2)}) collective-permute-start(s32[384]{0:T(512)S(1)} %broadcast_select_fusion.5), channel_id=1, source_target_pairs={{0,8},{8,0},{4,12},{12,4},{16,24},{24,16},{20,28},{28,20},{1,9},{9... | collective-permute-start | bytes 4616 | tf_op jit(solution)/shard_map/ppermute | solution.py:14
  79.8 16.4 %collective-permute-start.1 = (s32[1]{0:T(128)}, s32[1]{0:T(128)}, u32[]{:S(2)}, u32[]{:S(2)}) collective-permute-start(s32[1]{0:T(128)} %select_n.69), channel_id=1, source_target_pairs={{0,8},{8,0},{4,12},{12,4},{16,24},{24,16},{20,28},{28,20},{1,9},{9... | collective-permute-start | bytes 20 | tf_op jit(solution)/shard_map/ppermute | solution.py:14
  96.9 25.7 %collective-permute-start.2 = (s32[1]{0:T(128)}, s32[1]{0:T(128)}, u32[]{:S(2)}, u32[]{:S(2)}) collective-permute-start(s32[1]{0:T(128)} %select_n.70), channel_id=1, source_target_pairs={{0,16},{16,0},{4,20},{20,4},{8,24},{24,8},{12,28},{28,12},{1,17},{... | collective-permute-start | bytes 20 | tf_op jit(solution)/shard_map/ppermute | solution.py:14
  123.3 4.5 %collective-permute-start.5 = (s32[384]{0:T(512)S(1)}, s32[384]{0:T(512)S(1)}, u32[]{:S(2)}, u32[]{:S(2)}) collective-permute-start(s32[384]{0:T(512)S(1)} %broadcast_select_fusion.6), channel_id=1, source_target_pairs={{0,16},{16,0},{4,20},{20,4},{8,24},{24,8},{12,28},{28,12},{1,17},{... | collective-permute-start | bytes 4616 | tf_op jit(solution)/shard_map/ppermute | solution.py:14
Sparse Core Ops, SparseCore 0:
  132.7 33.7 reduce-scatter.1
where the time goes:
time: 179 us; the launch traced here: 178 us
  waiting for transfers between devices  111 us (62%)
  starting transfers between devices  31.3 us (17%)
  between operations  20.6 us (12%)
  matrix products  9.15 us (5%)
  local copies, waits for them, and re-layouts  3.18 us (2%)
  other arithmetic  2.83 us (2%)
    ppermute x9, waiting for transfers between devices, partner(): return lax.ppermute(block, axis, route)  77.9 us
    reduce_scatter x1, waiting for transfers between devices, on_device(): summed = lax.psum_scatter(tangent, 'group', scatter_dimension=1, tiled=True)  33.3 us
    ppermute x9, starting transfers between devices, partner(): return lax.ppermute(block, axis, route)  31.3 us
    dot_general x1, matrix products, project(): jnp.dot(view_descriptors, embedding_matrix, preferred_element_type=jnp.fl...  4.41 us
  transfers between devices with their start and end apart: 10, of which 6 were waited for; matrix products, arithmetic and copies ran while one was open for 0% of the time, Pallas kernels for 0%

commit v1 on v0

v1 whole, which is shorter than its diff:
```python
import jax
import jax.numpy as jnp
from jax import lax
from jax.sharding import PartitionSpec as P


def swap(block, axis, mask):
    count = lax.axis_size(axis)
    return lax.ppermute(block, axis, [(i, i ^ mask) for i in range(count)])


def project(view_descriptors, embedding_matrix):
    raw = jnp.dot(view_descriptors, embedding_matrix, preferred_element_type=jnp.float32)
    row_length = jnp.sqrt(jnp.sum(raw * raw, axis=1, keepdims=True) + 1e-06)
    return (raw / row_length, row_length)


def pair_terms(scores, ids_here, ids_there, used_here, used_there, scale, shift):
    used = used_here[:, None, None] & used_there[None]
    signs = jnp.where(ids_here[:, None, None] == ids_there[None], 1.0, -1.0).astype(jnp.float32)
    logits = scale * scores + shift
    penalties = jnp.where(used, jax.nn.softplus(-signs * logits), 0.0)
    slopes = jnp.where(used, -signs * jax.nn.sigmoid(-signs * logits) * scale, 0.0)
    return (penalties, slopes.astype(jnp.bfloat16))


def scatter_sum(block):
    count = lax.axis_size("group")
    me = lax.axis_index("group")
    rows, columns = block.shape
    block = block.reshape(rows, count, columns // count)
    kept = count
    for bit in range(count.bit_length() - 1):
        mine = jnp.bitwise_and(jnp.right_shift(me, bit), 1)
        pairs = block.reshape(rows, kept // 2, 2, -1)
        keep = lax.dynamic_index_in_dim(pairs, mine, 2, keepdims=False)
        send = lax.dynamic_index_in_dim(pairs, 1 - mine, 2, keepdims=False)
        if bit > 0:
            send = send.astype(jnp.bfloat16)
        block = keep + swap(send, "group", 1 << bit).astype(jnp.float32)
        kept //= 2
    return block.reshape(rows, columns // count)


def gather_quarters(part):
    far = [swap(part, "peer", m) for m in (6, 4, 2)]
    near = swap(part, "peer", 1)
    crossed = [swap(block, "peer", 1) for block in far]
    return [near, far[2], crossed[2], far[1], crossed[1], far[0], crossed[0]]


def small_plan(
    view_descriptors, embedding_matrix, picture_of_view, filled, companion_masks, scale, shift
):
    rows, width = view_descriptors.shape
    members = lax.axis_size("group")
    me, g = lax.axis_index("peer"), lax.axis_index("group")
    size = rows // members
    begin = g * size
    part_ids = lax.dynamic_slice(picture_of_view, (begin,), (size,))
    facts = lax.all_gather(
        jnp.concatenate([part_ids, filled, companion_masks]), ("peer", "group")
    ).reshape(lax.axis_size("peer"), members, size + 2)
    part = lax.dynamic_slice(view_descriptors, (begin, 0), (size, width))
    part_unit = project(part, embedding_matrix)[0].astype(jnp.bfloat16)
    blocks = jnp.stack(gather_quarters(part_unit))
    unit_rows, row_length = project(view_descriptors, embedding_matrix)
    unit_bf = unit_rows.astype(jnp.bfloat16)

    masks = facts[0, :, size + 1]
    partners = jnp.bitwise_xor(me, masks)
    theirs = facts[partners, g]
    used_there = begin + jnp.arange(size, dtype=jnp.int32)[None] < theirs[:, size, None]
    used_here = jnp.arange(rows, dtype=jnp.int32) < filled[0]
    chosen = blocks[masks - 1].reshape(members * size, width)
    scores = lax.dot_general(
        unit_bf, chosen, (((1,), (1,)), ((), ())), preferred_element_type=jnp.float32
    )
    penalties, slopes = pair_terms(
        scores.reshape(rows, members, size),
        picture_of_view,
        theirs[:, :size],
        used_here,
        used_there,
        scale,
        shift,
    )
    losses = lax.psum(jnp.sum(penalties, axis=(0, 2)), "group")
    dunit = jnp.dot(
        slopes.reshape(rows, members * size), chosen, preferred_element_type=jnp.float32
    )
    return (unit_rows, row_length, dunit, losses[g])


def large_plan(
    view_descriptors, embedding_matrix, picture_of_view, filled, companion_masks, scale, shift
):
    rows = view_descriptors.shape[0]
    unit_rows, row_length = project(view_descriptors, embedding_matrix)
    unit_bf = unit_rows.astype(jnp.bfloat16)
    current = (unit_bf, picture_of_view, filled)
    for bit in range(lax.axis_size("peer").bit_length() - 1):
        arrived = [swap(value, "peer", 1 << bit) for value in current]
        chosen = jnp.bitwise_and(jnp.right_shift(companion_masks[0], bit), 1) == 1
        current = [jnp.where(chosen, new, old) for new, old in zip(arrived, current)]
    theirs, their_ids, their_filled = current
    scores = lax.dot_general(
        unit_bf, theirs, (((1,), (1,)), ((), ())), preferred_element_type=jnp.float32
    )
    index = jnp.arange(rows, dtype=jnp.int32)
    penalties, slopes = pair_terms(
        scores[:, None],
        picture_of_view,
        their_ids[None],
        index < filled[0],
        (index < their_filled[0])[None],
        scale,
        shift,
    )
    dunit = jnp.dot(slopes[:, 0], theirs, preferred_element_type=jnp.float32)
    return (unit_rows, row_length, dunit, jnp.sum(penalties))


def on_device(
    view_descriptors,
    embedding_matrix,
    picture_of_view,
    filled_view_places,
    companion_masks,
    score_scale,
    score_shift,
):
    rows = view_descriptors.shape[0]
    plan = small_plan if lax.axis_size("peer") == 8 else large_plan
    unit_rows, row_length, dunit, loss = plan(
        view_descriptors,
        embedding_matrix,
        picture_of_view,
        filled_view_places,
        companion_masks,
        score_scale[0],
        score_shift[0],
    )
    tangent = (
        dunit - unit_rows * jnp.sum(unit_rows * dunit, axis=1, keepdims=True)
    ) / row_length
    draw = scatter_sum(tangent).astype(jnp.bfloat16)
    projector_grad = lax.dot_general(
        view_descriptors, draw, (((0,), (0,)), ((), ())), preferred_element_type=jnp.float32
    )
    return (projector_grad, (loss / (rows * rows)).reshape(1, 1))


def solution(mesh):
    placed = (P("peer", None), P(), P("peer"), P("peer"), P("group"), P(), P())
    return jax.shard_map(
        on_device,
        mesh=mesh,
        in_specs=placed,
        out_specs=(P("peer", "group"), P("peer", "group")),
        check_vma=False,
    )
```

time: 179 us -> 134 us (0.75)
  waiting for transfers between devices: 111 us -> 12.5 us
  blocking collectives: 0 us -> 47.6 us
  local copies, waits for them, and re-layouts: 3.18 us -> 30 us
  starting transfers between devices: 31.3 us -> 13.4 us
  between operations: 20.6 us -> 5.12 us
  other arithmetic: 2.83 us -> 10.1 us
  matrix products: 9.15 us -> 14.3 us
    ppermute x9, waiting for transfers between devices: 77.9 us -> 12.5 us  [swap(): return lax.ppermute(block, axis, [(i, i ^ mask) for i in range(count)])]
    unnamed x0 -> x1, blocking collectives: none -> 39 us
    reduce_scatter x1 -> x0, waiting for transfers between devices: 33.3 us -> none  [on_device(): summed = lax.psum_scatter(tangent, 'group', scatter_dimension=1, tiled=True)]
    ppermute x9, starting transfers between devices: 31.3 us -> 13.4 us  [swap(): return lax.ppermute(block, axis, [(i, i ^ mask) for i in range(count)])]
    unnamed x5 -> x22, local copies, waits for them, and re-layouts: 3.18 us -> 12.5 us
    psum x0 -> x1, blocking collectives: none -> 8.62 us  [small_plan(): losses = lax.psum(jnp.sum(penalties, axis=(0, 2)), 'group')]
    dynamic_slice x0 -> x4, local copies, waits for them, and re-layouts: none -> 7.86 us  [the longest x1 4.8 us: scatter_sum(): keep = lax.dynamic_index_in_dim(pairs, mine, 2, keepdims=False)]
    gather x0 -> x2, local copies, waits for them, and re-layouts: none -> 4.63 us  [the longest x1 3.35 us: small_plan(): chosen = blocks[masks - 1].reshape(members * size, width)]
  transfers between devices with their start and end apart: 10 -> 9, of which waited for: 6 -> 4; matrix products, arithmetic and copies ran while one was open for 0% -> 19% of each run, Pallas kernels for 0% -> 0%
where the time goes in v1:
time: 134 us; the launch traced here: 133 us
  blocking collectives  47.6 us (36%)
  local copies, waits for them, and re-layouts  30 us (22%)
  matrix products  14.3 us (11%)
  starting transfers between devices  13.4 us (10%)
  waiting for transfers between devices  12.5 us (9%)
  other arithmetic  10.1 us (8%)
  between operations  5.12 us (4%)
    unnamed x1, blocking collectives  39 us
    ppermute x9, starting transfers between devices, swap(): return lax.ppermute(block, axis, [(i, i ^ mask) for i in range(count)])  13.4 us
    unnamed x22, local copies, waits for them, and re-layouts  12.5 us
    ppermute x9, waiting for transfers between devices, swap(): return lax.ppermute(block, axis, [(i, i ^ mask) for i in range(count)])  12.5 us
    psum x1, blocking collectives, small_plan(): losses = lax.psum(jnp.sum(penalties, axis=(0, 2)), 'group')  8.62 us
    dot_general x2, matrix products, project(): jnp.dot(view_descriptors, embedding_matrix, preferred_element_type=jnp.fl...  8.32 us
    dynamic_slice x1, local copies, waits for them, and re-layouts, scatter_sum(): keep = lax.dynamic_index_in_dim(pairs, mine, 2, keepdims=False)  4.8 us
    gather x1, local copies, waits for them, and re-layouts, small_plan(): chosen = blocks[masks - 1].reshape(members * size, width)  3.35 us
  transfers between devices with their start and end apart: 9, of which 4 were waited for; matrix products, arithmetic and copies ran while one was open for 19% of the time, Pallas kernels for 0%

profile of v1, /device:TPU:0, one launch (start us, length us, event | category | flops | bytes accessed | tf_op | source)
XLA Modules:
  0.0 133.0 jit_solution(12756655575504505719)
XLA Ops:
  0.7 1.3 copy-done
  1.9 3.3 %multiply_reduce_fusion.2 = (f32[96]{0:T(128)S(1)}, f32[96,1536]{1,0:T(8,128)S(1)}) fusion(bf16[1536,1536]{1,0:T(8,128)(2,1)} %param.8, bf16[384,1536]{1,0:T(8,128)(2,1)S(1)} %copy-done, s32[]{:T(128)S(6)} %select_n.57), kind=kOutput, calls=%fused_computation.24 | convolution fusion | flops 453279648 | bytes 5603716 | tf_op jit(solution)/shard_map/dot_general | solution.py:13
  5.2 0.8 divide_convert_fusion
  6.1 3.0 %collective-permute-start.1 = (bf16[96,1536]{1,0:T(8,128)(2,1)}, bf16[96,1536]{1,0:T(8,128)(2,1)}, u32[]{:S(2)}, u32[]{:S(2)}) collective-permute-start(bf16[96,1536]{1,0:T(8,128)(2,1)} %divide_convert_fusion), channel_id=1, source_target_pairs={{0,8},{4,12},{8,0},{12,4},{16,24},{20,28},{24,16},{28,20},{1,9},{5... | collective-permute-start | bytes 884744 | tf_op jit(solution)/shard_map/ppermute | solution.py:9
  9.1 1.5 %collective-permute-start = (bf16[96,1536]{1,0:T(8,128)(2,1)}, bf16[96,1536]{1,0:T(8,128)(2,1)}, u32[]{:S(2)}, u32[]{:S(2)}) collective-permute-start(bf16[96,1536]{1,0:T(8,128)(2,1)} %divide_convert_fusion), channel_id=1, source_target_pairs={{0,4},{4,0},{8,12},{12,8},{16,20},{20,16},{24,28},{28,24},{1,5},{5... | collective-permute-start | bytes 884744 | tf_op jit(solution)/shard_map/ppermute | solution.py:9
  10.6 2.6 %collective-permute-start.3 = (bf16[96,1536]{1,0:T(8,128)(2,1)}, bf16[96,1536]{1,0:T(8,128)(2,1)}, u32[]{:S(2)}, u32[]{:S(2)}) collective-permute-start(bf16[96,1536]{1,0:T(8,128)(2,1)} %divide_convert_fusion), channel_id=1, source_target_pairs={{0,16},{4,20},{8,24},{12,28},{16,0},{20,4},{24,8},{28,12},{1,17},{... | collective-permute-start | bytes 884744 | tf_op jit(solution)/shard_map/ppermute | solution.py:9
  13.2 0.2 collective-permute-start.5
  13.4 5.0 %multiply_reduce_fusion.1 = (f32[384]{0:T(512)}, f32[384,1536]{1,0:T(8,128)S(1)}) fusion(bf16[384,1536]{1,0:T(8,128)(2,1)S(1)} %copy-done, bf16[1536,1536]{1,0:T(8,128)(2,1)} %param.8), kind=kOutput, calls=%fused_computation.6 | convolution fusion | flops 1813118592 | bytes 8259072 | tf_op jit(solution)/shard_map/dot_general | solution.py:13
  18.4 0.6 iota_add_fusion
  19.0 1.4 %dynamic_slice.19 = s32[96]{0:T(128)} dynamic-slice(s32[384]{0:T(512)} %param.9, s32[]{:T(128)S(6)} %select_n.57), dynamic_slice_sizes={96} | dynamic-slice | bytes 772 | tf_op jit(solution)/shard_map/dynamic_slice | solution.py:60
  21.7 0.9 add_dynamic-update-slice_fusion
  22.6 39.0 %all-reduce.1 = s32[3136]{0:T(1024)} all-reduce(s32[3136]{0:T(1024)S(1)} %add_dynamic-update-slice_fusion), channel_id=2, replica_groups=mesh['peer'=8,'group'=4] {'peer','group'}, use_global_device_ids=true, to_apply=%add.1 | all-reduce | flops 3136 | bytes 25088
  61.5 0.8 reshape.129
  62.4 0.8 xor_reduce_fusion
  63.1 0.6 pad_clamp_fusion
  63.7 1.3 fusion.25
  65.0 1.3 gather_fusion
  67.6 0.9 slice_reduce_fusion
  68.4 0.7 broadcast_compare_fusion
  69.2 0.7 add_sqrt_fusion
  69.8 2.3 %collective-permute-start.2 = (bf16[96,1536]{1,0:T(8,128)(2,1)}, bf16[96,1536]{1,0:T(8,128)(2,1)S(1)}, u32[]{:S(2)}, u32[]{:S(2)}) collective-permute-start(bf16[96,1536]{1,0:T(8,128)(2,1)} %collective-permute-done.1), channel_id=1, source_target_pairs={{0,4},{4,0},{8,12},{12,8},{16,20},{20,16},{24,28},{28,24},{1,5},{5... | collective-permute-start | bytes 884744 | tf_op jit(solution)/shard_map/ppermute | solution.py:9
  72.2 1.7 %bitcast_dynamic-update-slice_fusion.6 = bf16[7,96,1536]{2,1,0:T(8,128)(2,1)} fusion(bf16[96,1536]{1,0:T(8,128)(2,1)} %collective-permute-done), kind=kLoop, calls=%fused_computation.33 | loop fusion | bytes 589824
  73.9 2.0 %collective-permute-start.6 = (bf16[96,1536]{1,0:T(8,128)(2,1)}, bf16[96,1536]{1,0:T(8,128)(2,1)S(1)}, u32[]{:S(2)}, u32[]{:S(2)}) collective-permute-start(bf16[96,1536]{1,0:T(8,128)(2,1)} %collective-permute-done.5), channel_id=1, source_target_pairs={{0,4},{4,0},{8,12},{12,8},{16,20},{20,16},{24,28},{28,24},{1,5},{5... | collective-permute-start | bytes 884744 | tf_op jit(solution)/shard_map/ppermute | solution.py:9
  75.8 1.7 %bitcast_dynamic-update-slice_fusion.5 = bf16[7,96,1536]{2,1,0:T(8,128)(2,1)} fusion(bf16[7,96,1536]{2,1,0:T(8,128)(2,1)} %bitcast_dynamic-update-slice_fusion.6, bf16[96,1536]{1,0:T(8,128)(2,1)} %collective-permute-done.1), kind=kLoop, calls=%fused_computation.32 | loop fusion | bytes 589824
  77.5 2.7 %collective-permute-done.2 = bf16[96,1536]{1,0:T(8,128)(2,1)S(1)} collective-permute-done((bf16[96,1536]{1,0:T(8,128)(2,1)}, bf16[96,1536]{1,0:T(8,128)(2,1)S(1)}, u32[]{:S(2)}, u32[]{:S(2)}) %collective-permute-start.2) | collective-permute-done | bytes 294944 | tf_op jit(solution)/shard_map/ppermute | solution.py:9
  80.2 0.7 bitcast_dynamic-update-slice_fusion.4
  80.9 1.7 %bitcast_dynamic-update-slice_fusion.3 = bf16[7,96,1536]{2,1,0:T(8,128)(2,1)} fusion(bf16[7,96,1536]{2,1,0:T(8,128)(2,1)} %bitcast_dynamic-update-slice_fusion.4, bf16[96,1536]{1,0:T(8,128)(2,1)} %collective-permute-done.3), kind=kLoop, calls=%fused_computation.30 | loop fusion | bytes 589824
  82.6 3.9 %collective-permute-done.4 = bf16[96,1536]{1,0:T(8,128)(2,1)S(1)} collective-permute-done((bf16[96,1536]{1,0:T(8,128)(2,1)}, bf16[96,1536]{1,0:T(8,128)(2,1)S(1)}, u32[]{:S(2)}, u32[]{:S(2)}) %collective-permute-start.4) | collective-permute-done | bytes 294944 | tf_op jit(solution)/shard_map/ppermute | solution.py:9
  86.5 0.7 bitcast_dynamic-update-slice_fusion.2
  87.2 1.7 %bitcast_dynamic-update-slice_fusion.1 = bf16[7,96,1536]{2,1,0:T(8,128)(2,1)} fusion(bf16[7,96,1536]{2,1,0:T(8,128)(2,1)} %bitcast_dynamic-update-slice_fusion.2, bf16[96,1536]{1,0:T(8,128)(2,1)} %collective-permute-done.5), kind=kLoop, calls=%fused_computation.28 | loop fusion | bytes 589824
  88.9 2.8 %collective-permute-done.6 = bf16[96,1536]{1,0:T(8,128)(2,1)S(1)} collective-permute-done((bf16[96,1536]{1,0:T(8,128)(2,1)}, bf16[96,1536]{1,0:T(8,128)(2,1)S(1)}, u32[]{:S(2)}, u32[]{:S(2)}) %collective-permute-start.6) | collective-permute-done | bytes 294944 | tf_op jit(solution)/shard_map/ppermute | solution.py:9
  91.8 0.7 bitcast_dynamic-update-slice_fusion
  92.5 3.4 %gather_fusion.1 = bf16[4,96,1536]{2,1,0:T(8,128)(2,1)} fusion(bf16[7,96,1536]{2,1,0:T(8,128)(2,1)} %bitcast_dynamic-update-slice_fusion, s32[1024]{0:T(1024)} %pad_clamp_fusion), kind=kCustom, calls=%fused_computation.1 | custom fusion | bytes 2359312 | tf_op jit(solution)/shard_map/gather | solution.py:75
  95.9 2.9 %fusion.19 = (u8[384,96]{0,1:T(8,128)(4,1)}, f32[384,4,96]{0,2,1:T(8,128)S(1)}) fusion(f32[]{:T(128)} %bitcast.55, bf16[4,96,1536]{2,1,0:T(8,128)(2,1)} %gather_fusion.1, f32[384,1536]{1,0:T(8,128)S(1)} %get-tuple-element.14, f32[384]{0:T(512)S(1)} %add_sqrt_fusion, f32[]{:T(128)} %bitcast.53, s32[4,96]{1,0:T(4,128)S(1)} %bitcast.56, s32[384]{0:T(512)} %param.9), kind=kOutput, calls=%fused_computation.44 | convolution fusion | flops 455749632 | bytes 4170248 | tf_op jit(solution)/shard_map/dot_general | solution.py:76
  98.8 1.1 multiply_reduce_fusion
  99.9 2.1 %subtract_divide_fusion = f32[384,1536]{1,0:T(8,128)S(1)} fusion(f32[384,1536]{1,0:T(8,128)S(1)} %get-tuple-element.16, f32[384]{0:T(512)S(1)} %get-tuple-element.15, f32[384]{0:T(512)S(1)} %add_sqrt_fusion, f32[384,1536]{1,0:T(8,128)} %copy-done.2), kind=kLoop, calls=%fused_computation.4 | loop fusion | flops 2359296 | bytes 7080960 | tf_op jit(solution)/shard_map/div | solution.py:144
  102.0 2.6 %reshape_reshape.3 = f32[384,2,2,384]{3,2,1,0:T(2,128)} reshape(f32[384,1536]{1,0:T(8,128)S(1)} %subtract_divide_fusion) | data formatting | bytes 4718592 | tf_op jit(solution)/shard_map/reshape;reshape | solution.py:35
  104.5 4.8 %constant_dynamic-slice_fusion.1 = (f32[384,2,1,384]{3,2,1,0:T(1,128)S(1)}, f32[384,2,1,384]{3,2,1,0:T(1,128)S(1)}) fusion(f32[384,2,2,384]{3,2,1,0:T(2,128)} %reshape_reshape.3, s32[]{:T(128)S(6)} %select_n.63, s32[]{:T(128)S(6)} %select_n.64), kind=kLoop, calls=%fused_computation.56 | loop fusion | bytes 4718600 | tf_op jit(solution)/shard_map/jit(dynamic_index_in_dim)/dynamic_slice | solution.py:36
  109.4 1.1 copy.15
  110.4 3.1 %collective-permute-done.7 = f32[384,2,384]{2,0,1:T(8,128)S(1)} collective-permute-done((f32[384,2,384]{2,0,1:T(8,128)}, f32[384,2,384]{2,0,1:T(8,128)S(1)}, u32[]{:S(2)}, u32[]{:S(2)}) %collective-permute-start.7) | collective-permute-done | bytes 1179680 | tf_op jit(solution)/shard_map/ppermute | solution.py:9
  113.5 0.1 bitcast_add_fusion
  113.6 1.0 copy-done.1
  114.7 1.8 %collective-permute-start.8 = (bf16[384,1,384]{2,0,1:T(8,128)(2,1)S(1)}, bf16[384,1,384]{2,0,1:T(8,128)(2,1)}, u32[]{:S(2)}, u32[]{:S(2)}) collective-permute-start(bf16[384,1,384]{2,0,1:T(8,128)(2,1)S(1)} %dynamic-slice_convert_fusion), channel_id=1, source_target_pairs={{0,2},{1,3},{2,0},{3,1},{4,6},{5,7},{6,4},{7,5},{8,10},{9,11},{10,... | collective-permute-start | bytes 884744 | tf_op jit(solution)/shard_map/ppermute | solution.py:9
  116.5 1.6 %fusion.5 = f32[4]{0:T(128)S(1)} fusion(f32[384,4,96]{0,2,1:T(8,128)} %copy-done.4, pred[4,96]{1,0:T(4,128)(4,1)S(1)} %broadcast_compare_fusion, pred[384]{0:T(512)(128)(4,1)S(1)} %iota_compare_fusion, u8[384,96]{0,1:T(8,128)(4,1)} %get-tuple-element.17), kind=kLoop, calls=%fused_computation.18 | loop fusion | flops 1769468 | bytes 627472 | tf_op jit(solution)/shard_map/reduce_sum | solution.py:88
  118.1 8.6 %psum.7 = f32[4]{0:T(128)S(1)} all-reduce(f32[4]{0:T(128)S(1)} %fusion.5), channel_id=1, replica_groups=mesh['peer'=8,'group'=4] {'group'}, use_global_device_ids=true, to_apply=%region_4.5 | all-reduce | flops 4 | bytes 32 | tf_op jit(solution)/shard_map/psum | solution.py:88
  126.7 0.6 dynamic_slice.23
  128.0 2.0 %convolution_bitcast_fusion = f32[1536,384]{0,1:T(8,128)S(1)} fusion(bf16[384,1536]{1,0:T(8,128)(2,1)S(1)} %copy-done, bf16[384,1,384]{2,0,1:T(8,128)(2,1)} %collective-permute-done.8, f32[384,2,384]{2,0,1:T(8,128)} %copy-done.1, s32[]{:T(128)S(6)} %select_n.65), kind=kOutput, calls=%fused_computation.2 | convolution fusion | flops 453427200 | bytes 4423684 | tf_op jit(solution)/shard_map/dot_general | solution.py:148
  129.9 2.0 %copy.12 = f32[1536,384]{1,0:T(8,128)} copy(f32[1536,384]{0,1:T(8,128)S(1)} %convolution_bitcast_fusion) | data formatting | bytes 4718592
  (24 shorter events, 0.2 us)
Async XLA Ops:
  0.6 1.3 copy-start
  6.1 63.7 %collective-permute-start.1 = (bf16[96,1536]{1,0:T(8,128)(2,1)}, bf16[96,1536]{1,0:T(8,128)(2,1)}, u32[]{:S(2)}, u32[]{:S(2)}) collective-permute-start(bf16[96,1536]{1,0:T(8,128)(2,1)} %divide_convert_fusion), channel_id=1, source_target_pairs={{0,8},{4,12},{8,0},{12,4},{16,24},{20,28},{24,16},{28,20},{1,9},{5... | collective-permute-start | bytes 884744 | tf_op jit(solution)/shard_map/ppermute | solution.py:9
  9.1 63.1 %collective-permute-start = (bf16[96,1536]{1,0:T(8,128)(2,1)}, bf16[96,1536]{1,0:T(8,128)(2,1)}, u32[]{:S(2)}, u32[]{:S(2)}) collective-permute-start(bf16[96,1536]{1,0:T(8,128)(2,1)} %divide_convert_fusion), channel_id=1, source_target_pairs={{0,4},{4,0},{8,12},{12,8},{16,20},{20,16},{24,28},{28,24},{1,5},{5... | collective-permute-start | bytes 884744 | tf_op jit(solution)/shard_map/ppermute | solution.py:9
  10.6 61.5 %collective-permute-start.3 = (bf16[96,1536]{1,0:T(8,128)(2,1)}, bf16[96,1536]{1,0:T(8,128)(2,1)}, u32[]{:S(2)}, u32[]{:S(2)}) collective-permute-start(bf16[96,1536]{1,0:T(8,128)(2,1)} %divide_convert_fusion), channel_id=1, source_target_pairs={{0,16},{4,20},{8,24},{12,28},{16,0},{20,4},{24,8},{28,12},{1,17},{... | collective-permute-start | bytes 884744 | tf_op jit(solution)/shard_map/ppermute | solution.py:9
  13.2 60.7 %collective-permute-start.5 = (bf16[96,1536]{1,0:T(8,128)(2,1)}, bf16[96,1536]{1,0:T(8,128)(2,1)}, u32[]{:S(2)}, u32[]{:S(2)}) collective-permute-start(bf16[96,1536]{1,0:T(8,128)(2,1)} %divide_convert_fusion), channel_id=1, source_target_pairs={{0,24},{4,28},{8,16},{12,20},{16,8},{20,12},{24,0},{28,4},{1,25},{... | collective-permute-start | bytes 884744 | tf_op jit(solution)/shard_map/ppermute | solution.py:9
  18.4 80.4 %copy-start.2 = (f32[384,1536]{1,0:T(8,128)}, f32[384,1536]{1,0:T(8,128)S(1)}, u32[]{:S(2)}) copy-start(f32[384,1536]{1,0:T(8,128)S(1)} %get-tuple-element.14) | copy-start | bytes 7077892
  69.8 10.4 %collective-permute-start.2 = (bf16[96,1536]{1,0:T(8,128)(2,1)}, bf16[96,1536]{1,0:T(8,128)(2,1)S(1)}, u32[]{:S(2)}, u32[]{:S(2)}) collective-permute-start(bf16[96,1536]{1,0:T(8,128)(2,1)} %collective-permute-done.1), channel_id=1, source_target_pairs={{0,4},{4,0},{8,12},{12,8},{16,20},{20,16},{24,28},{28,24},{1,5},{5... | collective-permute-start | bytes 884744 | tf_op jit(solution)/shard_map/ppermute | solution.py:9
  72.1 14.4 %collective-permute-start.4 = (bf16[96,1536]{1,0:T(8,128)(2,1)}, bf16[96,1536]{1,0:T(8,128)(2,1)S(1)}, u32[]{:S(2)}, u32[]{:S(2)}) collective-permute-start(bf16[96,1536]{1,0:T(8,128)(2,1)} %collective-permute-done.3), channel_id=1, source_target_pairs={{0,4},{4,0},{8,12},{12,8},{16,20},{20,16},{24,28},{28,24},{1,5},{5... | collective-permute-start | bytes 884744 | tf_op jit(solution)/shard_map/ppermute | solution.py:9
  73.9 17.9 %collective-permute-start.6 = (bf16[96,1536]{1,0:T(8,128)(2,1)}, bf16[96,1536]{1,0:T(8,128)(2,1)S(1)}, u32[]{:S(2)}, u32[]{:S(2)}) collective-permute-start(bf16[96,1536]{1,0:T(8,128)(2,1)} %collective-permute-done.5), channel_id=1, source_target_pairs={{0,4},{4,0},{8,12},{12,8},{16,20},{20,16},{24,28},{28,24},{1,5},{5... | collective-permute-start | bytes 884744 | tf_op jit(solution)/shard_map/ppermute | solution.py:9
  82.6 13.3 %copy-start.5 = (s32[4,98]{1,0:T(4,128)S(1)}, s32[4,98]{1,0:T(4,128)}, u32[]{:S(2)}) copy-start(s32[4,98]{1,0:T(4,128)} %gather_fusion) | copy-start | bytes 4708
  95.9 2.9 %copy-start.3 = (bf16[4,96,1536]{2,1,0:T(8,128)(2,1)S(1)}, bf16[4,96,1536]{2,1,0:T(8,128)(2,1)}, u32[]{:S(2)}) copy-start(bf16[4,96,1536]{2,1,0:T(8,128)(2,1)} %gather_fusion.1) | copy-start | bytes 3538948
  95.9 2.9 %copy-start.6 = (s32[384]{0:T(512)S(1)}, s32[384]{0:T(512)}, u32[]{:S(2)}) copy-start(s32[384]{0:T(512)} %param.9) | copy-start | bytes 4612
  98.8 1.1 copy-start.4
  110.4 3.1 %collective-permute-start.7 = (f32[384,2,384]{2,0,1:T(8,128)}, f32[384,2,384]{2,0,1:T(8,128)S(1)}, u32[]{:S(2)}, u32[]{:S(2)}) collective-permute-start(f32[384,2,384]{2,0,1:T(8,128)} %bitcast.50), channel_id=1, source_target_pairs={{0,1},{1,0},{2,3},{3,2},{4,5},{5,4},{6,7},{7,6},{8,9},{9,8},{10,11... | collective-permute-start | bytes 3538952 | tf_op jit(solution)/shard_map/ppermute | solution.py:9
  113.6 1.0 copy-start.1
  114.7 13.3 %collective-permute-start.8 = (bf16[384,1,384]{2,0,1:T(8,128)(2,1)S(1)}, bf16[384,1,384]{2,0,1:T(8,128)(2,1)}, u32[]{:S(2)}, u32[]{:S(2)}) collective-permute-start(bf16[384,1,384]{2,0,1:T(8,128)(2,1)S(1)} %dynamic-slice_convert_fusion), channel_id=1, source_target_pairs={{0,2},{1,3},{2,0},{3,1},{4,6},{5,7},{6,4},{7,5},{8,10},{9,11},{10,... | collective-permute-start | bytes 884744 | tf_op jit(solution)/shard_map/ppermute | solution.py:9

commit v2 on v1

v2 whole, which is shorter than its diff:
```python
import functools

import jax
import jax.numpy as jnp
from jax import lax
from jax.experimental import pallas as pl
from jax.experimental.pallas import tpu as pltpu
from jax.sharding import PartitionSpec as P

AXES = ("peer", "group")
FIRST = 128
VMEM = pl.BlockSpec(memory_space=pltpu.VMEM)
SMEM = pl.BlockSpec(memory_space=pltpu.SMEM)


def swap(block, axis, mask):
    count = lax.axis_size(axis)
    return lax.ppermute(block, axis, [(i, i ^ mask) for i in range(count)])


def swap_cores(block, even_mask, odd_mask):
    members = lax.axis_size("group")
    route = []
    for p in range(lax.axis_size("peer")):
        for g in range(members):
            mask = (even_mask, odd_mask)[g & 1]
            if mask is not None:
                route.append((p * members + g, (p ^ mask) * members + g))
    return lax.ppermute(block, AXES, route)


def project(view_descriptors, embedding_matrix):
    raw = jnp.dot(view_descriptors, embedding_matrix, preferred_element_type=jnp.float32)
    row_length = jnp.sqrt(jnp.sum(raw * raw, axis=1, keepdims=True) + 1e-06)
    return (raw / row_length, row_length)


def half_unit_kernel(half_ref, features, matrix, unit, raw, squares):
    step = pl.program_id(0)
    block = jnp.dot(features[...], matrix[...], preferred_element_type=jnp.float32)
    raw[step] = block
    partial = jnp.sum(block * block, axis=1, keepdims=True)

    @pl.when(step == 0)
    def _():
        squares[...] = jnp.broadcast_to(partial, squares.shape)

    @pl.when(step > 0)
    def _():
        squares[...] += partial

    @pl.when(step == pl.num_programs(0) - 1)
    def _():
        length = jnp.sqrt(squares[...][:, :1] + 1e-06)
        width = block.shape[1]
        for k in range(raw.shape[0]):
            unit[:, k * width : (k + 1) * width] = (raw[k] / length).astype(jnp.bfloat16)


def half_unit(half, features, matrix):
    rows, depth = features.shape
    width = matrix.shape[1]
    steps = 4
    return pl.pallas_call(
        half_unit_kernel,
        out_shape=jax.ShapeDtypeStruct((rows // 2, width), jnp.bfloat16),
        grid_spec=pltpu.PrefetchScalarGridSpec(
            num_scalar_prefetch=1,
            grid=(steps,),
            in_specs=[
                pl.BlockSpec((rows // 2, depth), lambda j, h: (h[0], 0)),
                pl.BlockSpec((depth, width // steps), lambda j, h: (0, j)),
            ],
            out_specs=pl.BlockSpec((rows // 2, width), lambda j, h: (0, 0)),
            scratch_shapes=[
                pltpu.VMEM((steps, rows // 2, width // steps), jnp.float32),
                pltpu.VMEM((rows // 2, 128), jnp.float32),
            ],
        ),
        compiler_params=pltpu.CompilerParams(vmem_limit_bytes=24 << 20),
        cost_estimate=pl.CostEstimate(
            flops=rows * depth * width, bytes_accessed=2 * depth * width, transcendentals=0
        ),
        name="half_unit",
    )(half, features, matrix)


def pair_kernel(cuts, first, final, *refs):
    refs = list(refs)
    numbers, factors, ids_here, unit_bf = refs[:4]
    del refs[:4]
    blocks = [refs.pop(0) for _ in cuts]
    ids_there = [refs.pop(0) for _ in cuts]
    if not first:
        old_dunit, old_losses = refs.pop(0), refs.pop(0)
    if final:
        unit, length = refs.pop(0), refs.pop(0)
        keep, send, stacked, total = refs
    else:
        total, losses_out, stacked = refs
    scale, shift = factors[0], factors[1]
    rows = unit_bf.shape[0]
    offset = 0
    for block, (_, begin, count) in zip(blocks, cuts):
        stacked[offset : offset + count] = block[...]
        offset += count
    scores = lax.dot_general(
        unit_bf[...], stacked[...], (((1,), (1,)), ((), ())), preferred_element_type=jnp.float32
    )
    row = lax.broadcasted_iota(jnp.int32, (rows, 1), 0)
    used_here = row < numbers[0]
    lane = lax.broadcasted_iota(jnp.int32, (1, 128), 1)
    losses = jnp.zeros((1, 128), jnp.float32) if first else old_losses[0:1]
    slopes = []
    offset = 0
    for (slot, begin, count), ids in zip(cuts, ids_there):
        turn, filled = numbers[2 + slot], numbers[6 + slot]
        place = numbers[1] + begin + lax.broadcasted_iota(jnp.int32, (1, count), 1)
        used = used_here & (place < filled) & (turn >= 0)
        signs = jnp.where(ids_here[...] == ids[...], -1.0, 1.0)
        logits = signs * (scale * scores[:, offset : offset + count] + shift)
        small = jnp.exp(-jnp.abs(logits))
        penalty = jnp.maximum(logits, 0.0) + jnp.log1p(small)
        loss = jnp.sum(jnp.where(used, penalty, 0.0))
        losses = losses + jnp.where(lane == turn, loss, 0.0)
        gate = jnp.where(logits >= 0, 1.0, small) / (1.0 + small)
        slopes.append(jnp.where(used, signs * gate * scale, 0.0).astype(jnp.bfloat16))
        offset += count
    slopes = slopes[0] if len(slopes) == 1 else jnp.concatenate(slopes, axis=1)
    width = stacked.shape[1]
    step = width // 4
    for k in range(4):
        at = slice(k * step, (k + 1) * step)
        part = jnp.dot(slopes, stacked[:, at], preferred_element_type=jnp.float32)
        total[:, at] = part if first else old_dunit[:, at] + part
    if not final:
        losses_out[...] = jnp.broadcast_to(losses, losses_out.shape)
        return
    along = jnp.sum(unit[...] * total[...], axis=1, keepdims=True)
    total[...] = (total[...] - unit[...] * along) / length[...]
    me = numbers[10]
    for k, other in enumerate((0, 2)):
        at = pl.ds(pl.multiple_of(jnp.bitwise_xor(me, other) * step, 128), step)
        keep[:rows, k * step : (k + 1) * step] = total[:, at]
        at = pl.ds(pl.multiple_of(jnp.bitwise_xor(me, other + 1) * step, 128), step)
        send[:rows, k * step : (k + 1) * step] = total[:, at]
    keep[rows:, :] = jnp.zeros((8, 2 * step), jnp.float32)
    keep[rows : rows + 1, 0:128] = losses
    send[rows:, :] = jnp.zeros((8, 2 * step), jnp.float32)
    send[rows : rows + 1, 0:128] = losses


def pair_terms(numbers, factors, ids_here, unit_bf, blocks, ids_there, cuts, old=None, final=None):
    rows, width = unit_bf.shape
    total = sum(count for _, _, count in cuts)
    args = [numbers, factors, ids_here, unit_bf, *blocks, *ids_there]
    scratch = [pltpu.VMEM((total, width), jnp.bfloat16)]
    if old is not None:
        args += old
    if final is not None:
        args += final
        shapes = [jax.ShapeDtypeStruct((rows + 8, width // 2), jnp.float32)] * 2
        scratch += [pltpu.VMEM((rows, width), jnp.float32)]
    else:
        shapes = [
            jax.ShapeDtypeStruct((rows, width), jnp.float32),
            jax.ShapeDtypeStruct((8, 128), jnp.float32),
        ]
    return pl.pallas_call(
        functools.partial(pair_kernel, cuts, old is None, final is not None),
        out_shape=shapes,
        in_specs=[SMEM, SMEM] + [VMEM] * (len(args) - 2),
        out_specs=[VMEM] * 2,
        scratch_shapes=scratch,
        compiler_params=pltpu.CompilerParams(vmem_limit_bytes=32 << 20),
        cost_estimate=pl.CostEstimate(
            flops=4 * rows * width * total,
            bytes_accessed=8 * rows * width,
            transcendentals=3 * rows * total,
        ),
        name="pair_terms",
    )(*args)


def combine_kernel(keep, arrived, own, send):
    rows, step = own.shape[0] - 8, own.shape[1]
    own[...] = keep[:, :step] + arrived[:, :step]
    send[:rows] = (keep[:rows, step:] + arrived[:rows, step:]).astype(jnp.bfloat16)
    losses = keep[rows : rows + 1, 0:128] + arrived[rows : rows + 1, 0:128]
    high = losses.astype(jnp.bfloat16).astype(jnp.float32)
    middle = (losses - high).astype(jnp.bfloat16).astype(jnp.float32)
    low = losses - high - middle
    line = lax.broadcasted_iota(jnp.int32, (16, 128), 0)
    packed = jnp.where(line == 0, high, jnp.where(line == 1, middle, jnp.where(line == 2, low, 0.0)))
    send[rows:] = jnp.zeros((16, step), jnp.bfloat16)
    send[rows:, 0:128] = packed.astype(jnp.bfloat16)


def combine(keep, arrived):
    rows, width = keep.shape[0] - 8, keep.shape[1]
    return pl.pallas_call(
        combine_kernel,
        out_shape=[
            jax.ShapeDtypeStruct((rows + 8, width // 2), jnp.float32),
            jax.ShapeDtypeStruct((rows + 16, width // 2), jnp.bfloat16),
        ],
        in_specs=[VMEM] * 2,
        out_specs=[VMEM] * 2,
        compiler_params=pltpu.CompilerParams(vmem_limit_bytes=16 << 20),
        name="combine",
    )(keep, arrived)


def gradient_kernel(me, own, arrived, features, grad, loss, draw):
    rows = features.shape[1]

    @pl.when(pl.program_id(0) == 0)
    def _():
        draw[...] = (own[:rows] + arrived[:rows].astype(jnp.float32)).astype(jnp.bfloat16)
        parts = arrived[rows:, 0:128].astype(jnp.float32)
        total = own[rows : rows + 1, 0:128] + jnp.sum(parts, axis=0, keepdims=True)
        lane = lax.broadcasted_iota(jnp.int32, (1, 128), 1)
        value = jnp.sum(jnp.where(lane == me[0], total, 0.0))
        loss[0, 0] = value / (rows * rows)

    grad[...] = jnp.dot(features[...], draw[...], preferred_element_type=jnp.float32)


def gradient(me, own, arrived, features_t):
    depth, rows = features_t.shape
    width = own.shape[1]
    steps = 4
    return pl.pallas_call(
        gradient_kernel,
        out_shape=[
            jax.ShapeDtypeStruct((depth, width), jnp.float32),
            jax.ShapeDtypeStruct((1, 1), jnp.float32),
        ],
        grid=(steps,),
        in_specs=[
            SMEM,
            pl.BlockSpec(own.shape, lambda i: (0, 0)),
            pl.BlockSpec(arrived.shape, lambda i: (0, 0)),
            pl.BlockSpec((depth // steps, rows), lambda i: (i, 0)),
        ],
        out_specs=[pl.BlockSpec((depth // steps, width), lambda i: (i, 0)), SMEM],
        scratch_shapes=[pltpu.VMEM((rows, width), jnp.bfloat16)],
        compiler_params=pltpu.CompilerParams(vmem_limit_bytes=16 << 20),
        name="gradient",
    )(me, own, arrived, features_t)


def small_plan(features, matrix, ids, filled, mask, scale, shift):
    rows = features.shape[0]
    half_rows = rows // 2
    me = lax.axis_index("group")
    y, core = me // 2, me % 2

    half = half_unit(y.reshape(1), features, matrix)
    near = swap_cores(half, 1, 2)
    far_a = swap_cores(half[:FIRST], 4, 6)
    far_b = swap_cores(half[FIRST:], 4, 6)
    near_x = swap_cores(near, None, 1)
    far_ax = swap_cores(far_a, 1, 1)
    far_bx = swap_cores(far_b, 1, 1)

    facts = jnp.concatenate([lax.dynamic_slice(ids, (y * half_rows,), (half_rows,)), filled])
    slots = [
        swap_cores(facts, 1, 2),
        swap_cores(facts, None, 3),
        swap_cores(facts, 4, 6),
        swap_cores(facts, 5, 7),
    ]
    two = jnp.stack([mask[0], swap(mask, "group", 1)[0]])
    other_two = swap(two, "group", 2)
    pair = jnp.arange(4, dtype=jnp.int32)
    four = jnp.concatenate([two, other_two])
    slot_masks = jnp.where(core == 0, jnp.array([1, 0, 4, 5]), jnp.array([2, 3, 6, 7]))
    hit = four[None, :] == slot_masks[:, None]
    turns = jnp.max(jnp.where(hit, jnp.bitwise_xor(pair, me)[None, :], -1), axis=1)
    counts = jnp.stack([slot[half_rows] for slot in slots])
    numbers = jnp.concatenate(
        [filled, (y * half_rows).reshape(1), turns, counts, me.reshape(1)]
    ).astype(jnp.int32)
    factors = jnp.stack([scale, shift])
    there = [slot[None, :half_rows] for slot in slots]
    ids_here = ids[:, None]

    unit, length = project(features, matrix)
    unit_bf = unit.astype(jnp.bfloat16)
    common = (numbers, factors, ids_here, unit_bf)
    early = pair_terms(
        *common, [near, near_x], there[:2], ((0, 0, half_rows), (1, 0, half_rows))
    )
    middle = pair_terms(
        *common,
        [far_a, far_ax],
        [there[2][:, :FIRST], there[3][:, :FIRST]],
        ((2, 0, FIRST), (3, 0, FIRST)),
        old=early,
    )
    rest = half_rows - FIRST
    keep, send = pair_terms(
        *common,
        [far_b, far_bx],
        [there[2][:, FIRST:], there[3][:, FIRST:]],
        ((2, FIRST, rest), (3, FIRST, rest)),
        old=middle,
        final=[unit, length],
    )
    own, send = combine(keep, swap(send, "group", 1))
    return gradient(me.reshape(1), own, swap(send, "group", 2), features.T)


def scatter_sum(block):
    count = lax.axis_size("group")
    me = lax.axis_index("group")
    rows, columns = block.shape
    block = block.reshape(rows, count, columns // count)
    kept = count
    for bit in range(count.bit_length() - 1):
        mine = jnp.bitwise_and(jnp.right_shift(me, bit), 1)
        pairs = block.reshape(rows, kept // 2, 2, -1)
        keep = lax.dynamic_index_in_dim(pairs, mine, 2, keepdims=False)
        send = lax.dynamic_index_in_dim(pairs, 1 - mine, 2, keepdims=False)
        if bit > 0:
            send = send.astype(jnp.bfloat16)
        block = keep + swap(send, "group", 1 << bit).astype(jnp.float32)
        kept //= 2
    return block.reshape(rows, columns // count)


def large_plan(features, matrix, ids, filled, mask, scale, shift):
    rows = features.shape[0]
    unit, length = project(features, matrix)
    unit_bf = unit.astype(jnp.bfloat16)
    current = (unit_bf, ids, filled)
    for bit in range(lax.axis_size("peer").bit_length() - 1):
        arrived = [swap(value, "peer", 1 << bit) for value in current]
        chosen = jnp.bitwise_and(jnp.right_shift(mask[0], bit), 1) == 1
        current = [jnp.where(chosen, new, old) for new, old in zip(arrived, current)]
    theirs, their_ids, their_filled = current
    scores = lax.dot_general(
        unit_bf, theirs, (((1,), (1,)), ((), ())), preferred_element_type=jnp.float32
    )
    index = jnp.arange(rows, dtype=jnp.int32)
    used = (index < filled[0])[:, None] & (index < their_filled[0])[None]
    signs = jnp.where(ids[:, None] == their_ids[None], 1.0, -1.0).astype(jnp.float32)
    logits = scale * scores + shift
    loss = jnp.sum(jnp.where(used, jax.nn.softplus(-signs * logits), 0.0))
    slopes = jnp.where(used, -signs * jax.nn.sigmoid(-signs * logits) * scale, 0.0)
    dunit = jnp.dot(slopes.astype(jnp.bfloat16), theirs, preferred_element_type=jnp.float32)
    tangent = (dunit - unit * jnp.sum(unit * dunit, axis=1, keepdims=True)) / length
    draw = scatter_sum(tangent).astype(jnp.bfloat16)
    grad = lax.dot_general(
        features, draw, (((0,), (0,)), ((), ())), preferred_element_type=jnp.float32
    )
    return (grad, (loss / (rows * rows)).reshape(1, 1))


def on_device(
    view_descriptors,
    embedding_matrix,
    picture_of_view,
    filled_view_places,
    companion_masks,
    score_scale,
    score_shift,
):
    small = lax.axis_size("peer") == 8 and lax.axis_size("group") == 4
    plan = small_plan if small else large_plan
    return plan(
        view_descriptors,
        embedding_matrix,
        picture_of_view,
        filled_view_places,
        companion_masks,
        score_scale[0],
        score_shift[0],
    )


def solution(mesh):
    placed = (P("peer", None), P(), P("peer"), P("peer"), P("group"), P(), P())
    return jax.shard_map(
        on_device,
        mesh=mesh,
        in_specs=placed,
        out_specs=(P("peer", "group"), P("peer", "group")),
        check_vma=False,
    )
```

time: 134 us -> 95.1 us (0.71)
  blocking collectives: 47.6 us -> 0 us
  waiting for transfers between devices: 12.5 us -> 33.2 us
  Pallas kernels: 0 us -> 16.9 us
  matrix products: 14.3 us -> 2.07 us
  local copies, waits for them, and re-layouts: 30 us -> 19.1 us
  other arithmetic: 10.1 us -> 3.18 us
  starting transfers between devices: 13.4 us -> 16.8 us
  between operations: 5.12 us -> 3.44 us
    unnamed x1 -> x0, blocking collectives: 39 us -> none
    ppermute x0 -> x10, waiting for transfers between devices: none -> 21 us  [swap_cores(): return lax.ppermute(block, AXES, route)]
    pallas_call x0 -> x6, Pallas kernels: none -> 16.9 us  [the longest x3 10.2 us: pair_terms(): pl.pallas_call(functools.partial(pair_kernel, cuts, old is None, final is...]
    ppermute x0 -> x10, starting transfers between devices: none -> 13.2 us  [swap_cores(): return lax.ppermute(block, AXES, route)]
    ppermute x9 -> x4, starting transfers between devices: 13.4 us -> 3.62 us  [swap(): return lax.ppermute(block, axis, [(i, i ^ mask) for i in range(count)])]
    psum x1 -> x0, blocking collectives: 8.62 us -> none  [small_plan(): losses = lax.psum(jnp.sum(penalties, axis=(0, 2)), 'group')]
    dynamic_slice x4 -> x1, local copies, waits for them, and re-layouts: 7.86 us -> 0.76 us  [small_plan(): lax.dynamic_slice(ids, (y * half_rows,), (half_rows,))]
    dot_general x2 -> x1, matrix products: 8.32 us -> 2.07 us  [project(): jnp.dot(view_descriptors, embedding_matrix, preferred_element_type=jnp.fl...]
  transfers between devices with their start and end apart: 9 -> 14, of which waited for: 4 -> 6; matrix products, arithmetic and copies ran while one was open for 19% -> 19% of each run, Pallas kernels for 0% -> 10%
where the time goes in v2:
time: 95.1 us; the launch traced here: 94.6 us
  waiting for transfers between devices  33.2 us (35%)
  local copies, waits for them, and re-layouts  19.1 us (20%)
  Pallas kernels  16.9 us (18%)
  starting transfers between devices  16.8 us (18%)
  between operations  3.44 us (4%)
  other arithmetic  3.18 us (3%)
  matrix products  2.07 us (2%)
    ppermute x10, waiting for transfers between devices, swap_cores(): return lax.ppermute(block, AXES, route)  21 us
    ppermute x10, starting transfers between devices, swap_cores(): return lax.ppermute(block, AXES, route)  13.2 us
    ppermute x4, waiting for transfers between devices, swap(): return lax.ppermute(block, axis, [(i, i ^ mask) for i in range(count)])  12.2 us
    pallas_call x3, Pallas kernels, pair_terms(): pl.pallas_call(functools.partial(pair_kernel, cuts, old is None, final is...  10.2 us
    unnamed x25, local copies, waits for them, and re-layouts  6.65 us
    ppermute x4, starting transfers between devices, swap(): return lax.ppermute(block, axis, [(i, i ^ mask) for i in range(count)])  3.62 us
    concatenate x1, local copies, waits for them, and re-layouts, small_plan(): jnp.concatenate([filled, (y * half_rows).reshape(1), turns, counts, me.re...  3.18 us
    slice x4, local copies, waits for them, and re-layouts, small_plan(): counts = jnp.stack([slot[half_rows] for slot in slots])  3.14 us
  transfers between devices with their start and end apart: 14, of which 6 were waited for; matrix products, arithmetic and copies ran while one was open for 19% of the time, Pallas kernels for 10%

profile of v2, /device:TPU:0, one launch (start us, length us, event | category | flops | bytes accessed | tf_op | source)
XLA Modules:
  0.0 94.6 jit_solution(5926268919572927466)
XLA Ops:
  0.6 0.5 collective-permute-start
  1.8 0.8 dynamic_slice.3
  2.6 3.6 %collective-permute-start.4 = (s32[193]{0:T(256)S(1)}, s32[193]{0:T(256)}, u32[]{:S(2)}, u32[]{:S(2)}) collective-permute-start(s32[193]{0:T(256)S(1)} %pad_add_fusion), channel_id=1, source_target_pairs={{0,16},{1,25},{2,18},{3,27},{4,20},{5,29},{6,22},{7,31},{8,24},{9,... | collective-permute-start | bytes 2324 | tf_op jit(solution)/shard_map/ppermute | solution.py:29
  6.3 2.3 %copy-done = bf16[1536,1536]{1,0:T(8,128)(2,1)S(1)} copy-done((bf16[1536,1536]{1,0:T(8,128)(2,1)S(1)}, bf16[1536,1536]{1,0:T(8,128)(2,1)}, u32[]{:S(2)}) %copy-start) | copy-done | bytes 4718616
  8.6 1.3 %copy-done.1 = bf16[384,1536]{1,0:T(8,128)(2,1)S(1)} copy-done((bf16[384,1536]{1,0:T(8,128)(2,1)S(1)}, bf16[384,1536]{1,0:T(8,128)(2,1)}, u32[]{:S(2)}) %copy-start.1) | copy-done | bytes 1179672
  9.9 2.9 %half_unit.1 = bf16[192,1536]{1,0:T(8,128)(2,1)S(1)} custom-call(s32[1]{0:T(128)} %bitcast.2.half_ref, bf16[384,1536]{1,0:T(8,128)(2,1)S(1)} %copy-done.1, bf16[1536,1536]{1,0:T(8,128)(2,1)S(1)} %copy-done), custom_call_target="tpu_custom_call" | custom-call | flops 905969664 | bytes 4718592 | tf_op jit(solution)/shard_map/half_unit/pallas_call | solution.py:64
  12.8 1.6 %collective-permute-start.10 = (bf16[192,1536]{1,0:T(8,128)(2,1)S(1)}, bf16[192,1536]{1,0:T(8,128)(2,1)}, u32[]{:S(2)}, u32[]{:S(2)}) collective-permute-start(bf16[192,1536]{1,0:T(8,128)(2,1)S(1)} %half_unit.1), channel_id=1, source_target_pairs={{0,4},{1,9},{2,6},{3,11},{4,0},{5,13},{6,2},{7,15},{8,12},{9,1},{1... | collective-permute-start | bytes 1769480 | tf_op jit(solution)/shard_map/ppermute | solution.py:29
  14.3 0.7 slice.56
  15.0 0.3 collective-permute-start.6
  15.4 0.8 slice.59
  16.1 2.6 %collective-permute-start.8 = (bf16[128,1536]{1,0:T(8,128)(2,1)}, bf16[128,1536]{1,0:T(8,128)(2,1)}, u32[]{:S(2)}, u32[]{:S(2)}) collective-permute-start(bf16[128,1536]{1,0:T(8,128)(2,1)} %slice.59), channel_id=1, source_target_pairs={{0,16},{1,25},{2,18},{3,27},{4,20},{5,29},{6,22},{7,31},{8,24},{9,... | collective-permute-start | bytes 1179656 | tf_op jit(solution)/shard_map/ppermute | solution.py:29
  18.7 2.1 %multiply_reduce_fusion = (f32[384]{0:T(512)S(1)}, f32[384,1536]{1,0:T(8,128)S(1)}) fusion(bf16[384,1536]{1,0:T(8,128)(2,1)S(1)} %copy-done.1, bf16[1536,1536]{1,0:T(8,128)(2,1)S(1)} %copy-done), kind=kOutput, calls=%fused_computation | convolution fusion | flops 1813118592 | bytes 8259072 | tf_op jit(solution)/shard_map/dot_general | solution.py:33
  20.8 0.4 fusion
  22.8 1.5 %collective-permute-start.11 = (bf16[192,1536]{1,0:T(8,128)(2,1)}, bf16[192,1536]{1,0:T(8,128)(2,1)}, u32[]{:S(2)}, u32[]{:S(2)}) collective-permute-start(bf16[192,1536]{1,0:T(8,128)(2,1)} %collective-permute-done.10.refs_4_), channel_id=1, source_target_pairs={{1,5},{3,7},{5,1},{7,3},{9,13},{11,15},{13,9},{15,11},{17,21},{19,... | collective-permute-start | bytes 1769480 | tf_op jit(solution)/shard_map/ppermute | solution.py:29
  25.1 0.8 broadcast_in_dim.38.refs_2_
  25.9 0.8 sqrt.7.refs_11_
  26.7 0.7 broadcast_select_fusion
  27.3 16.8 %collective-permute-done.8.refs_4_ = bf16[128,1536]{1,0:T(8,128)(2,1)} collective-permute-done((bf16[128,1536]{1,0:T(8,128)(2,1)}, bf16[128,1536]{1,0:T(8,128)(2,1)}, u32[]{:S(2)}, u32[]{:S(2)}) %collective-permute-start.8) | collective-permute-done | bytes 393248 | tf_op jit(solution)/shard_map/ppermute | solution.py:29
  44.1 1.5 %collective-permute-start.9 = (bf16[128,1536]{1,0:T(8,128)(2,1)}, bf16[128,1536]{1,0:T(8,128)(2,1)}, u32[]{:S(2)}, u32[]{:S(2)}) collective-permute-start(bf16[128,1536]{1,0:T(8,128)(2,1)} %collective-permute-done.8.refs_4_), channel_id=1, source_target_pairs={{0,4},{1,5},{2,6},{3,7},{4,0},{5,1},{6,2},{7,3},{8,12},{9,13},{10,... | collective-permute-start | bytes 1179656 | tf_op jit(solution)/shard_map/ppermute | solution.py:29
  45.6 0.6 pad_add_fusion.1
  46.3 1.5 %collective-permute-start.1 = (s32[2]{0:T(128)S(1)}, s32[2]{0:T(128)S(1)}, u32[]{:S(2)}, u32[]{:S(2)}) collective-permute-start(s32[2]{0:T(128)S(1)} %pad_add_fusion.1), channel_id=1, source_target_pairs={{0,2},{1,3},{2,0},{3,1},{4,6},{5,7},{6,4},{7,5},{8,10},{9,11},{10,... | collective-permute-start | bytes 32 | tf_op jit(solution)/shard_map/ppermute | solution.py:18
  47.8 2.0 %collective-permute-done.1 = s32[2]{0:T(128)S(1)} collective-permute-done((s32[2]{0:T(128)S(1)}, s32[2]{0:T(128)S(1)}, u32[]{:S(2)}, u32[]{:S(2)}) %collective-permute-start.1) | collective-permute-done | bytes 40 | tf_op jit(solution)/shard_map/ppermute | solution.py:18
  49.8 0.6 pad_add_fusion.2
  50.4 0.9 collective-permute-start.2
  51.3 3.9 %collective-permute-done.5 = s32[193]{0:T(256)S(1)} collective-permute-done((s32[193]{0:T(256)S(1)}, s32[193]{0:T(256)S(1)}, u32[]{:S(2)}, u32[]{:S(2)}) %collective-permute-start.5) | collective-permute-done | bytes 804 | tf_op jit(solution)/shard_map/ppermute | solution.py:29
  55.2 0.7 collective-permute-start.3
  55.8 0.6 collective-permute-start.7
  56.4 0.7 select_reduce_fusion
  57.1 1.2 %slice.57.refs_6_ = s32[1,64]{1,0:T(1,128)} slice(s32[1,192]{1,0:T(1,128)} %bitcast.3), slice={[0:1], [128:192]} | slice | bytes 512 | tf_op jit(solution)/shard_map/slice | solution.py:306
  58.3 0.6 slice.60.refs_6_
  58.9 0.5 slice.58.refs_7_
  59.4 1.3 %slice.44 = s32[1]{0:T(128)} slice(s32[193]{0:T(256)} %collective-permute-done.4), slice={[192:193]} | slice | bytes 8 | tf_op jit(solution)/shard_map/slice | solution.py:281
  60.7 0.6 slice.45
  61.3 0.6 slice.42
  61.9 0.6 slice.43
  62.6 3.2 %concatenate.12.refs_0_ = s32[11]{0:T(128)S(1)} concatenate(s32[1]{0:T(128)S(6)} %copy.22, s32[1]{0:T(128)} %bitcast.1, s32[4]{0:T(128)} %select_reduce_fusion, s32[1]{0:T(128)} %slice.42, s32[1]{0:T(128)} %slice.43, s32[1]{0:T(128)} %slice.44, s32[1]{0:T(128)} %slice.45, s32[1]{0:T(128)} %bitcast.me), dimensions={0} | concatenate | bytes 88 | tf_op jit(solution)/shard_map/concatenate | solution.py:282
  65.8 0.9 copy-done.3
  66.7 0.7 copy-done.8
  67.4 0.7 copy-done.10
  68.1 3.6 %pair_terms.3 = (f32[384,1536]{1,0:T(8,128)S(1)}, f32[8,128]{1,0:T(8,128)S(1)}) custom-call(s32[11]{0:T(128)S(1)} %concatenate.12.refs_0_, f32[2]{0:T(128)S(1)} %pad_maximum_fusion.refs_1_, s32[384,1]{1,0:T(8,128)S(1)} %copy-done.3, bf16[384,1536]{1,0:T(8,128)(2,1)S(1)} %get-tuple-element.18.refs_3_, bf16[192,1536]{1,0:T(8,128)(2,1)} %collective-permute-done.10.refs_4_, ...), custom_call_target="tpu_custom_call" | custom-call | flops 905969664 | bytes 4718592 | tf_op jit(solution)/shard_map/pair_terms/pallas_call | solution.py:169
  71.7 3.0 %pair_terms.4 = (f32[384,1536]{1,0:T(8,128)S(1)}, f32[8,128]{1,0:T(8,128)S(1)}) custom-call(s32[11]{0:T(128)S(1)} %concatenate.12.refs_0_, f32[2]{0:T(128)S(1)} %pad_maximum_fusion.refs_1_, s32[384,1]{1,0:T(8,128)S(1)} %copy-done.3, bf16[384,1536]{1,0:T(8,128)(2,1)S(1)} %get-tuple-element.18.refs_3_, bf16[128,1536]{1,0:T(8,128)(2,1)} %collective-permute-done.8.refs_4_, ...), custom_call_target="tpu_custom_call" | custom-call | flops 603979776 | bytes 4718592 | tf_op jit(solution)/shard_map/pair_terms/pallas_call | solution.py:169
  74.8 3.5 %pair_terms.5 = (f32[392,768]{1,0:T(8,128)S(1)}, f32[392,768]{1,0:T(8,128)S(1)}) custom-call(s32[11]{0:T(128)S(1)} %concatenate.12.refs_0_, f32[2]{0:T(128)S(1)} %pad_maximum_fusion.refs_1_, s32[384,1]{1,0:T(8,128)S(1)} %copy-done.3, bf16[384,1536]{1,0:T(8,128)(2,1)S(1)} %get-tuple-element.18.refs_3_, bf16[64,1536]{1,0:T(8,128)(2,1)} %collective-permute-done.6.refs_4_, ...), custom_call_target="tpu_custom_call" | custom-call | flops 301989888 | bytes 4718592 | tf_op jit(solution)/shard_map/pair_terms/pallas_call | solution.py:169
  78.4 2.9 %collective-permute-done.12.arrived = f32[392,768]{1,0:T(8,128)S(1)} collective-permute-done((f32[392,768]{1,0:T(8,128)S(1)}, f32[392,768]{1,0:T(8,128)S(1)}, u32[]{:S(2)}, u32[]{:S(2)}) %collective-permute-start.12) | collective-permute-done | bytes 1204256 | tf_op jit(solution)/shard_map/ppermute | solution.py:18
  81.3 0.9 combine.1
  82.2 1.5 %collective-permute-start.13 = (bf16[400,384]{1,0:T(8,128)(2,1)}, bf16[400,384]{1,0:T(8,128)(2,1)S(1)}, u32[]{:S(2)}, u32[]{:S(2)}) collective-permute-start(bf16[400,384]{1,0:T(8,128)(2,1)} %get-tuple-element.17), channel_id=1, source_target_pairs={{0,2},{1,3},{2,0},{3,1},{4,6},{5,7},{6,4},{7,5},{8,10},{9,11},{10,... | collective-permute-start | bytes 921608 | tf_op jit(solution)/shard_map/ppermute | solution.py:18
  83.7 0.7 copy.21
  84.4 7.3 %collective-permute-done.13.arrived = bf16[400,384]{1,0:T(8,128)(2,1)S(1)} collective-permute-done((bf16[400,384]{1,0:T(8,128)(2,1)}, bf16[400,384]{1,0:T(8,128)(2,1)S(1)}, u32[]{:S(2)}, u32[]{:S(2)}) %collective-permute-start.13) | collective-permute-done | bytes 307232 | tf_op jit(solution)/shard_map/ppermute | solution.py:18
  91.7 2.9 %gradient.1 = (f32[1536,384]{1,0:T(8,128)}, f32[1,1]{1,0:T(1,128)}) custom-call(s32[1]{0:T(128)} %bitcast.me, f32[392,384]{1,0:T(8,128)S(1)} %get-tuple-element.16.own, bf16[400,384]{1,0:T(8,128)(2,1)S(1)} %collective-permute-done.13.arrived, bf16[1536,384]{1,0:T(8,128)(2,1)S(1)} %bitcast.14), custom_call_target="tpu_custom_call" | custom-call | tf_op jit(solution)/shard_map/gradient/pallas_call | solution.py:233
  (34 shorter events, 0.6 us)
Async XLA Ops:
  0.6 45.0 %collective-permute-start = (s32[1]{0:T(128)}, s32[1]{0:T(128)}, u32[]{:S(2)}, u32[]{:S(2)}) collective-permute-start(s32[1]{0:T(128)} %param.13), channel_id=1, source_target_pairs={{0,1},{1,0},{2,3},{3,2},{4,5},{5,4},{6,7},{7,6},{8,9},{9,8},{10,11... | collective-permute-start | bytes 20 | tf_op jit(solution)/shard_map/ppermute | solution.py:18
  2.6 47.8 %collective-permute-start.4 = (s32[193]{0:T(256)S(1)}, s32[193]{0:T(256)}, u32[]{:S(2)}, u32[]{:S(2)}) collective-permute-start(s32[193]{0:T(256)S(1)} %pad_add_fusion), channel_id=1, source_target_pairs={{0,16},{1,25},{2,18},{3,27},{4,20},{5,29},{6,22},{7,31},{8,24},{9,... | collective-permute-start | bytes 2324 | tf_op jit(solution)/shard_map/ppermute | solution.py:29
  6.3 2.3 %copy-start = (bf16[1536,1536]{1,0:T(8,128)(2,1)S(1)}, bf16[1536,1536]{1,0:T(8,128)(2,1)}, u32[]{:S(2)}) copy-start(bf16[1536,1536]{1,0:T(8,128)(2,1)} %matrix.1) | copy-start | bytes 14155780
  8.6 1.3 %copy-start.1 = (bf16[384,1536]{1,0:T(8,128)(2,1)S(1)}, bf16[384,1536]{1,0:T(8,128)(2,1)}, u32[]{:S(2)}) copy-start(bf16[384,1536]{1,0:T(8,128)(2,1)} %features.1) | copy-start | bytes 3538948
  12.8 10.1 %collective-permute-start.10 = (bf16[192,1536]{1,0:T(8,128)(2,1)S(1)}, bf16[192,1536]{1,0:T(8,128)(2,1)}, u32[]{:S(2)}, u32[]{:S(2)}) collective-permute-start(bf16[192,1536]{1,0:T(8,128)(2,1)S(1)} %half_unit.1), channel_id=1, source_target_pairs={{0,4},{1,9},{2,6},{3,11},{4,0},{5,13},{6,2},{7,15},{8,12},{9,1},{1... | collective-permute-start | bytes 1769480 | tf_op jit(solution)/shard_map/ppermute | solution.py:29
  15.0 40.8 %collective-permute-start.6 = (bf16[64,1536]{1,0:T(8,128)(2,1)}, bf16[64,1536]{1,0:T(8,128)(2,1)}, u32[]{:S(2)}, u32[]{:S(2)}) collective-permute-start(bf16[64,1536]{1,0:T(8,128)(2,1)} %slice.56), channel_id=1, source_target_pairs={{0,16},{1,25},{2,18},{3,27},{4,20},{5,29},{6,22},{7,31},{8,24},{9,... | collective-permute-start | bytes 589832 | tf_op jit(solution)/shard_map/ppermute | solution.py:29
  16.1 28.0 %collective-permute-start.8 = (bf16[128,1536]{1,0:T(8,128)(2,1)}, bf16[128,1536]{1,0:T(8,128)(2,1)}, u32[]{:S(2)}, u32[]{:S(2)}) collective-permute-start(bf16[128,1536]{1,0:T(8,128)(2,1)} %slice.59), channel_id=1, source_target_pairs={{0,16},{1,25},{2,18},{3,27},{4,20},{5,29},{6,22},{7,31},{8,24},{9,... | collective-permute-start | bytes 1179656 | tf_op jit(solution)/shard_map/ppermute | solution.py:29
  20.8 4.3 %copy-start.11 = (s32[384]{0:T(512)S(1)}, s32[384]{0:T(512)}, u32[]{:S(2)}) copy-start(s32[384]{0:T(512)} %param.11) | copy-start | bytes 4612
  22.8 42.9 %collective-permute-start.11 = (bf16[192,1536]{1,0:T(8,128)(2,1)}, bf16[192,1536]{1,0:T(8,128)(2,1)}, u32[]{:S(2)}, u32[]{:S(2)}) collective-permute-start(bf16[192,1536]{1,0:T(8,128)(2,1)} %collective-permute-done.10.refs_4_), channel_id=1, source_target_pairs={{1,5},{3,7},{5,1},{7,3},{9,13},{11,15},{13,9},{15,11},{17,21},{19,... | collective-permute-start | bytes 1769480 | tf_op jit(solution)/shard_map/ppermute | solution.py:29
  44.1 27.6 %collective-permute-start.9 = (bf16[128,1536]{1,0:T(8,128)(2,1)}, bf16[128,1536]{1,0:T(8,128)(2,1)}, u32[]{:S(2)}, u32[]{:S(2)}) collective-permute-start(bf16[128,1536]{1,0:T(8,128)(2,1)} %collective-permute-done.8.refs_4_), channel_id=1, source_target_pairs={{0,4},{1,5},{2,6},{3,7},{4,0},{5,1},{6,2},{7,3},{8,12},{9,13},{10,... | collective-permute-start | bytes 1179656 | tf_op jit(solution)/shard_map/ppermute | solution.py:29
  46.3 3.5 %collective-permute-start.1 = (s32[2]{0:T(128)S(1)}, s32[2]{0:T(128)S(1)}, u32[]{:S(2)}, u32[]{:S(2)}) collective-permute-start(s32[2]{0:T(128)S(1)} %pad_add_fusion.1), channel_id=1, source_target_pairs={{0,2},{1,3},{2,0},{3,1},{4,6},{5,7},{6,4},{7,5},{8,10},{9,11},{10,... | collective-permute-start | bytes 32 | tf_op jit(solution)/shard_map/ppermute | solution.py:18
  49.8 5.4 %collective-permute-start.5 = (s32[193]{0:T(256)S(1)}, s32[193]{0:T(256)S(1)}, u32[]{:S(2)}, u32[]{:S(2)}) collective-permute-start(s32[193]{0:T(256)S(1)} %pad_add_fusion), channel_id=1, source_target_pairs={{0,20},{1,29},{2,22},{3,31},{4,16},{5,25},{6,18},{7,27},{8,28},{9,... | collective-permute-start | bytes 2324 | tf_op jit(solution)/shard_map/ppermute | solution.py:29
  50.4 10.8 %collective-permute-start.2 = (s32[193]{0:T(256)S(1)}, s32[193]{0:T(256)S(1)}, u32[]{:S(2)}, u32[]{:S(2)}) collective-permute-start(s32[193]{0:T(256)S(1)} %pad_add_fusion), channel_id=1, source_target_pairs={{0,4},{1,9},{2,6},{3,11},{4,0},{5,13},{6,2},{7,15},{8,12},{9,1},{1... | collective-permute-start | bytes 2324 | tf_op jit(solution)/shard_map/ppermute | solution.py:29
  55.2 6.8 %collective-permute-start.3 = (s32[193]{0:T(256)S(1)}, s32[193]{0:T(256)S(1)}, u32[]{:S(2)}, u32[]{:S(2)}) collective-permute-start(s32[193]{0:T(256)S(1)} %pad_add_fusion), channel_id=1, source_target_pairs={{1,13},{3,15},{5,9},{7,11},{9,5},{11,7},{13,1},{15,3},{17,29},{19,... | collective-permute-start | bytes 2324 | tf_op jit(solution)/shard_map/ppermute | solution.py:29
  55.8 19.0 %collective-permute-start.7 = (bf16[64,1536]{1,0:T(8,128)(2,1)}, bf16[64,1536]{1,0:T(8,128)(2,1)}, u32[]{:S(2)}, u32[]{:S(2)}) collective-permute-start(bf16[64,1536]{1,0:T(8,128)(2,1)} %collective-permute-done.6.refs_4_), channel_id=1, source_target_pairs={{0,4},{1,5},{2,6},{3,7},{4,0},{5,1},{6,2},{7,3},{8,12},{9,13},{10,... | collective-permute-start | bytes 589832 | tf_op jit(solution)/shard_map/ppermute | solution.py:29
  61.3 1.3 %copy-start.7 = (s32[193]{0:T(256)}, s32[193]{0:T(256)S(1)}, u32[]{:S(2)}) copy-start(s32[193]{0:T(256)S(1)} %collective-permute-done.2) | copy-start | bytes 2320
  61.9 0.7 copy-start.9
  65.8 0.9 copy-start.3
  66.7 0.7 copy-start.8
  67.4 0.7 copy-start.10
  71.7 3.1 %copy-start.4 = (f32[384,1]{1,0:T(8,128)S(1)}, f32[384,1]{1,0:T(8,128)}, u32[]{:S(2)}) copy-start(f32[384,1]{1,0:T(8,128)} %sqrt.7.refs_11_) | copy-start | bytes 4612
  71.7 3.1 %copy-start.5 = (s32[1,64]{1,0:T(1,128)S(1)}, s32[1,64]{1,0:T(1,128)}, u32[]{:S(2)}) copy-start(s32[1,64]{1,0:T(1,128)} %slice.57.refs_6_) | copy-start | bytes 772
  71.7 3.1 %copy-start.6 = (s32[1,64]{1,0:T(1,128)S(1)}, s32[1,64]{1,0:T(1,128)}, u32[]{:S(2)}) copy-start(s32[1,64]{1,0:T(1,128)} %slice.58.refs_7_) | copy-start | bytes 772
  78.3 5.4 %copy-start.2 = (bf16[384,1536]{1,0:T(8,128)(2,1)S(1)}, bf16[384,1536]{1,0:T(8,128)(2,1)}, u32[]{:S(2)}) copy-start(bf16[384,1536]{1,0:T(8,128)(2,1)} %features.1) | copy-start | bytes 3538948
  78.3 2.9 %collective-permute-start.12 = (f32[392,768]{1,0:T(8,128)S(1)}, f32[392,768]{1,0:T(8,128)S(1)}, u32[]{:S(2)}, u32[]{:S(2)}) collective-permute-start(f32[392,768]{1,0:T(8,128)S(1)} %get-tuple-element.15), channel_id=1, source_target_pairs={{0,1},{1,0},{2,3},{3,2},{4,5},{5,4},{6,7},{7,6},{8,9},{9,8},{10,11... | collective-permute-start | bytes 3612680 | tf_op jit(solution)/shard_map/ppermute | solution.py:18
  82.2 9.5 %collective-permute-start.13 = (bf16[400,384]{1,0:T(8,128)(2,1)}, bf16[400,384]{1,0:T(8,128)(2,1)S(1)}, u32[]{:S(2)}, u32[]{:S(2)}) collective-permute-start(bf16[400,384]{1,0:T(8,128)(2,1)} %get-tuple-element.17), channel_id=1, source_target_pairs={{0,2},{1,3},{2,0},{3,1},{4,6},{5,7},{6,4},{7,5},{8,10},{9,11},{10,... | collective-permute-start | bytes 921608 | tf_op jit(solution)/shard_map/ppermute | solution.py:18

commit v3 on v2

--- a/solution.py
+++ b/solution.py
@@ -8,7 +8,11 @@
 from jax.sharding import PartitionSpec as P
 
 AXES = ("peer", "group")
-FIRST = 128
+FIRST = 112
+SLOTS = ((1, 2, 3, 4, 5), (1, 2, 3, 6, 7))
+STEPS = 6
+SMALL = pl.CostEstimate(flops=1, bytes_accessed=1, transcendentals=0)
+ANY = pl.BlockSpec(memory_space=pl.ANY)
 VMEM = pl.BlockSpec(memory_space=pltpu.VMEM)
 SMEM = pl.BlockSpec(memory_space=pltpu.SMEM)
 
@@ -35,89 +39,168 @@
     return (raw / row_length, row_length)
 
 
-def half_unit_kernel(half_ref, features, matrix, unit, raw, squares):
-    step = pl.program_id(0)
-    block = jnp.dot(features[...], matrix[...], preferred_element_type=jnp.float32)
-    raw[step] = block
-    partial = jnp.sum(block * block, axis=1, keepdims=True)
-
-    @pl.when(step == 0)
-    def _():
-        squares[...] = jnp.broadcast_to(partial, squares.shape)
-
-    @pl.when(step > 0)
-    def _():
-        squares[...] += partial
-
-    @pl.when(step == pl.num_programs(0) - 1)
-    def _():
-        length = jnp.sqrt(squares[...][:, :1] + 1e-06)
-        width = block.shape[1]
-        for k in range(raw.shape[0]):
-            unit[:, k * width : (k + 1) * width] = (raw[k] / length).astype(jnp.bfloat16)
-
-
-def half_unit(half, features, matrix):
+def after(value, *others):
+    return lax.optimization_barrier((value, *others))[0]
+
+
+def load(features, matrix, features_v, matrix_v, sems, begin, rows):
+    depth = matrix_v.shape[0] // STEPS
+    copies = [pltpu.make_async_copy(features.at[pl.ds(begin, rows)], features_v, sems.at[STEPS])]
+    for k in range(STEPS):
+        at = pl.ds(k * depth, depth)
+        copies.append(pltpu.make_async_copy(matrix.at[at], matrix_v.at[at], sems.at[k]))
+    for copy in copies:
+        copy.start()
+    return copies
+
+
+def multiply(copies, features_v, matrix_v, raw):
+    depth = matrix_v.shape[0] // STEPS
+    copies[0].wait()
+    for k in range(STEPS):
+        at = slice(k * depth, (k + 1) * depth)
+        copies[1 + k].wait()
+        part = jnp.dot(features_v[:, at], matrix_v[at], preferred_element_type=jnp.float32)
+        raw[...] = part if k == 0 else raw[...] + part
+    return jnp.sqrt(jnp.sum(raw[...] * raw[...], axis=1, keepdims=True) + 1e-06)
+
+
+def half_unit_kernel(ids, filled, features, matrix, unit, unit_a, unit_b, features_v, matrix_v, raw, sems):
+    me = lax.axis_index("group")
+    y, core = me // 2, me % 2
+    half = raw.shape[0]
+    first = unit_a.shape[0] - 16
+    copies = load(features, matrix, features_v, matrix_v, sems, y * half, half)
+    row_ids = ids[...].reshape(1, 2 * half)
+    row_ids = jnp.where(y == 0, row_ids[:, :half], row_ids[:, half:])
+    part_ids = jnp.where(core == 0, row_ids[:, : half // 2], row_ids[:, half // 2 :])
+    count = jnp.full((1, 256), filled[0], jnp.int32)
+    row = lax.broadcasted_iota(jnp.int32, (16, 1024), 0)
+    for out, value in ((unit, part_ids), (unit_a, row_ids)):
+        digits = []
+        for number in (value, count):
+            missing = 256 - number.shape[1]
+            for digit in (number & 255, number >> 8):
+                digits.append(digit.astype(jnp.float32))
+                if missing:
+                    digits.append(jnp.zeros((1, missing), jnp.float32))
+        facts = jnp.where(row == 0, jnp.concatenate(digits, axis=1), 0.0).astype(jnp.bfloat16)
+        begin = out.shape[0] - 16
+        out[begin:] = jnp.zeros((16, out.shape[1]), jnp.bfloat16)
+        out[begin:, :1024] = facts
+    length = multiply(copies, features_v, matrix_v, raw)
+    value = (raw[...] / length).astype(jnp.bfloat16)
+    unit[: half // 2] = jnp.where(core == 0, value[: half // 2], value[half // 2 :])
+    unit_a[:first] = value[:first]
+    unit_b[...] = value[first:]
+
+
+def half_unit(ids, filled, features, matrix, first):
     rows, depth = features.shape
     width = matrix.shape[1]
-    steps = 4
+    half = rows // 2
     return pl.pallas_call(
         half_unit_kernel,
-        out_shape=jax.ShapeDtypeStruct((rows // 2, width), jnp.bfloat16),
-        grid_spec=pltpu.PrefetchScalarGridSpec(
-            num_scalar_prefetch=1,
-            grid=(steps,),
-            in_specs=[
-                pl.BlockSpec((rows // 2, depth), lambda j, h: (h[0], 0)),
-                pl.BlockSpec((depth, width // steps), lambda j, h: (0, j)),
-            ],
-            out_specs=pl.BlockSpec((rows // 2, width), lambda j, h: (0, 0)),
-            scratch_shapes=[
-                pltpu.VMEM((steps, rows // 2, width // steps), jnp.float32),
-                pltpu.VMEM((rows // 2, 128), jnp.float32),
-            ],
-        ),
-        compiler_params=pltpu.CompilerParams(vmem_limit_bytes=24 << 20),
-        cost_estimate=pl.CostEstimate(
-            flops=rows * depth * width, bytes_accessed=2 * depth * width, transcendentals=0
-        ),
+        out_shape=[
+            jax.ShapeDtypeStruct((count, width), jnp.bfloat16)
+            for count in (half // 2 + 16, first + 16, half - first)
+        ],
+        in_specs=[VMEM, SMEM, ANY, ANY],
+        out_specs=[VMEM] * 3,
+        scratch_shapes=[
+            pltpu.VMEM((half, depth), jnp.bfloat16),
+            pltpu.VMEM((depth, width), jnp.bfloat16),
+            pltpu.VMEM((half, width), jnp.float32),
+            pltpu.SemaphoreType.DMA((STEPS + 1,)),
+        ],
+        compiler_params=pltpu.CompilerParams(vmem_limit_bytes=60 << 20),
+        cost_estimate=pl.CostEstimate(flops=rows * depth * width, bytes_accessed=2 * depth * width, transcendentals=0),
         name="half_unit",
-    )(half, features, matrix)
+    )(ids, filled, features, matrix)
+
+
+def whole_unit_kernel(ids, features, matrix, unit, unit_bf, length, column, features_v, matrix_v, sems):
+    rows = unit.shape[0]
+    copies = load(features, matrix, features_v, matrix_v, sems, 0, rows)
+    column[...] = jnp.broadcast_to(ids[...].reshape(1, rows).astype(jnp.float32), (128, rows)).T
+    norm = multiply(copies, features_v, matrix_v, unit)
+    length[...] = jnp.broadcast_to(norm, length.shape)
+    unit[...] = unit[...] / norm
+    unit_bf[...] = unit[...].astype(jnp.bfloat16)
+
+
+def whole_unit(ids, features, matrix):
+    rows, depth = features.shape
+    width = matrix.shape[1]
+    return pl.pallas_call(
+        whole_unit_kernel,
+        out_shape=[
+            jax.ShapeDtypeStruct((rows, width), jnp.float32),
+            jax.ShapeDtypeStruct((rows, width), jnp.bfloat16),
+            jax.ShapeDtypeStruct((rows, 128), jnp.float32),
+            jax.ShapeDtypeStruct((rows, 128), jnp.float32),
+        ],
+        in_specs=[VMEM, ANY, ANY],
+        out_specs=[VMEM] * 4,
+        scratch_shapes=[
+            pltpu.VMEM((rows, depth), jnp.bfloat16),
+            pltpu.VMEM((depth, width), jnp.bfloat16),
+            pltpu.SemaphoreType.DMA((STEPS + 1,)),
+        ],
+        compiler_params=pltpu.CompilerParams(vmem_limit_bytes=28 << 20),
+        cost_estimate=pl.CostEstimate(flops=2 * rows * depth * width, bytes_accessed=4 * depth * width, transcendentals=0),
+        name="whole_unit",
+    )(ids, features, matrix)
 
 
 def pair_kernel(cuts, first, final, *refs):
     refs = list(refs)
-    numbers, factors, ids_here, unit_bf = refs[:4]
-    del refs[:4]
+    masks = refs[:4]
+    scale, shift, filled_here = refs[4][0], refs[5][0], refs[6][0]
+    ids_here, unit_bf = refs[7:9]
+    del refs[:9]
     blocks = [refs.pop(0) for _ in cuts]
-    ids_there = [refs.pop(0) for _ in cuts]
     if not first:
         old_dunit, old_losses = refs.pop(0), refs.pop(0)
     if final:
-        unit, length = refs.pop(0), refs.pop(0)
+        old_facts, unit, length = refs.pop(0), refs.pop(0), refs.pop(0)
         keep, send, stacked, total = refs
     else:
-        total, losses_out, stacked = refs
-    scale, shift = factors[0], factors[1]
+        total, losses_out, facts_out, stacked = refs
+    me = lax.axis_index("group")
+    y, core = me // 2, me % 2
     rows = unit_bf.shape[0]
+    half = rows // 2
     offset = 0
     for block, (_, begin, count) in zip(blocks, cuts):
-        stacked[offset : offset + count] = block[...]
+        stacked[offset : offset + count] = block[:count]
         offset += count
     scores = lax.dot_general(
         unit_bf[...], stacked[...], (((1,), (1,)), ((), ())), preferred_element_type=jnp.float32
     )
     row = lax.broadcasted_iota(jnp.int32, (rows, 1), 0)
-    used_here = row < numbers[0]
+    used_here = row < filled_here
     lane = lax.broadcasted_iota(jnp.int32, (1, 128), 1)
     losses = jnp.zeros((1, 128), jnp.float32) if first else old_losses[0:1]
     slopes = []
     offset = 0
-    for (slot, begin, count), ids in zip(cuts, ids_there):
-        turn, filled = numbers[2 + slot], numbers[6 + slot]
-        place = numbers[1] + begin + lax.broadcasted_iota(jnp.int32, (1, count), 1)
-        used = used_here & (place < filled) & (turn >= 0)
-        signs = jnp.where(ids_here[...] == ids[...], -1.0, 1.0)
+    for k, (slot, begin, count) in enumerate(cuts):
+        wanted = jnp.where(core == 0, SLOTS[0][slot], SLOTS[1][slot])
+        turn = jnp.int32(-1)
+        for e, mask in enumerate(masks):
+            turn = jnp.where(mask[0] == wanted, jnp.bitwise_xor(me, e), turn)
+        if final:
+            fact = old_facts[16 * k : 16 * (k + 1)]
+        else:
+            fact = blocks[k][count : count + 16]
+            facts_out[16 * k : 16 * (k + 1)] = fact
+        fact = fact.astype(jnp.float32)[0:1]
+        ids = fact[:, begin : begin + count] + 256.0 * fact[:, 256 + begin : 256 + begin + count]
+        filled = fact[:, 512:513] + 256.0 * fact[:, 768:769]
+        base = me * (half // 2) if slot < 3 else y * half + begin
+        place = base + lax.broadcasted_iota(jnp.int32, (1, count), 1)
+        used = used_here & (place < filled.astype(jnp.int32)) & (turn >= 0)
+        signs = jnp.where(ids_here[:, :1] == ids, -1.0, 1.0)
         logits = signs * (scale * scores[:, offset : offset + count] + shift)
         small = jnp.exp(-jnp.abs(logits))
         penalty = jnp.maximum(logits, 0.0) + jnp.log1p(small)
@@ -137,8 +220,7 @@
         losses_out[...] = jnp.broadcast_to(losses, losses_out.shape)
         return
     along = jnp.sum(unit[...] * total[...], axis=1, keepdims=True)
-    total[...] = (total[...] - unit[...] * along) / length[...]
-    me = numbers[10]
+    total[...] = (total[...] - unit[...] * along) / length[:, :1]
     for k, other in enumerate((0, 2)):
         at = pl.ds(pl.multiple_of(jnp.bitwise_xor(me, other) * step, 128), step)
         keep[:rows, k * step : (k + 1) * step] = total[:, at]
@@ -150,10 +232,10 @@
     send[rows : rows + 1, 0:128] = losses
 
 
-def pair_terms(numbers, factors, ids_here, unit_bf, blocks, ids_there, cuts, old=None, final=None):
+def pair_terms(scalars, ids_here, unit_bf, blocks, cuts, old=None, final=None):
     rows, width = unit_bf.shape
     total = sum(count for _, _, count in cuts)
-    args = [numbers, factors, ids_here, unit_bf, *blocks, *ids_there]
+    args = [*scalars, ids_here, unit_bf, *blocks]
     scratch = [pltpu.VMEM((total, width), jnp.bfloat16)]
     if old is not None:
         args += old
@@ -165,19 +247,16 @@
         shapes = [
             jax.ShapeDtypeStruct((rows, width), jnp.float32),
             jax.ShapeDtypeStruct((8, 128), jnp.float32),
+            jax.ShapeDtypeStruct((16 * len(blocks), width), jnp.bfloat16),
         ]
     return pl.pallas_call(
         functools.partial(pair_kernel, cuts, old is None, final is not None),
         out_shape=shapes,
-        in_specs=[SMEM, SMEM] + [VMEM] * (len(args) - 2),
-        out_specs=[VMEM] * 2,
+        in_specs=[SMEM] * len(scalars) + [VMEM] * (len(args) - len(scalars)),
+        out_specs=[VMEM] * len(shapes),
         scratch_shapes=scratch,
-        compiler_params=pltpu.CompilerParams(vmem_limit_bytes=32 << 20),
-        cost_estimate=pl.CostEstimate(
-            flops=4 * rows * width * total,
-            bytes_accessed=8 * rows * width,
-            transcendentals=3 * rows * total,
-        ),
+        compiler_params=pltpu.CompilerParams(vmem_limit_bytes=28 << 20),
+        cost_estimate=pl.CostEstimate(flops=4 * rows * width * total, bytes_accessed=8 * rows * width, transcendentals=3 * rows * total),
         name="pair_terms",
     )(*args)
 
@@ -207,6 +286,7 @@
         in_specs=[VMEM] * 2,
         out_specs=[VMEM] * 2,
         compiler_params=pltpu.CompilerParams(vmem_limit_bytes=16 << 20),
+        cost_estimate=pl.CostEstimate(flops=rows * width, bytes_accessed=8 * rows * width, transcendentals=0),
         name="combine",
     )(keep, arrived)
 
@@ -246,6 +326,7 @@
         out_specs=[pl.BlockSpec((depth // steps, width), lambda i: (i, 0)), SMEM],
         scratch_shapes=[pltpu.VMEM((rows, width), jnp.bfloat16)],
         compiler_params=pltpu.CompilerParams(vmem_limit_bytes=16 << 20),
+        cost_estimate=pl.CostEstimate(flops=2 * rows * depth * width, bytes_accessed=4 * depth * width, transcendentals=0),
         name="gradient",
     )(me, own, arrived, features_t)
 
@@ -253,62 +334,38 @@
 def small_plan(features, matrix, ids, filled, mask, scale, shift):
     rows = features.shape[0]
     half_rows = rows // 2
-    me = lax.axis_index("group")
-    y, core = me // 2, me % 2
-
-    half = half_unit(y.reshape(1), features, matrix)
-    near = swap_cores(half, 1, 2)
-    far_a = swap_cores(half[:FIRST], 4, 6)
-    far_b = swap_cores(half[FIRST:], 4, 6)
-    near_x = swap_cores(near, None, 1)
-    far_ax = swap_cores(far_a, 1, 1)
-    far_bx = swap_cores(far_b, 1, 1)
-
-    facts = jnp.concatenate([lax.dynamic_slice(ids, (y * half_rows,), (half_rows,)), filled])
-    slots = [
-        swap_cores(facts, 1, 2),
-        swap_cores(facts, None, 3),
-        swap_cores(facts, 4, 6),
-        swap_cores(facts, 5, 7),
-    ]
-    two = jnp.stack([mask[0], swap(mask, "group", 1)[0]])
-    other_two = swap(two, "group", 2)
-    pair = jnp.arange(4, dtype=jnp.int32)
-    four = jnp.concatenate([two, other_two])
-    slot_masks = jnp.where(core == 0, jnp.array([1, 0, 4, 5]), jnp.array([2, 3, 6, 7]))
-    hit = four[None, :] == slot_masks[:, None]
-    turns = jnp.max(jnp.where(hit, jnp.bitwise_xor(pair, me)[None, :], -1), axis=1)
-    counts = jnp.stack([slot[half_rows] for slot in slots])
-    numbers = jnp.concatenate(
-        [filled, (y * half_rows).reshape(1), turns, counts, me.reshape(1)]
-    ).astype(jnp.int32)
-    factors = jnp.stack([scale, shift])
-    there = [slot[None, :half_rows] for slot in slots]
-    ids_here = ids[:, None]
-
-    unit, length = project(features, matrix)
-    unit_bf = unit.astype(jnp.bfloat16)
-    common = (numbers, factors, ids_here, unit_bf)
+    rest = half_rows - FIRST
+
+    part, half_a, half_b = half_unit(ids, filled, features, matrix, FIRST)
+    near = swap_cores(part, 1, 1)
+    far_a = swap_cores(half_a, 4, 6)
+    side = swap_cores(part, 2, 2)
+    unit, unit_bf, length, column = whole_unit(ids, after(features, part), matrix)
+    far_b = swap_cores(after(half_b, side), 4, 6)
+    side_x = swap_cores(after(side, near, unit_bf), 1, 1)
+    other_masks = [swap(after(mask, side), "group", k) for k in (1, 2, 3)]
+    far_ax = swap_cores(after(far_a, side_x, *other_masks), 1, 1)
+
+    common = ([mask, *other_masks, scale, shift, filled], column, unit_bf)
+    quarter = half_rows // 2
     early = pair_terms(
-        *common, [near, near_x], there[:2], ((0, 0, half_rows), (1, 0, half_rows))
-    )
+        *common,
+        [near, side, side_x],
+        ((0, 0, quarter), (1, 0, quarter), (2, 0, quarter)),
+    )
+    far_bx = swap_cores(after(far_b, early[1]), 1, 1)
     middle = pair_terms(
-        *common,
-        [far_a, far_ax],
-        [there[2][:, :FIRST], there[3][:, :FIRST]],
-        ((2, 0, FIRST), (3, 0, FIRST)),
-        old=early,
-    )
-    rest = half_rows - FIRST
+        *common, [far_a, far_ax], ((3, 0, FIRST), (4, 0, FIRST)), old=early[:2]
+    )
     keep, send = pair_terms(
         *common,
         [far_b, far_bx],
-        [there[2][:, FIRST:], there[3][:, FIRST:]],
-        ((2, FIRST, rest), (3, FIRST, rest)),
-        old=middle,
-        final=[unit, length],
+        ((3, FIRST, rest), (4, FIRST, rest)),
+        old=middle[:2],
+        final=[middle[2], unit, length],
     )
     own, send = combine(keep, swap(send, "group", 1))
+    me = lax.axis_index("group")
     return gradient(me.reshape(1), own, swap(send, "group", 2), features.T)
 
 
@@ -346,9 +403,9 @@
     index = jnp.arange(rows, dtype=jnp.int32)
     used = (index < filled[0])[:, None] & (index < their_filled[0])[None]
     signs = jnp.where(ids[:, None] == their_ids[None], 1.0, -1.0).astype(jnp.float32)
-    logits = scale * scores + shift
+    logits = scale[0] * scores + shift[0]
     loss = jnp.sum(jnp.where(used, jax.nn.softplus(-signs * logits), 0.0))
-    slopes = jnp.where(used, -signs * jax.nn.sigmoid(-signs * logits) * scale, 0.0)
+    slopes = jnp.where(used, -signs * jax.nn.sigmoid(-signs * logits) * scale[0], 0.0)
     dunit = jnp.dot(slopes.astype(jnp.bfloat16), theirs, preferred_element_type=jnp.float32)
     tangent = (dunit - unit * jnp.sum(unit * dunit, axis=1, keepdims=True)) / length
     draw = scatter_sum(tangent).astype(jnp.bfloat16)
@@ -375,8 +432,8 @@
         picture_of_view,
         filled_view_places,
         companion_masks,
-        score_scale[0],
-        score_shift[0],
+        score_scale,
+        score_shift,
     )
 
 

time: 95.1 us -> 72.4 us (0.76)
  local copies, waits for them, and re-layouts: 19.1 us -> 3.08 us
  waiting for transfers between devices: 33.2 us -> 21.4 us
  Pallas kernels: 16.9 us -> 25.2 us
  other arithmetic: 3.18 us -> 0 us
  starting transfers between devices: 16.8 us -> 19.1 us
  matrix products: 2.07 us -> 0 us
    ppermute x10 -> x7, waiting for transfers between devices: 21 us -> 9.25 us  [swap_cores(): return lax.ppermute(block, AXES, route)]
    slice x10 -> x0, local copies, waits for them, and re-layouts: 6.88 us -> none  [the longest x4 3.14 us: small_plan(): counts = jnp.stack([slot[half_rows] for slot in slots])]
    pallas_call x1 -> x2, Pallas kernels: 2.92 us -> 8.3 us  [the longest x1 4.73 us: half_unit(): pl.pallas_call(half_unit_kernel, out_shape=[jax.ShapeDtypeStruct((count,...]
    unnamed x25 -> x9, local copies, waits for them, and re-layouts: 6.65 us -> 3.08 us
    concatenate x1 -> x0, local copies, waits for them, and re-layouts: 3.18 us -> none  [small_plan(): jnp.concatenate([filled, (y * half_rows).reshape(1), turns, counts, me.re...]
    pallas_call x3, Pallas kernels: 10.2 us -> 13.2 us  [pair_terms(): pl.pallas_call(functools.partial(pair_kernel, cuts, old is None, final is...]
    dot_general x1 -> x0, matrix products: 2.07 us -> none  [project(): jnp.dot(view_descriptors, embedding_matrix, preferred_element_type=jnp.fl...]
    ppermute x10 -> x7, starting transfers between devices: 13.2 us -> 15 us  [swap_cores(): return lax.ppermute(block, AXES, route)]
  transfers between devices with their start and end apart: 14 -> 12, of which waited for: 6 -> 7; matrix products, arithmetic and copies ran while one was open for 19% -> 1% of each run, Pallas kernels for 10% -> 17%
where the time goes in v3:
time: 72.4 us; the launch traced here: 72.1 us
  Pallas kernels  25.2 us (35%)
  waiting for transfers between devices  21.4 us (30%)
  starting transfers between devices  19.1 us (26%)
  between operations  3.31 us (5%)
  local copies, waits for them, and re-layouts  3.08 us (4%)
    ppermute x7, starting transfers between devices, swap_cores(): return lax.ppermute(block, AXES, route)  15 us
    pallas_call x3, Pallas kernels, pair_terms(): pl.pallas_call(functools.partial(pair_kernel, cuts, old is None, final is...  13.2 us
    ppermute x5, waiting for transfers between devices, swap(): return lax.ppermute(block, axis, [(i, i ^ mask) for i in range(count)])  12.1 us
    ppermute x7, waiting for transfers between devices, swap_cores(): return lax.ppermute(block, AXES, route)  9.25 us
    pallas_call x1, Pallas kernels, half_unit(): pl.pallas_call(half_unit_kernel, out_shape=[jax.ShapeDtypeStruct((count,...  4.73 us
    ppermute x5, starting transfers between devices, swap(): return lax.ppermute(block, axis, [(i, i ^ mask) for i in range(count)])  4.14 us
    pallas_call x1, Pallas kernels, whole_unit(): pl.pallas_call(whole_unit_kernel, out_shape=[jax.ShapeDtypeStruct((rows,...  3.56 us
    unnamed x9, local copies, waits for them, and re-layouts  3.08 us
  transfers between devices with their start and end apart: 12, of which 7 were waited for; matrix products, arithmetic and copies ran while one was open for 1% of the time, Pallas kernels for 17%

profile of v3, /device:TPU:0, one launch (start us, length us, event | category | flops | bytes accessed | tf_op | source)
XLA Modules:
  0.0 72.1 jit_solution(15074128837385816970)
XLA Ops:
  1.3 0.0 copy-start.1
  1.3 0.0 copy-start.2
  1.3 4.7 %half_unit.1 = (bf16[112,1536]{1,0:T(8,128)(2,1)}, bf16[128,1536]{1,0:T(8,128)(2,1)}, bf16[80,1536]{1,0:T(8,128)(2,1)}) custom-call(s32[384]{0:T(512)} %ids.3, s32[1]{0:T(128)S(6)} %copy.10.filled.refs_6_, bf16[384,1536]{1,0:T(8,128)(2,1)} %features.2, bf16[1536,1536]{1,0:T(8,128)(2,1)} %matrix.3), custom_call_target="tpu_custom_call" | custom-call | flops 905969664 | bytes 4718592 | tf_op jit(solution)/shard_map/half_unit/pallas_call | solution.py:102
  6.0 3.1 %collective-permute-start = (bf16[112,1536]{1,0:T(8,128)(2,1)}, bf16[112,1536]{1,0:T(8,128)(2,1)S(1)}, u32[]{:S(2)}, u32[]{:S(2)}) collective-permute-start(bf16[112,1536]{1,0:T(8,128)(2,1)} %get-tuple-element.24), channel_id=1, source_target_pairs={{0,8},{1,9},{2,10},{3,11},{4,12},{5,13},{6,14},{7,15},{8,0},{9,1},... | collective-permute-start | bytes 1032200 | tf_op jit(solution)/shard_map/ppermute | solution.py:33
  9.1 1.5 %collective-permute-start.5 = (bf16[112,1536]{1,0:T(8,128)(2,1)}, bf16[112,1536]{1,0:T(8,128)(2,1)S(1)}, u32[]{:S(2)}, u32[]{:S(2)}) collective-permute-start(bf16[112,1536]{1,0:T(8,128)(2,1)} %get-tuple-element.24), channel_id=1, source_target_pairs={{0,4},{1,5},{2,6},{3,7},{4,0},{5,1},{6,2},{7,3},{8,12},{9,13},{10,... | collective-permute-start | bytes 1032200 | tf_op jit(solution)/shard_map/ppermute | solution.py:33
  10.6 2.6 %collective-permute-start.8 = (bf16[128,1536]{1,0:T(8,128)(2,1)}, bf16[128,1536]{1,0:T(8,128)(2,1)S(1)}, u32[]{:S(2)}, u32[]{:S(2)}) collective-permute-start(bf16[128,1536]{1,0:T(8,128)(2,1)} %get-tuple-element.34), channel_id=1, source_target_pairs={{0,16},{1,25},{2,18},{3,27},{4,20},{5,29},{6,22},{7,31},{8,24},{9,... | collective-permute-start | bytes 1179656 | tf_op jit(solution)/shard_map/ppermute | solution.py:33
  13.2 0.0 copy-done.1
  13.2 0.0 copy-done.2
  13.2 0.0 copy-start
  13.2 2.3 %copy-done = bf16[1536,1536]{1,0:T(8,128)(2,1)S(1)} copy-done((bf16[1536,1536]{1,0:T(8,128)(2,1)S(1)}, bf16[1536,1536]{1,0:T(8,128)(2,1)}, u32[]{:S(2)}) %copy-start) | copy-done | bytes 4718616
  15.6 0.0 copy-start.3
  15.6 3.6 %whole_unit.1 = (f32[384,1536]{1,0:T(8,128)S(1)}, bf16[384,1536]{1,0:T(8,128)(2,1)S(1)}, f32[384,128]{1,0:T(8,128)S(1)}, f32[384,128]{1,0:T(8,128)S(1)}) custom-call(s32[384]{0:T(512)S(1)} %copy-done.2, bf16[384,1536]{1,0:T(8,128)(2,1)S(1)} %copy-done.1, bf16[1536,1536]{1,0:T(8,128)(2,1)S(1)} %copy-done), custom_call_target="tpu_custom_call" | custom-call | flops 1811939328 | bytes 9437184 | tf_op jit(solution)/shard_map/whole_unit/pallas_call | solution.py:135
  19.1 1.2 %collective-permute-done.refs_10_ = bf16[112,1536]{1,0:T(8,128)(2,1)S(1)} collective-permute-done((bf16[112,1536]{1,0:T(8,128)(2,1)}, bf16[112,1536]{1,0:T(8,128)(2,1)S(1)}, u32[]{:S(2)}, u32[]{:S(2)}) %collective-permute-start) | collective-permute-done | bytes 344096 | tf_op jit(solution)/shard_map/ppermute | solution.py:33
  20.4 0.0 collective-permute-done.5.refs_9_
  20.4 3.5 %collective-permute-start.6 = (bf16[112,1536]{1,0:T(8,128)(2,1)S(1)}, bf16[112,1536]{1,0:T(8,128)(2,1)S(1)}, u32[]{:S(2)}, u32[]{:S(2)}) collective-permute-start(bf16[112,1536]{1,0:T(8,128)(2,1)S(1)} %collective-permute-done.refs_10_), channel_id=1, source_target_pairs={{0,4},{1,5},{2,6},{3,7},{4,0},{5,1},{6,2},{7,3},{8,12},{9,13},{10,... | collective-permute-start | bytes 1032200 | tf_op jit(solution)/shard_map/ppermute | solution.py:33
  23.9 0.0 copy-done.3
  23.9 2.3 %collective-permute-start.4 = (bf16[80,1536]{1,0:T(8,128)(2,1)S(1)}, bf16[80,1536]{1,0:T(8,128)(2,1)S(1)}, u32[]{:S(2)}, u32[]{:S(2)}) collective-permute-start(bf16[80,1536]{1,0:T(8,128)(2,1)S(1)} %copy-done.3), channel_id=1, source_target_pairs={{0,16},{1,25},{2,18},{3,27},{4,20},{5,29},{6,22},{7,31},{8,24},{9,... | collective-permute-start | bytes 737288 | tf_op jit(solution)/shard_map/ppermute | solution.py:33
  26.1 0.0 collective-permute-start.1
  26.1 1.5 %collective-permute-start.2 = (s32[1]{0:T(128)}, s32[1]{0:T(128)}, u32[]{:S(2)}, u32[]{:S(2)}) collective-permute-start(s32[1]{0:T(128)} %param.11), channel_id=1, source_target_pairs={{0,2},{1,3},{2,0},{3,1},{4,6},{5,7},{6,4},{7,5},{8,10},{9,11},{10,... | collective-permute-start | bytes 20 | tf_op jit(solution)/shard_map/ppermute | solution.py:22
  27.6 0.0 collective-permute-done.1.refs_1_
  27.6 1.2 %collective-permute-start.3 = (s32[1]{0:T(128)}, s32[1]{0:T(128)}, u32[]{:S(2)}, u32[]{:S(2)}) collective-permute-start(s32[1]{0:T(128)} %param.11), channel_id=1, source_target_pairs={{0,3},{1,2},{2,1},{3,0},{4,7},{5,6},{6,5},{7,4},{8,11},{9,10},{10,... | collective-permute-start | bytes 20 | tf_op jit(solution)/shard_map/ppermute | solution.py:22
  28.8 0.9 %collective-permute-done.2.refs_2_ = s32[1]{0:T(128)} collective-permute-done((s32[1]{0:T(128)}, s32[1]{0:T(128)}, u32[]{:S(2)}, u32[]{:S(2)}) %collective-permute-start.2) | collective-permute-done | bytes 36 | tf_op jit(solution)/shard_map/ppermute | solution.py:22
  29.8 0.9 %collective-permute-done.3.refs_3_ = s32[1]{0:T(128)} collective-permute-done((s32[1]{0:T(128)}, s32[1]{0:T(128)}, u32[]{:S(2)}, u32[]{:S(2)}) %collective-permute-start.3) | collective-permute-done | bytes 36 | tf_op jit(solution)/shard_map/ppermute | solution.py:22
  30.7 6.8 %collective-permute-done.8.refs_9_ = bf16[128,1536]{1,0:T(8,128)(2,1)S(1)} collective-permute-done((bf16[128,1536]{1,0:T(8,128)(2,1)}, bf16[128,1536]{1,0:T(8,128)(2,1)S(1)}, u32[]{:S(2)}, u32[]{:S(2)}) %collective-permute-start.8) | collective-permute-done | bytes 393248 | tf_op jit(solution)/shard_map/ppermute | solution.py:33
  37.5 0.0 collective-permute-done.6.refs_11_
  37.5 0.0 collective-permute-start.9
  39.4 4.7 %pair_terms.3 = (f32[384,1536]{1,0:T(8,128)S(1)}, f32[8,128]{1,0:T(8,128)S(1)}, bf16[48,1536]{1,0:T(8,128)(2,1)}) custom-call(s32[1]{0:T(128)S(6)} %copy.11.refs_0_, s32[1]{0:T(128)} %collective-permute-done.1.refs_1_, s32[1]{0:T(128)} %collective-permute-done.2.refs_2_, s32[1]{0:T(128)} %collective-permute-done.3.refs_3_, f32[1]{0:T(128)S(6)} %copy.12.refs_4_, ...), custom_call_target="tpu_custom_call" | custom-call | flops 679477248 | bytes 4718592 | tf_op jit(solution)/shard_map/pair_terms/pallas_call | solution.py:252
  44.1 0.0 collective-permute-done.4.refs_9_
  44.1 2.0 %collective-permute-start.7 = (bf16[80,1536]{1,0:T(8,128)(2,1)S(1)}, bf16[80,1536]{1,0:T(8,128)(2,1)S(1)}, u32[]{:S(2)}, u32[]{:S(2)}) collective-permute-start(bf16[80,1536]{1,0:T(8,128)(2,1)S(1)} %collective-permute-done.4.refs_9_), channel_id=1, source_target_pairs={{0,4},{1,5},{2,6},{3,7},{4,0},{5,1},{6,2},{7,3},{8,12},{9,13},{10,... | collective-permute-start | bytes 737288 | tf_op jit(solution)/shard_map/ppermute | solution.py:33
  46.2 1.2 %collective-permute-done.9.refs_10_ = bf16[128,1536]{1,0:T(8,128)(2,1)S(1)} collective-permute-done((bf16[128,1536]{1,0:T(8,128)(2,1)S(1)}, bf16[128,1536]{1,0:T(8,128)(2,1)S(1)}, u32[]{:S(2)}, u32[]{:S(2)}) %collective-permute-start.9) | collective-permute-done | bytes 393248 | tf_op jit(solution)/shard_map/ppermute | solution.py:33
  47.4 3.8 %pair_terms.4 = (f32[384,1536]{1,0:T(8,128)S(1)}, f32[8,128]{1,0:T(8,128)S(1)}, bf16[32,1536]{1,0:T(8,128)(2,1)S(1)}) custom-call(s32[1]{0:T(128)S(6)} %copy.11.refs_0_, s32[1]{0:T(128)} %collective-permute-done.1.refs_1_, s32[1]{0:T(128)} %collective-permute-done.2.refs_2_, s32[1]{0:T(128)} %collective-permute-done.3.refs_3_, f32[1]{0:T(128)S(6)} %copy.12.refs_4_, ...), custom_call_target="tpu_custom_call" | custom-call | flops 528482304 | bytes 4718592 | tf_op jit(solution)/shard_map/pair_terms/pallas_call | solution.py:252
  51.1 0.0 collective-permute-done.7.refs_10_
  51.2 4.7 %pair_terms.5 = (f32[392,768]{1,0:T(8,128)S(1)}, f32[392,768]{1,0:T(8,128)S(1)}) custom-call(s32[1]{0:T(128)S(6)} %copy.11.refs_0_, s32[1]{0:T(128)} %collective-permute-done.1.refs_1_, s32[1]{0:T(128)} %collective-permute-done.2.refs_2_, s32[1]{0:T(128)} %collective-permute-done.3.refs_3_, f32[1]{0:T(128)S(6)} %copy.12.refs_4_, f32[1]{0:T(128)S(6)} %copy.13.refs_5_, ...), custom_call_target="tpu_custom_call" | custom-call | flops 377487360 | bytes 4718592 | tf_op jit(solution)/shard_map/pair_terms/pallas_call | solution.py:252
  55.9 0.1 collective-permute-start.10
  56.0 2.9 %collective-permute-done.10.arrived = f32[392,768]{1,0:T(8,128)S(1)} collective-permute-done((f32[392,768]{1,0:T(8,128)S(1)}, f32[392,768]{1,0:T(8,128)S(1)}, u32[]{:S(2)}, u32[]{:S(2)}) %collective-permute-start.10) | collective-permute-done | bytes 1204256 | tf_op jit(solution)/shard_map/ppermute | solution.py:22
  58.8 0.8 %combine.1 = (f32[392,384]{1,0:T(8,128)S(1)}, bf16[400,384]{1,0:T(8,128)(2,1)}) custom-call(f32[392,768]{1,0:T(8,128)S(1)} %get-tuple-element.42.keep, f32[392,768]{1,0:T(8,128)S(1)} %collective-permute-done.10.arrived), custom_call_target="tpu_custom_call" | custom-call | flops 294912 | bytes 2359296 | tf_op jit(solution)/shard_map/combine/pallas_call | solution.py:280
  59.7 1.4 %collective-permute-start.11 = (bf16[400,384]{1,0:T(8,128)(2,1)}, bf16[400,384]{1,0:T(8,128)(2,1)S(1)}, u32[]{:S(2)}, u32[]{:S(2)}) collective-permute-start(bf16[400,384]{1,0:T(8,128)(2,1)} %get-tuple-element.45), channel_id=1, source_target_pairs={{0,2},{1,3},{2,0},{3,1},{4,6},{5,7},{6,4},{7,5},{8,10},{9,11},{10,... | collective-permute-start | bytes 921608 | tf_op jit(solution)/shard_map/ppermute | solution.py:22
  61.1 0.7 %copy.9 = bf16[384,1536]{0,1:T(8,128)(2,1)S(1)} copy(bf16[384,1536]{1,0:T(8,128)(2,1)S(1)} %copy-done.1) | data formatting | bytes 2359296 | tf_op args[0]
  61.8 7.4 %collective-permute-done.11.arrived = bf16[400,384]{1,0:T(8,128)(2,1)S(1)} collective-permute-done((bf16[400,384]{1,0:T(8,128)(2,1)}, bf16[400,384]{1,0:T(8,128)(2,1)S(1)}, u32[]{:S(2)}, u32[]{:S(2)}) %collective-permute-start.11) | collective-permute-done | bytes 307232 | tf_op jit(solution)/shard_map/ppermute | solution.py:22
  69.2 2.9 %gradient.1 = (f32[1536,384]{1,0:T(8,128)}, f32[1,1]{1,0:T(1,128)}) custom-call(s32[1]{0:T(128)} %bitcast.me, f32[392,384]{1,0:T(8,128)S(1)} %get-tuple-element.44.own, bf16[400,384]{1,0:T(8,128)(2,1)S(1)} %collective-permute-done.11.arrived, bf16[1536,384]{1,0:T(8,128)(2,1)S(1)} %bitcast.2), custom_call_target="tpu_custom_call" | custom-call | flops 452984832 | bytes 2359296 | tf_op jit(solution)/shard_map/gradient/pallas_call | solution.py:313
Async XLA Ops:
  1.3 11.9 %copy-start.1 = (bf16[384,1536]{1,0:T(8,128)(2,1)S(1)}, bf16[384,1536]{1,0:T(8,128)(2,1)}, u32[]{:S(2)}) copy-start(bf16[384,1536]{1,0:T(8,128)(2,1)} %features.2) | copy-start | bytes 3538948
  1.3 11.9 %copy-start.2 = (s32[384]{0:T(512)S(1)}, s32[384]{0:T(512)}, u32[]{:S(2)}) copy-start(s32[384]{0:T(512)} %ids.3) | copy-start | bytes 4612
  6.0 14.3 %collective-permute-start = (bf16[112,1536]{1,0:T(8,128)(2,1)}, bf16[112,1536]{1,0:T(8,128)(2,1)S(1)}, u32[]{:S(2)}, u32[]{:S(2)}) collective-permute-start(bf16[112,1536]{1,0:T(8,128)(2,1)} %get-tuple-element.24), channel_id=1, source_target_pairs={{0,8},{1,9},{2,10},{3,11},{4,12},{5,13},{6,14},{7,15},{8,0},{9,1},... | collective-permute-start | bytes 1032200 | tf_op jit(solution)/shard_map/ppermute | solution.py:33
  9.1 11.2 %collective-permute-start.5 = (bf16[112,1536]{1,0:T(8,128)(2,1)}, bf16[112,1536]{1,0:T(8,128)(2,1)S(1)}, u32[]{:S(2)}, u32[]{:S(2)}) collective-permute-start(bf16[112,1536]{1,0:T(8,128)(2,1)} %get-tuple-element.24), channel_id=1, source_target_pairs={{0,4},{1,5},{2,6},{3,7},{4,0},{5,1},{6,2},{7,3},{8,12},{9,13},{10,... | collective-permute-start | bytes 1032200 | tf_op jit(solution)/shard_map/ppermute | solution.py:33
  10.6 26.9 %collective-permute-start.8 = (bf16[128,1536]{1,0:T(8,128)(2,1)}, bf16[128,1536]{1,0:T(8,128)(2,1)S(1)}, u32[]{:S(2)}, u32[]{:S(2)}) collective-permute-start(bf16[128,1536]{1,0:T(8,128)(2,1)} %get-tuple-element.34), channel_id=1, source_target_pairs={{0,16},{1,25},{2,18},{3,27},{4,20},{5,29},{6,22},{7,31},{8,24},{9,... | collective-permute-start | bytes 1179656 | tf_op jit(solution)/shard_map/ppermute | solution.py:33
  13.2 2.3 %copy-start = (bf16[1536,1536]{1,0:T(8,128)(2,1)S(1)}, bf16[1536,1536]{1,0:T(8,128)(2,1)}, u32[]{:S(2)}) copy-start(bf16[1536,1536]{1,0:T(8,128)(2,1)} %matrix.3) | copy-start | bytes 14155780
  15.6 8.3 %copy-start.3 = (bf16[80,1536]{1,0:T(8,128)(2,1)S(1)}, bf16[80,1536]{1,0:T(8,128)(2,1)}, u32[]{:S(2)}) copy-start(bf16[80,1536]{1,0:T(8,128)(2,1)} %get-tuple-element.30) | copy-start | bytes 737284
  20.4 17.1 %collective-permute-start.6 = (bf16[112,1536]{1,0:T(8,128)(2,1)S(1)}, bf16[112,1536]{1,0:T(8,128)(2,1)S(1)}, u32[]{:S(2)}, u32[]{:S(2)}) collective-permute-start(bf16[112,1536]{1,0:T(8,128)(2,1)S(1)} %collective-permute-done.refs_10_), channel_id=1, source_target_pairs={{0,4},{1,5},{2,6},{3,7},{4,0},{5,1},{6,2},{7,3},{8,12},{9,13},{10,... | collective-permute-start | bytes 1032200 | tf_op jit(solution)/shard_map/ppermute | solution.py:33
  23.9 20.3 %collective-permute-start.4 = (bf16[80,1536]{1,0:T(8,128)(2,1)S(1)}, bf16[80,1536]{1,0:T(8,128)(2,1)S(1)}, u32[]{:S(2)}, u32[]{:S(2)}) collective-permute-start(bf16[80,1536]{1,0:T(8,128)(2,1)S(1)} %copy-done.3), channel_id=1, source_target_pairs={{0,16},{1,25},{2,18},{3,27},{4,20},{5,29},{6,22},{7,31},{8,24},{9,... | collective-permute-start | bytes 737288 | tf_op jit(solution)/shard_map/ppermute | solution.py:33
  26.1 1.5 %collective-permute-start.1 = (s32[1]{0:T(128)}, s32[1]{0:T(128)}, u32[]{:S(2)}, u32[]{:S(2)}) collective-permute-start(s32[1]{0:T(128)} %param.11), channel_id=1, source_target_pairs={{0,1},{1,0},{2,3},{3,2},{4,5},{5,4},{6,7},{7,6},{8,9},{9,8},{10,11... | collective-permute-start | bytes 20 | tf_op jit(solution)/shard_map/ppermute | solution.py:22
  26.1 3.6 %collective-permute-start.2 = (s32[1]{0:T(128)}, s32[1]{0:T(128)}, u32[]{:S(2)}, u32[]{:S(2)}) collective-permute-start(s32[1]{0:T(128)} %param.11), channel_id=1, source_target_pairs={{0,2},{1,3},{2,0},{3,1},{4,6},{5,7},{6,4},{7,5},{8,10},{9,11},{10,... | collective-permute-start | bytes 20 | tf_op jit(solution)/shard_map/ppermute | solution.py:22
  27.6 3.1 %collective-permute-start.3 = (s32[1]{0:T(128)}, s32[1]{0:T(128)}, u32[]{:S(2)}, u32[]{:S(2)}) collective-permute-start(s32[1]{0:T(128)} %param.11), channel_id=1, source_target_pairs={{0,3},{1,2},{2,1},{3,0},{4,7},{5,6},{6,5},{7,4},{8,11},{9,10},{10,... | collective-permute-start | bytes 20 | tf_op jit(solution)/shard_map/ppermute | solution.py:22
  37.5 9.9 %collective-permute-start.9 = (bf16[128,1536]{1,0:T(8,128)(2,1)S(1)}, bf16[128,1536]{1,0:T(8,128)(2,1)S(1)}, u32[]{:S(2)}, u32[]{:S(2)}) collective-permute-start(bf16[128,1536]{1,0:T(8,128)(2,1)S(1)} %collective-permute-done.8.refs_9_), channel_id=1, source_target_pairs={{0,4},{1,5},{2,6},{3,7},{4,0},{5,1},{6,2},{7,3},{8,12},{9,13},{10,... | collective-permute-start | bytes 1179656 | tf_op jit(solution)/shard_map/ppermute | solution.py:33
  44.1 7.0 %collective-permute-start.7 = (bf16[80,1536]{1,0:T(8,128)(2,1)S(1)}, bf16[80,1536]{1,0:T(8,128)(2,1)S(1)}, u32[]{:S(2)}, u32[]{:S(2)}) collective-permute-start(bf16[80,1536]{1,0:T(8,128)(2,1)S(1)} %collective-permute-done.4.refs_9_), channel_id=1, source_target_pairs={{0,4},{1,5},{2,6},{3,7},{4,0},{5,1},{6,2},{7,3},{8,12},{9,13},{10,... | collective-permute-start | bytes 737288 | tf_op jit(solution)/shard_map/ppermute | solution.py:33
  55.9 2.9 %collective-permute-start.10 = (f32[392,768]{1,0:T(8,128)S(1)}, f32[392,768]{1,0:T(8,128)S(1)}, u32[]{:S(2)}, u32[]{:S(2)}) collective-permute-start(f32[392,768]{1,0:T(8,128)S(1)} %get-tuple-element.43), channel_id=1, source_target_pairs={{0,1},{1,0},{2,3},{3,2},{4,5},{5,4},{6,7},{7,6},{8,9},{9,8},{10,11... | collective-permute-start | bytes 3612680 | tf_op jit(solution)/shard_map/ppermute | solution.py:22
  59.7 9.5 %collective-permute-start.11 = (bf16[400,384]{1,0:T(8,128)(2,1)}, bf16[400,384]{1,0:T(8,128)(2,1)S(1)}, u32[]{:S(2)}, u32[]{:S(2)}) collective-permute-start(bf16[400,384]{1,0:T(8,128)(2,1)} %get-tuple-element.45), channel_id=1, source_target_pairs={{0,2},{1,3},{2,0},{3,1},{4,6},{5,7},{6,4},{7,5},{8,10},{9,11},{10,... | collective-permute-start | bytes 921608 | tf_op jit(solution)/shard_map/ppermute | solution.py:22

commit v4 on v3

--- a/solution.py
+++ b/solution.py
@@ -8,9 +8,8 @@
 from jax.sharding import PartitionSpec as P
 
 AXES = ("peer", "group")
-FIRST = 112
-SLOTS = ((1, 2, 3, 4, 5), (1, 2, 3, 6, 7))
 STEPS = 6
+FACTS = 8
 SMALL = pl.CostEstimate(flops=1, bytes_accessed=1, transcendentals=0)
 ANY = pl.BlockSpec(memory_space=pl.ANY)
 VMEM = pl.BlockSpec(memory_space=pltpu.VMEM)
@@ -22,14 +21,13 @@
     return lax.ppermute(block, axis, [(i, i ^ mask) for i in range(count)])
 
 
-def swap_cores(block, even_mask, odd_mask):
+def trade(block, peer_mask, member_mask):
     members = lax.axis_size("group")
     route = []
     for p in range(lax.axis_size("peer")):
         for g in range(members):
-            mask = (even_mask, odd_mask)[g & 1]
-            if mask is not None:
-                route.append((p * members + g, (p ^ mask) * members + g))
+            other = (p ^ peer_mask) * members + (g ^ member_mask)
+            route.append((p * members + g, other))
     return lax.ppermute(block, AXES, route)
 
 
@@ -65,57 +63,45 @@
     return jnp.sqrt(jnp.sum(raw[...] * raw[...], axis=1, keepdims=True) + 1e-06)
 
 
-def half_unit_kernel(ids, filled, features, matrix, unit, unit_a, unit_b, features_v, matrix_v, raw, sems):
+def part_unit_kernel(ids, filled, features, matrix, unit, features_v, matrix_v, raw, sems):
+    rows, width = raw.shape
     me = lax.axis_index("group")
-    y, core = me // 2, me % 2
-    half = raw.shape[0]
-    first = unit_a.shape[0] - 16
-    copies = load(features, matrix, features_v, matrix_v, sems, y * half, half)
-    row_ids = ids[...].reshape(1, 2 * half)
-    row_ids = jnp.where(y == 0, row_ids[:, :half], row_ids[:, half:])
-    part_ids = jnp.where(core == 0, row_ids[:, : half // 2], row_ids[:, half // 2 :])
-    count = jnp.full((1, 256), filled[0], jnp.int32)
-    row = lax.broadcasted_iota(jnp.int32, (16, 1024), 0)
-    for out, value in ((unit, part_ids), (unit_a, row_ids)):
-        digits = []
-        for number in (value, count):
-            missing = 256 - number.shape[1]
-            for digit in (number & 255, number >> 8):
-                digits.append(digit.astype(jnp.float32))
-                if missing:
-                    digits.append(jnp.zeros((1, missing), jnp.float32))
-        facts = jnp.where(row == 0, jnp.concatenate(digits, axis=1), 0.0).astype(jnp.bfloat16)
-        begin = out.shape[0] - 16
-        out[begin:] = jnp.zeros((16, out.shape[1]), jnp.bfloat16)
-        out[begin:, :1024] = facts
+    copies = load(features, matrix, features_v, matrix_v, sems, me * rows, rows)
+    all_ids = ids[...].reshape(1, 4 * rows)
+    here = all_ids[:, :rows]
+    for k in range(1, 4):
+        here = jnp.where(me == k, all_ids[:, k * rows : (k + 1) * rows], here)
+    here = jnp.concatenate([here, jnp.zeros((1, 128 - rows), jnp.int32)], axis=1)
+    count = jnp.full((1, 128), filled[0], jnp.int32)
+    digits = [here & 255, here >> 8, count & 255, count >> 8]
+    digits.append(jnp.zeros((1, width - 512), jnp.int32))
+    facts = jnp.concatenate(digits, axis=1).astype(jnp.float32)
+    row = lax.broadcasted_iota(jnp.int32, (FACTS, width), 0)
+    facts = jnp.where(row == 0, facts, 0.0)
     length = multiply(copies, features_v, matrix_v, raw)
-    value = (raw[...] / length).astype(jnp.bfloat16)
-    unit[: half // 2] = jnp.where(core == 0, value[: half // 2], value[half // 2 :])
-    unit_a[:first] = value[:first]
-    unit_b[...] = value[first:]
-
-
-def half_unit(ids, filled, features, matrix, first):
+    unit[...] = jnp.concatenate([raw[...] / length, facts], axis=0).astype(jnp.bfloat16)
+
+
+def part_unit(ids, filled, features, matrix):
     rows, depth = features.shape
     width = matrix.shape[1]
-    half = rows // 2
+    part = rows // 4
     return pl.pallas_call(
-        half_unit_kernel,
-        out_shape=[
-            jax.ShapeDtypeStruct((count, width), jnp.bfloat16)
-            for count in (half // 2 + 16, first + 16, half - first)
-        ],
+        part_unit_kernel,
+        out_shape=jax.ShapeDtypeStruct((part + FACTS, width), jnp.bfloat16),
         in_specs=[VMEM, SMEM, ANY, ANY],
-        out_specs=[VMEM] * 3,
+        out_specs=VMEM,
         scratch_shapes=[
-            pltpu.VMEM((half, depth), jnp.bfloat16),
+            pltpu.VMEM((part, depth), jnp.bfloat16),
             pltpu.VMEM((depth, width), jnp.bfloat16),
-            pltpu.VMEM((half, width), jnp.float32),
+            pltpu.VMEM((part, width), jnp.float32),
             pltpu.SemaphoreType.DMA((STEPS + 1,)),
         ],
         compiler_params=pltpu.CompilerParams(vmem_limit_bytes=60 << 20),
-        cost_estimate=pl.CostEstimate(flops=rows * depth * width, bytes_accessed=2 * depth * width, transcendentals=0),
-        name="half_unit",
+        cost_estimate=pl.CostEstimate(
+            flops=rows * depth * width, bytes_accessed=2 * depth * width, transcendentals=0
+        ),
+        name="part_unit",
     )(ids, filled, features, matrix)
 
 
@@ -155,25 +141,25 @@
 
 def pair_kernel(cuts, first, final, *refs):
     refs = list(refs)
-    masks = refs[:4]
-    scale, shift, filled_here = refs[4][0], refs[5][0], refs[6][0]
+    scale, shift, filled_here = refs[0][0], refs[1][0], refs[2][0]
+    masks = [ref[0] for ref in refs[3:7]]
     ids_here, unit_bf = refs[7:9]
     del refs[:9]
     blocks = [refs.pop(0) for _ in cuts]
     if not first:
         old_dunit, old_losses = refs.pop(0), refs.pop(0)
     if final:
-        old_facts, unit, length = refs.pop(0), refs.pop(0), refs.pop(0)
+        unit, length = refs.pop(0), refs.pop(0)
         keep, send, stacked, total = refs
     else:
-        total, losses_out, facts_out, stacked = refs
+        total, losses_out, stacked = refs
     me = lax.axis_index("group")
-    y, core = me // 2, me % 2
     rows = unit_bf.shape[0]
-    half = rows // 2
+    part = rows // 4
     offset = 0
-    for block, (_, begin, count) in zip(blocks, cuts):
-        stacked[offset : offset + count] = block[:count]
+    values = [block[...] for block in blocks]
+    for value, (_, _, count, _) in zip(values, cuts):
+        stacked[offset : offset + count] = value[:count]
         offset += count
     scores = lax.dot_general(
         unit_bf[...], stacked[...], (((1,), (1,)), ((), ())), preferred_element_type=jnp.float32
@@ -184,22 +170,16 @@
     losses = jnp.zeros((1, 128), jnp.float32) if first else old_losses[0:1]
     slopes = []
     offset = 0
-    for k, (slot, begin, count) in enumerate(cuts):
-        wanted = jnp.where(core == 0, SLOTS[0][slot], SLOTS[1][slot])
+    for mask, begin, count, owner in cuts:
         turn = jnp.int32(-1)
-        for e, mask in enumerate(masks):
-            turn = jnp.where(mask[0] == wanted, jnp.bitwise_xor(me, e), turn)
-        if final:
-            fact = old_facts[16 * k : 16 * (k + 1)]
-        else:
-            fact = blocks[k][count : count + 16]
-            facts_out[16 * k : 16 * (k + 1)] = fact
-        fact = fact.astype(jnp.float32)[0:1]
-        ids = fact[:, begin : begin + count] + 256.0 * fact[:, 256 + begin : 256 + begin + count]
-        filled = fact[:, 512:513] + 256.0 * fact[:, 768:769]
-        base = me * (half // 2) if slot < 3 else y * half + begin
-        place = base + lax.broadcasted_iota(jnp.int32, (1, count), 1)
-        used = used_here & (place < filled.astype(jnp.int32)) & (turn >= 0)
+        for e, other in enumerate(masks):
+            turn = jnp.where(other == mask, jnp.bitwise_xor(me, e), turn)
+        fact = values[owner][-FACTS:].astype(jnp.float32)[0:1]
+        ids = fact[:, begin : begin + count] + 256.0 * fact[:, 128 + begin : 128 + begin + count]
+        filled = fact[:, 256 : 256 + count] + 256.0 * fact[:, 384 : 384 + count]
+        place = me * part + begin + lax.broadcasted_iota(jnp.int32, (1, count), 1)
+        there = (place < filled.astype(jnp.int32)) & (turn >= 0)
+        used = used_here & there
         signs = jnp.where(ids_here[:, :1] == ids, -1.0, 1.0)
         logits = signs * (scale * scores[:, offset : offset + count] + shift)
         small = jnp.exp(-jnp.abs(logits))
@@ -234,7 +214,7 @@
 
 def pair_terms(scalars, ids_here, unit_bf, blocks, cuts, old=None, final=None):
     rows, width = unit_bf.shape
-    total = sum(count for _, _, count in cuts)
+    total = sum(count for _, _, count, _ in cuts)
     args = [*scalars, ids_here, unit_bf, *blocks]
     scratch = [pltpu.VMEM((total, width), jnp.bfloat16)]
     if old is not None:
@@ -247,7 +227,6 @@
         shapes = [
             jax.ShapeDtypeStruct((rows, width), jnp.float32),
             jax.ShapeDtypeStruct((8, 128), jnp.float32),
-            jax.ShapeDtypeStruct((16 * len(blocks), width), jnp.bfloat16),
         ]
     return pl.pallas_call(
         functools.partial(pair_kernel, cuts, old is None, final is not None),
@@ -333,36 +312,31 @@
 
 def small_plan(features, matrix, ids, filled, mask, scale, shift):
     rows = features.shape[0]
-    half_rows = rows // 2
-    rest = half_rows - FIRST
-
-    part, half_a, half_b = half_unit(ids, filled, features, matrix, FIRST)
-    near = swap_cores(part, 1, 1)
-    far_a = swap_cores(half_a, 4, 6)
-    side = swap_cores(part, 2, 2)
-    unit, unit_bf, length, column = whole_unit(ids, after(features, part), matrix)
-    far_b = swap_cores(after(half_b, side), 4, 6)
-    side_x = swap_cores(after(side, near, unit_bf), 1, 1)
-    other_masks = [swap(after(mask, side), "group", k) for k in (1, 2, 3)]
-    far_ax = swap_cores(after(far_a, side_x, *other_masks), 1, 1)
-
-    common = ([mask, *other_masks, scale, shift, filled], column, unit_bf)
-    quarter = half_rows // 2
+    part = rows // 4
+
+    mine = part_unit(ids, filled, features, matrix)
+    far = trade(mine, 6, 0)
+    near = trade(mine, 1, 0)
+    side = trade(mine, 2, 0)
+    unit, unit_bf, length, column = whole_unit(ids, after(features, mine), matrix)
+    others = [swap(after(mask, unit_bf), "group", k) for k in (1, 2, 3)]
+    far_s = trade(after(far, unit_bf, *others), 2, 0)
+    far_x = trade(after(far, unit_bf, *others), 1, 0)
+    side_x = trade(after(side, unit_bf, near), 1, 0)
+    common = ([scale, shift, filled, mask, *others], column, unit_bf)
     early = pair_terms(
-        *common,
-        [near, side, side_x],
-        ((0, 0, quarter), (1, 0, quarter), (2, 0, quarter)),
-    )
-    far_bx = swap_cores(after(far_b, early[1]), 1, 1)
+        *common, [near, side, far], ((1, 0, part, 0), (2, 0, part, 1), (6, 0, part, 2))
+    )
+    last = trade(after(far_x, early[1]), 2, 0)
     middle = pair_terms(
-        *common, [far_a, far_ax], ((3, 0, FIRST), (4, 0, FIRST)), old=early[:2]
+        *common, [far_s, far_x], ((4, 0, part, 0), (7, 0, part, 1)), old=early
     )
     keep, send = pair_terms(
         *common,
-        [far_b, far_bx],
-        ((3, FIRST, rest), (4, FIRST, rest)),
-        old=middle[:2],
-        final=[middle[2], unit, length],
+        [side_x, last],
+        ((3, 0, part, 0), (5, 0, part, 1)),
+        old=middle,
+        final=[unit, length],
     )
     own, send = combine(keep, swap(send, "group", 1))
     me = lax.axis_index("group")

time: 72.4 us -> 63.1 us (0.87)
  waiting for transfers between devices: 21.4 us -> 15.7 us
  starting transfers between devices: 19.1 us -> 16.9 us
  Pallas kernels: 25.2 us -> 23.9 us
    ppermute x7, waiting for transfers between devices: 9.25 us -> 3.15 us  [trade(): return lax.ppermute(block, AXES, route)]
    ppermute x7, starting transfers between devices: 15 us -> 12.8 us  [trade(): return lax.ppermute(block, AXES, route)]
    pallas_call x3, Pallas kernels: 13.2 us -> 12.3 us  [pair_terms(): pl.pallas_call(functools.partial(pair_kernel, cuts, old is None, final is...]
    unnamed x9 -> x7, local copies, waits for them, and re-layouts: 3.08 us -> 3.07 us
  transfers between devices with their start and end apart: 12 -> 12, of which waited for: 7 -> 7; matrix products, arithmetic and copies ran while one was open for 1% -> 1% of each run, Pallas kernels for 17% -> 18%
where the time goes in v4:
time: 63.1 us; the launch traced here: 62.8 us
  Pallas kernels  23.9 us (38%)
  starting transfers between devices  16.9 us (27%)
  waiting for transfers between devices  15.7 us (25%)
  between operations  3.31 us (5%)
  local copies, waits for them, and re-layouts  3.07 us (5%)
    ppermute x7, starting transfers between devices, trade(): return lax.ppermute(block, AXES, route)  12.8 us
    ppermute x5, waiting for transfers between devices, swap(): return lax.ppermute(block, axis, [(i, i ^ mask) for i in range(count)])  12.5 us
    pallas_call x3, Pallas kernels, pair_terms(): pl.pallas_call(functools.partial(pair_kernel, cuts, old is None, final is...  12.3 us
    pallas_call x1, Pallas kernels, part_unit(): pl.pallas_call(part_unit_kernel, out_shape=jax.ShapeDtypeStruct((part + F...  4.35 us
    ppermute x5, starting transfers between devices, swap(): return lax.ppermute(block, axis, [(i, i ^ mask) for i in range(count)])  4.04 us
    pallas_call x1, Pallas kernels, whole_unit(): pl.pallas_call(whole_unit_kernel, out_shape=[jax.ShapeDtypeStruct((rows,...  3.53 us
    ppermute x7, waiting for transfers between devices, trade(): return lax.ppermute(block, AXES, route)  3.15 us
    unnamed x7, local copies, waits for them, and re-layouts  3.07 us
  transfers between devices with their start and end apart: 12, of which 7 were waited for; matrix products, arithmetic and copies ran while one was open for 1% of the time, Pallas kernels for 18%

profile of v4, /device:TPU:0, one launch (start us, length us, event | category | flops | bytes accessed | tf_op | source)
XLA Modules:
  0.0 62.8 jit_solution(11794712437211361577)
XLA Ops:
  1.3 0.0 copy-start.1
  1.3 0.0 copy-start.2
  1.3 4.4 %part_unit.1 = bf16[104,1536]{1,0:T(8,128)(2,1)} custom-call(s32[384]{0:T(512)} %ids.3, s32[1]{0:T(128)S(6)} %copy.10.filled.refs_2_, bf16[384,1536]{1,0:T(8,128)(2,1)} %features.2, bf16[1536,1536]{1,0:T(8,128)(2,1)} %matrix.3), custom_call_target="tpu_custom_call" | custom-call | flops 905969664 | bytes 4718592 | tf_op jit(solution)/shard_map/part_unit/pallas_call | solution.py:89
  5.7 5.1 %collective-permute-start.6 = (bf16[104,1536]{1,0:T(8,128)(2,1)}, bf16[104,1536]{1,0:T(8,128)(2,1)S(1)}, u32[]{:S(2)}, u32[]{:S(2)}) collective-permute-start(bf16[104,1536]{1,0:T(8,128)(2,1)} %part_unit.1), channel_id=1, source_target_pairs={{0,24},{1,25},{2,26},{3,27},{4,28},{5,29},{6,30},{7,31},{8,16},{9,... | collective-permute-start | bytes 958472 | tf_op jit(solution)/shard_map/ppermute | solution.py:31
  10.8 0.0 collective-permute-start.3
  10.8 1.5 %collective-permute-start.4 = (bf16[104,1536]{1,0:T(8,128)(2,1)}, bf16[104,1536]{1,0:T(8,128)(2,1)S(1)}, u32[]{:S(2)}, u32[]{:S(2)}) collective-permute-start(bf16[104,1536]{1,0:T(8,128)(2,1)} %part_unit.1), channel_id=1, source_target_pairs={{0,4},{1,5},{2,6},{3,7},{4,0},{5,1},{6,2},{7,3},{8,12},{9,13},{10,... | collective-permute-start | bytes 958472 | tf_op jit(solution)/shard_map/ppermute | solution.py:31
  12.3 0.0 copy-done.1
  12.3 0.0 copy-done.2
  12.3 0.0 copy-start
  12.3 2.3 %copy-done = bf16[1536,1536]{1,0:T(8,128)(2,1)S(1)} copy-done((bf16[1536,1536]{1,0:T(8,128)(2,1)S(1)}, bf16[1536,1536]{1,0:T(8,128)(2,1)}, u32[]{:S(2)}) %copy-start) | copy-done | bytes 4718616
  14.6 3.5 %whole_unit.1 = (f32[384,1536]{1,0:T(8,128)S(1)}, bf16[384,1536]{1,0:T(8,128)(2,1)S(1)}, f32[384,128]{1,0:T(8,128)S(1)}, f32[384,128]{1,0:T(8,128)S(1)}) custom-call(s32[384]{0:T(512)S(1)} %copy-done.2, bf16[384,1536]{1,0:T(8,128)(2,1)S(1)} %copy-done.1, bf16[1536,1536]{1,0:T(8,128)(2,1)S(1)} %copy-done), custom_call_target="tpu_custom_call" | custom-call | flops 1811939328 | bytes 9437184 | tf_op jit(solution)/shard_map/whole_unit/pallas_call | solution.py:121
  18.1 0.1 collective-permute-start
  18.2 1.6 %collective-permute-start.1 = (s32[1]{0:T(128)}, s32[1]{0:T(128)}, u32[]{:S(2)}, u32[]{:S(2)}) collective-permute-start(s32[1]{0:T(128)} %param.11), channel_id=1, source_target_pairs={{0,2},{1,3},{2,0},{3,1},{4,6},{5,7},{6,4},{7,5},{8,10},{9,11},{10,... | collective-permute-start | bytes 20 | tf_op jit(solution)/shard_map/ppermute | solution.py:21
  19.8 0.0 collective-permute-done.refs_4_
  19.8 1.0 %collective-permute-start.2 = (s32[1]{0:T(128)}, s32[1]{0:T(128)}, u32[]{:S(2)}, u32[]{:S(2)}) collective-permute-start(s32[1]{0:T(128)} %param.11), channel_id=1, source_target_pairs={{0,3},{1,2},{2,1},{3,0},{4,7},{5,6},{6,5},{7,4},{8,11},{9,10},{10,... | collective-permute-start | bytes 20 | tf_op jit(solution)/shard_map/ppermute | solution.py:21
  20.8 1.3 %collective-permute-done.1.refs_5_ = s32[1]{0:T(128)} collective-permute-done((s32[1]{0:T(128)}, s32[1]{0:T(128)}, u32[]{:S(2)}, u32[]{:S(2)}) %collective-permute-start.1) | collective-permute-done | bytes 36 | tf_op jit(solution)/shard_map/ppermute | solution.py:21
  22.1 0.9 %collective-permute-done.2.refs_6_ = s32[1]{0:T(128)} collective-permute-done((s32[1]{0:T(128)}, s32[1]{0:T(128)}, u32[]{:S(2)}, u32[]{:S(2)}) %collective-permute-start.2) | collective-permute-done | bytes 36 | tf_op jit(solution)/shard_map/ppermute | solution.py:21
  23.0 0.0 collective-permute-done.6.refs_11_
  23.0 0.5 collective-permute-start.7
  25.5 3.1 %collective-permute-start.9 = (bf16[104,1536]{1,0:T(8,128)(2,1)S(1)}, bf16[104,1536]{1,0:T(8,128)(2,1)S(1)}, u32[]{:S(2)}, u32[]{:S(2)}) collective-permute-start(bf16[104,1536]{1,0:T(8,128)(2,1)S(1)} %collective-permute-done.6.refs_11_), channel_id=1, source_target_pairs={{0,8},{1,9},{2,10},{3,11},{4,12},{5,13},{6,14},{7,15},{8,0},{9,1},... | collective-permute-start | bytes 958472 | tf_op jit(solution)/shard_map/ppermute | solution.py:31
  28.6 0.0 collective-permute-done.3.refs_10_
  28.6 0.0 collective-permute-done.4.refs_9_
  28.6 0.5 collective-permute-start.5
  29.1 4.1 %pair_terms.3 = (f32[384,1536]{1,0:T(8,128)S(1)}, f32[8,128]{1,0:T(8,128)S(1)}) custom-call(f32[1]{0:T(128)S(6)} %copy.12.refs_0_, f32[1]{0:T(128)S(6)} %copy.13.refs_1_, s32[1]{0:T(128)S(6)} %copy.10.filled.refs_2_, s32[1]{0:T(128)S(6)} %copy.11.refs_3_, s32[1]{0:T(128)} %collective-permute-done.refs_4_, s32[1]{0:T(128)} %collective-permute-done.1.refs_5_, ...), custom_call_target="tpu_custom_call" | custom-call | flops 679477248 | bytes 4718592 | tf_op jit(solution)/shard_map/pair_terms/pallas_call | solution.py:231
  33.2 0.2 collective-permute-done.7.refs_10_
  33.4 2.1 %collective-permute-start.8 = (bf16[104,1536]{1,0:T(8,128)(2,1)S(1)}, bf16[104,1536]{1,0:T(8,128)(2,1)S(1)}, u32[]{:S(2)}, u32[]{:S(2)}) collective-permute-start(bf16[104,1536]{1,0:T(8,128)(2,1)S(1)} %collective-permute-done.7.refs_10_), channel_id=1, source_target_pairs={{0,8},{1,9},{2,10},{3,11},{4,12},{5,13},{6,14},{7,15},{8,0},{9,1},... | collective-permute-start | bytes 958472 | tf_op jit(solution)/shard_map/ppermute | solution.py:31
  35.4 0.0 collective-permute-done.9.refs_9_
  35.4 3.8 %pair_terms.4 = (f32[384,1536]{1,0:T(8,128)S(1)}, f32[8,128]{1,0:T(8,128)S(1)}) custom-call(f32[1]{0:T(128)S(6)} %copy.12.refs_0_, f32[1]{0:T(128)S(6)} %copy.13.refs_1_, s32[1]{0:T(128)S(6)} %copy.10.filled.refs_2_, s32[1]{0:T(128)S(6)} %copy.11.refs_3_, s32[1]{0:T(128)} %collective-permute-done.refs_4_, s32[1]{0:T(128)} %collective-permute-done.1.refs_5_, ...), custom_call_target="tpu_custom_call" | custom-call | flops 452984832 | bytes 4718592 | tf_op jit(solution)/shard_map/pair_terms/pallas_call | solution.py:231
  39.2 0.4 collective-permute-done.5.refs_9_
  39.7 2.6 %collective-permute-done.8.refs_10_ = bf16[104,1536]{1,0:T(8,128)(2,1)S(1)} collective-permute-done((bf16[104,1536]{1,0:T(8,128)(2,1)S(1)}, bf16[104,1536]{1,0:T(8,128)(2,1)S(1)}, u32[]{:S(2)}, u32[]{:S(2)}) %collective-permute-start.8) | collective-permute-done | bytes 319520 | tf_op jit(solution)/shard_map/ppermute | solution.py:31
  42.2 4.4 %pair_terms.5 = (f32[392,768]{1,0:T(8,128)S(1)}, f32[392,768]{1,0:T(8,128)S(1)}) custom-call(f32[1]{0:T(128)S(6)} %copy.12.refs_0_, f32[1]{0:T(128)S(6)} %copy.13.refs_1_, s32[1]{0:T(128)S(6)} %copy.10.filled.refs_2_, s32[1]{0:T(128)S(6)} %copy.11.refs_3_, s32[1]{0:T(128)} %collective-permute-done.refs_4_, s32[1]{0:T(128)} %collective-permute-done.1.refs_5_, ...), custom_call_target="tpu_custom_call" | custom-call | flops 452984832 | bytes 4718592 | tf_op jit(solution)/shard_map/pair_terms/pallas_call | solution.py:231
  46.6 0.1 collective-permute-start.10
  46.7 2.9 %collective-permute-done.10.arrived = f32[392,768]{1,0:T(8,128)S(1)} collective-permute-done((f32[392,768]{1,0:T(8,128)S(1)}, f32[392,768]{1,0:T(8,128)S(1)}, u32[]{:S(2)}, u32[]{:S(2)}) %collective-permute-start.10) | collective-permute-done | bytes 1204256 | tf_op jit(solution)/shard_map/ppermute | solution.py:21
  49.6 0.8 %combine.1 = (f32[392,384]{1,0:T(8,128)S(1)}, bf16[400,384]{1,0:T(8,128)(2,1)}) custom-call(f32[392,768]{1,0:T(8,128)S(1)} %get-tuple-element.32.keep, f32[392,768]{1,0:T(8,128)S(1)} %collective-permute-done.10.arrived), custom_call_target="tpu_custom_call" | custom-call | flops 294912 | bytes 2359296 | tf_op jit(solution)/shard_map/combine/pallas_call | solution.py:259
  50.4 1.3 %collective-permute-start.11 = (bf16[400,384]{1,0:T(8,128)(2,1)}, bf16[400,384]{1,0:T(8,128)(2,1)S(1)}, u32[]{:S(2)}, u32[]{:S(2)}) collective-permute-start(bf16[400,384]{1,0:T(8,128)(2,1)} %get-tuple-element.35), channel_id=1, source_target_pairs={{0,2},{1,3},{2,0},{3,1},{4,6},{5,7},{6,4},{7,5},{8,10},{9,11},{10,... | collective-permute-start | bytes 921608 | tf_op jit(solution)/shard_map/ppermute | solution.py:21
  51.8 0.7 %copy.9 = bf16[384,1536]{0,1:T(8,128)(2,1)S(1)} copy(bf16[384,1536]{1,0:T(8,128)(2,1)S(1)} %copy-done.1) | data formatting | bytes 2359296 | tf_op args[0]
  52.5 7.4 %collective-permute-done.11.arrived = bf16[400,384]{1,0:T(8,128)(2,1)S(1)} collective-permute-done((bf16[400,384]{1,0:T(8,128)(2,1)}, bf16[400,384]{1,0:T(8,128)(2,1)S(1)}, u32[]{:S(2)}, u32[]{:S(2)}) %collective-permute-start.11) | collective-permute-done | bytes 307232 | tf_op jit(solution)/shard_map/ppermute | solution.py:21
  60.0 2.9 %gradient.1 = (f32[1536,384]{1,0:T(8,128)}, f32[1,1]{1,0:T(1,128)}) custom-call(s32[1]{0:T(128)} %bitcast.me, f32[392,384]{1,0:T(8,128)S(1)} %get-tuple-element.34.own, bf16[400,384]{1,0:T(8,128)(2,1)S(1)} %collective-permute-done.11.arrived, bf16[1536,384]{1,0:T(8,128)(2,1)S(1)} %bitcast.2), custom_call_target="tpu_custom_call" | custom-call | flops 452984832 | bytes 2359296 | tf_op jit(solution)/shard_map/gradient/pallas_call | solution.py:292
Async XLA Ops:
  1.3 11.0 %copy-start.1 = (bf16[384,1536]{1,0:T(8,128)(2,1)S(1)}, bf16[384,1536]{1,0:T(8,128)(2,1)}, u32[]{:S(2)}) copy-start(bf16[384,1536]{1,0:T(8,128)(2,1)} %features.2) | copy-start | bytes 3538948
  1.3 11.0 %copy-start.2 = (s32[384]{0:T(512)S(1)}, s32[384]{0:T(512)}, u32[]{:S(2)}) copy-start(s32[384]{0:T(512)} %ids.3) | copy-start | bytes 4612
  5.7 17.4 %collective-permute-start.6 = (bf16[104,1536]{1,0:T(8,128)(2,1)}, bf16[104,1536]{1,0:T(8,128)(2,1)S(1)}, u32[]{:S(2)}, u32[]{:S(2)}) collective-permute-start(bf16[104,1536]{1,0:T(8,128)(2,1)} %part_unit.1), channel_id=1, source_target_pairs={{0,24},{1,25},{2,26},{3,27},{4,28},{5,29},{6,30},{7,31},{8,16},{9,... | collective-permute-start | bytes 958472 | tf_op jit(solution)/shard_map/ppermute | solution.py:31
  10.8 17.8 %collective-permute-start.3 = (bf16[104,1536]{1,0:T(8,128)(2,1)}, bf16[104,1536]{1,0:T(8,128)(2,1)S(1)}, u32[]{:S(2)}, u32[]{:S(2)}) collective-permute-start(bf16[104,1536]{1,0:T(8,128)(2,1)} %part_unit.1), channel_id=1, source_target_pairs={{0,8},{1,9},{2,10},{3,11},{4,12},{5,13},{6,14},{7,15},{8,0},{9,1},... | collective-permute-start | bytes 958472 | tf_op jit(solution)/shard_map/ppermute | solution.py:31
  10.8 17.8 %collective-permute-start.4 = (bf16[104,1536]{1,0:T(8,128)(2,1)}, bf16[104,1536]{1,0:T(8,128)(2,1)S(1)}, u32[]{:S(2)}, u32[]{:S(2)}) collective-permute-start(bf16[104,1536]{1,0:T(8,128)(2,1)} %part_unit.1), channel_id=1, source_target_pairs={{0,4},{1,5},{2,6},{3,7},{4,0},{5,1},{6,2},{7,3},{8,12},{9,13},{10,... | collective-permute-start | bytes 958472 | tf_op jit(solution)/shard_map/ppermute | solution.py:31
  12.3 2.3 %copy-start = (bf16[1536,1536]{1,0:T(8,128)(2,1)S(1)}, bf16[1536,1536]{1,0:T(8,128)(2,1)}, u32[]{:S(2)}) copy-start(bf16[1536,1536]{1,0:T(8,128)(2,1)} %matrix.3) | copy-start | bytes 14155780
  18.1 1.7 %collective-permute-start = (s32[1]{0:T(128)}, s32[1]{0:T(128)}, u32[]{:S(2)}, u32[]{:S(2)}) collective-permute-start(s32[1]{0:T(128)} %param.11), channel_id=1, source_target_pairs={{0,1},{1,0},{2,3},{3,2},{4,5},{5,4},{6,7},{7,6},{8,9},{9,8},{10,11... | collective-permute-start | bytes 20 | tf_op jit(solution)/shard_map/ppermute | solution.py:21
  18.2 3.8 %collective-permute-start.1 = (s32[1]{0:T(128)}, s32[1]{0:T(128)}, u32[]{:S(2)}, u32[]{:S(2)}) collective-permute-start(s32[1]{0:T(128)} %param.11), channel_id=1, source_target_pairs={{0,2},{1,3},{2,0},{3,1},{4,6},{5,7},{6,4},{7,5},{8,10},{9,11},{10,... | collective-permute-start | bytes 20 | tf_op jit(solution)/shard_map/ppermute | solution.py:21
  19.8 3.2 %collective-permute-start.2 = (s32[1]{0:T(128)}, s32[1]{0:T(128)}, u32[]{:S(2)}, u32[]{:S(2)}) collective-permute-start(s32[1]{0:T(128)} %param.11), channel_id=1, source_target_pairs={{0,3},{1,2},{2,1},{3,0},{4,7},{5,6},{6,5},{7,4},{8,11},{9,10},{10,... | collective-permute-start | bytes 20 | tf_op jit(solution)/shard_map/ppermute | solution.py:21
  23.0 10.4 %collective-permute-start.7 = (bf16[104,1536]{1,0:T(8,128)(2,1)S(1)}, bf16[104,1536]{1,0:T(8,128)(2,1)S(1)}, u32[]{:S(2)}, u32[]{:S(2)}) collective-permute-start(bf16[104,1536]{1,0:T(8,128)(2,1)S(1)} %collective-permute-done.6.refs_11_), channel_id=1, source_target_pairs={{0,4},{1,5},{2,6},{3,7},{4,0},{5,1},{6,2},{7,3},{8,12},{9,13},{10,... | collective-permute-start | bytes 958472 | tf_op jit(solution)/shard_map/ppermute | solution.py:31
  25.5 9.9 %collective-permute-start.9 = (bf16[104,1536]{1,0:T(8,128)(2,1)S(1)}, bf16[104,1536]{1,0:T(8,128)(2,1)S(1)}, u32[]{:S(2)}, u32[]{:S(2)}) collective-permute-start(bf16[104,1536]{1,0:T(8,128)(2,1)S(1)} %collective-permute-done.6.refs_11_), channel_id=1, source_target_pairs={{0,8},{1,9},{2,10},{3,11},{4,12},{5,13},{6,14},{7,15},{8,0},{9,1},... | collective-permute-start | bytes 958472 | tf_op jit(solution)/shard_map/ppermute | solution.py:31
  28.6 11.1 %collective-permute-start.5 = (bf16[104,1536]{1,0:T(8,128)(2,1)S(1)}, bf16[104,1536]{1,0:T(8,128)(2,1)S(1)}, u32[]{:S(2)}, u32[]{:S(2)}) collective-permute-start(bf16[104,1536]{1,0:T(8,128)(2,1)S(1)} %collective-permute-done.3.refs_10_), channel_id=1, source_target_pairs={{0,4},{1,5},{2,6},{3,7},{4,0},{5,1},{6,2},{7,3},{8,12},{9,13},{10,... | collective-permute-start | bytes 958472 | tf_op jit(solution)/shard_map/ppermute | solution.py:31
  33.4 8.8 %collective-permute-start.8 = (bf16[104,1536]{1,0:T(8,128)(2,1)S(1)}, bf16[104,1536]{1,0:T(8,128)(2,1)S(1)}, u32[]{:S(2)}, u32[]{:S(2)}) collective-permute-start(bf16[104,1536]{1,0:T(8,128)(2,1)S(1)} %collective-permute-done.7.refs_10_), channel_id=1, source_target_pairs={{0,8},{1,9},{2,10},{3,11},{4,12},{5,13},{6,14},{7,15},{8,0},{9,1},... | collective-permute-start | bytes 958472 | tf_op jit(solution)/shard_map/ppermute | solution.py:31
  46.6 2.9 %collective-permute-start.10 = (f32[392,768]{1,0:T(8,128)S(1)}, f32[392,768]{1,0:T(8,128)S(1)}, u32[]{:S(2)}, u32[]{:S(2)}) collective-permute-start(f32[392,768]{1,0:T(8,128)S(1)} %get-tuple-element.33), channel_id=1, source_target_pairs={{0,1},{1,0},{2,3},{3,2},{4,5},{5,4},{6,7},{7,6},{8,9},{9,8},{10,11... | collective-permute-start | bytes 3612680 | tf_op jit(solution)/shard_map/ppermute | solution.py:21
  50.4 9.5 %collective-permute-start.11 = (bf16[400,384]{1,0:T(8,128)(2,1)}, bf16[400,384]{1,0:T(8,128)(2,1)S(1)}, u32[]{:S(2)}, u32[]{:S(2)}) collective-permute-start(bf16[400,384]{1,0:T(8,128)(2,1)} %get-tuple-element.35), channel_id=1, source_target_pairs={{0,2},{1,3},{2,0},{3,1},{4,6},{5,7},{6,4},{7,5},{8,10},{9,11},{10,... | collective-permute-start | bytes 921608 | tf_op jit(solution)/shard_map/ppermute | solution.py:21

commit v5 on v4

--- a/solution.py
+++ b/solution.py
@@ -13,7 +13,6 @@
 SMALL = pl.CostEstimate(flops=1, bytes_accessed=1, transcendentals=0)
 ANY = pl.BlockSpec(memory_space=pl.ANY)
 VMEM = pl.BlockSpec(memory_space=pltpu.VMEM)
-SMEM = pl.BlockSpec(memory_space=pltpu.SMEM)
 
 
 def swap(block, axis, mask):
@@ -63,16 +62,24 @@
     return jnp.sqrt(jnp.sum(raw[...] * raw[...], axis=1, keepdims=True) + 1e-06)
 
 
-def part_unit_kernel(ids, filled, features, matrix, unit, features_v, matrix_v, raw, sems):
+def part_unit_kernel(ids, filled, features, matrix, unit, ids_v, filled_s, features_v, matrix_v, raw, sems, small_sems):
     rows, width = raw.shape
     me = lax.axis_index("group")
     copies = load(features, matrix, features_v, matrix_v, sems, me * rows, rows)
-    all_ids = ids[...].reshape(1, 4 * rows)
+    small = [
+        pltpu.make_async_copy(ids, ids_v, small_sems.at[0]),
+        pltpu.make_async_copy(filled, filled_s, small_sems.at[1]),
+    ]
+    for copy in small:
+        copy.start()
+    for copy in small:
+        copy.wait()
+    all_ids = ids_v[...].reshape(1, 4 * rows)
     here = all_ids[:, :rows]
     for k in range(1, 4):
         here = jnp.where(me == k, all_ids[:, k * rows : (k + 1) * rows], here)
     here = jnp.concatenate([here, jnp.zeros((1, 128 - rows), jnp.int32)], axis=1)
-    count = jnp.full((1, 128), filled[0], jnp.int32)
+    count = jnp.full((1, 128), filled_s[0], jnp.int32)
     digits = [here & 255, here >> 8, count & 255, count >> 8]
     digits.append(jnp.zeros((1, width - 512), jnp.int32))
     facts = jnp.concatenate(digits, axis=1).astype(jnp.float32)
@@ -89,13 +96,16 @@
     return pl.pallas_call(
         part_unit_kernel,
         out_shape=jax.ShapeDtypeStruct((part + FACTS, width), jnp.bfloat16),
-        in_specs=[VMEM, SMEM, ANY, ANY],
+        in_specs=[ANY] * 4,
         out_specs=VMEM,
         scratch_shapes=[
+            pltpu.VMEM((rows,), jnp.int32),
+            pltpu.SMEM((1,), jnp.int32),
             pltpu.VMEM((part, depth), jnp.bfloat16),
             pltpu.VMEM((depth, width), jnp.bfloat16),
             pltpu.VMEM((part, width), jnp.float32),
             pltpu.SemaphoreType.DMA((STEPS + 1,)),
+            pltpu.SemaphoreType.DMA((2,)),
         ],
         compiler_params=pltpu.CompilerParams(vmem_limit_bytes=60 << 20),
         cost_estimate=pl.CostEstimate(
@@ -105,17 +115,21 @@
     )(ids, filled, features, matrix)
 
 
-def whole_unit_kernel(ids, features, matrix, unit, unit_bf, length, column, features_v, matrix_v, sems):
+def whole_unit_kernel(ids, filled, scale, shift, features, matrix, unit, unit_bf, length, column, numbers, features_v, matrix_v, sems):
     rows = unit.shape[0]
     copies = load(features, matrix, features_v, matrix_v, sems, 0, rows)
     column[...] = jnp.broadcast_to(ids[...].reshape(1, rows).astype(jnp.float32), (128, rows)).T
+    numbers[0:1] = jnp.broadcast_to(scale[...].reshape(1, 1), (1, 128))
+    numbers[1:2] = jnp.broadcast_to(shift[...].reshape(1, 1), (1, 128))
+    numbers[2:3] = jnp.broadcast_to(filled[...].reshape(1, 1), (1, 128)).astype(jnp.float32)
+    numbers[3:] = jnp.zeros((5, 128), jnp.float32)
     norm = multiply(copies, features_v, matrix_v, unit)
     length[...] = jnp.broadcast_to(norm, length.shape)
     unit[...] = unit[...] / norm
     unit_bf[...] = unit[...].astype(jnp.bfloat16)
 
 
-def whole_unit(ids, features, matrix):
+def whole_unit(ids, filled, scale, shift, features, matrix):
     rows, depth = features.shape
     width = matrix.shape[1]
     return pl.pallas_call(
@@ -125,26 +139,29 @@
             jax.ShapeDtypeStruct((rows, width), jnp.bfloat16),
             jax.ShapeDtypeStruct((rows, 128), jnp.float32),
             jax.ShapeDtypeStruct((rows, 128), jnp.float32),
-        ],
-        in_specs=[VMEM, ANY, ANY],
-        out_specs=[VMEM] * 4,
+            jax.ShapeDtypeStruct((8, 128), jnp.float32),
+        ],
+        in_specs=[VMEM] * 4 + [ANY] * 2,
+        out_specs=[VMEM] * 5,
         scratch_shapes=[
             pltpu.VMEM((rows, depth), jnp.bfloat16),
             pltpu.VMEM((depth, width), jnp.bfloat16),
             pltpu.SemaphoreType.DMA((STEPS + 1,)),
         ],
         compiler_params=pltpu.CompilerParams(vmem_limit_bytes=28 << 20),
-        cost_estimate=pl.CostEstimate(flops=2 * rows * depth * width, bytes_accessed=4 * depth * width, transcendentals=0),
+        cost_estimate=pl.CostEstimate(
+            flops=2 * rows * depth * width, bytes_accessed=4 * depth * width, transcendentals=0
+        ),
         name="whole_unit",
-    )(ids, features, matrix)
+    )(ids, filled, scale, shift, features, matrix)
 
 
 def pair_kernel(cuts, first, final, *refs):
     refs = list(refs)
-    scale, shift, filled_here = refs[0][0], refs[1][0], refs[2][0]
-    masks = [ref[0] for ref in refs[3:7]]
-    ids_here, unit_bf = refs[7:9]
-    del refs[:9]
+    numbers = refs[0]
+    masks = [ref[0:1] for ref in refs[1:5]]
+    ids_here, unit_bf = refs[5:7]
+    del refs[:7]
     blocks = [refs.pop(0) for _ in cuts]
     if not first:
         old_dunit, old_losses = refs.pop(0), refs.pop(0)
@@ -165,22 +182,23 @@
         unit_bf[...], stacked[...], (((1,), (1,)), ((), ())), preferred_element_type=jnp.float32
     )
     row = lax.broadcasted_iota(jnp.int32, (rows, 1), 0)
-    used_here = row < filled_here
+    used_here = row < numbers[2:3, 0:1].astype(jnp.int32)
     lane = lax.broadcasted_iota(jnp.int32, (1, 128), 1)
     losses = jnp.zeros((1, 128), jnp.float32) if first else old_losses[0:1]
     slopes = []
     offset = 0
     for mask, begin, count, owner in cuts:
-        turn = jnp.int32(-1)
+        turn = jnp.full((1, 128), -1, jnp.int32)
         for e, other in enumerate(masks):
             turn = jnp.where(other == mask, jnp.bitwise_xor(me, e), turn)
         fact = values[owner][-FACTS:].astype(jnp.float32)[0:1]
         ids = fact[:, begin : begin + count] + 256.0 * fact[:, 128 + begin : 128 + begin + count]
         filled = fact[:, 256 : 256 + count] + 256.0 * fact[:, 384 : 384 + count]
         place = me * part + begin + lax.broadcasted_iota(jnp.int32, (1, count), 1)
-        there = (place < filled.astype(jnp.int32)) & (turn >= 0)
+        there = (place < filled.astype(jnp.int32)) & (turn[:, :count] >= 0)
         used = used_here & there
         signs = jnp.where(ids_here[:, :1] == ids, -1.0, 1.0)
+        scale, shift = numbers[0:1, :count], numbers[1:2, :count]
         logits = signs * (scale * scores[:, offset : offset + count] + shift)
         small = jnp.exp(-jnp.abs(logits))
         penalty = jnp.maximum(logits, 0.0) + jnp.log1p(small)
@@ -212,10 +230,10 @@
     send[rows : rows + 1, 0:128] = losses
 
 
-def pair_terms(scalars, ids_here, unit_bf, blocks, cuts, old=None, final=None):
+def pair_terms(numbers, masks, ids_here, unit_bf, blocks, cuts, old=None, final=None):
     rows, width = unit_bf.shape
     total = sum(count for _, _, count, _ in cuts)
-    args = [*scalars, ids_here, unit_bf, *blocks]
+    args = [numbers, *masks, ids_here, unit_bf, *blocks]
     scratch = [pltpu.VMEM((total, width), jnp.bfloat16)]
     if old is not None:
         args += old
@@ -231,7 +249,7 @@
     return pl.pallas_call(
         functools.partial(pair_kernel, cuts, old is None, final is not None),
         out_shape=shapes,
-        in_specs=[SMEM] * len(scalars) + [VMEM] * (len(args) - len(scalars)),
+        in_specs=[VMEM] * len(args),
         out_specs=[VMEM] * len(shapes),
         scratch_shapes=scratch,
         compiler_params=pltpu.CompilerParams(vmem_limit_bytes=28 << 20),
@@ -270,44 +288,48 @@
     )(keep, arrived)
 
 
-def gradient_kernel(me, own, arrived, features, grad, loss, draw):
+def gradient_kernel(own, arrived, features, grad, loss, draw, parts, sems):
     rows = features.shape[1]
-
-    @pl.when(pl.program_id(0) == 0)
-    def _():
-        draw[...] = (own[:rows] + arrived[:rows].astype(jnp.float32)).astype(jnp.bfloat16)
-        parts = arrived[rows:, 0:128].astype(jnp.float32)
-        total = own[rows : rows + 1, 0:128] + jnp.sum(parts, axis=0, keepdims=True)
-        lane = lax.broadcasted_iota(jnp.int32, (1, 128), 1)
-        value = jnp.sum(jnp.where(lane == me[0], total, 0.0))
-        loss[0, 0] = value / (rows * rows)
-
-    grad[...] = jnp.dot(features[...], draw[...], preferred_element_type=jnp.float32)
-
-
-def gradient(me, own, arrived, features_t):
+    steps, height = parts.shape[:2]
+    draw[...] = (own[:rows] + arrived[:rows].astype(jnp.float32)).astype(jnp.bfloat16)
+    copies = []
+    for k in range(steps):
+        at = pl.ds(k * height, height)
+        parts[k] = jnp.dot(features[at], draw[...], preferred_element_type=jnp.float32)
+        copies.append(pltpu.make_async_copy(parts.at[k], grad.at[at], sems.at[k]))
+        copies[k].start()
+    low = jnp.sum(arrived[rows:, 0:128].astype(jnp.float32), axis=0, keepdims=True)
+    total = own[rows : rows + 1, 0:128] + low
+    lane = lax.broadcasted_iota(jnp.int32, (1, 128), 1)
+    mine = jnp.where(lane == lax.axis_index("group"), total, 0.0)
+    loss[...] = jnp.sum(mine, axis=1, keepdims=True) / (rows * rows)
+    for copy in copies:
+        copy.wait()
+
+
+def gradient(own, arrived, features_t):
     depth, rows = features_t.shape
     width = own.shape[1]
-    steps = 4
+    steps = 6
     return pl.pallas_call(
         gradient_kernel,
         out_shape=[
             jax.ShapeDtypeStruct((depth, width), jnp.float32),
             jax.ShapeDtypeStruct((1, 1), jnp.float32),
         ],
-        grid=(steps,),
-        in_specs=[
-            SMEM,
-            pl.BlockSpec(own.shape, lambda i: (0, 0)),
-            pl.BlockSpec(arrived.shape, lambda i: (0, 0)),
-            pl.BlockSpec((depth // steps, rows), lambda i: (i, 0)),
-        ],
-        out_specs=[pl.BlockSpec((depth // steps, width), lambda i: (i, 0)), SMEM],
-        scratch_shapes=[pltpu.VMEM((rows, width), jnp.bfloat16)],
+        in_specs=[VMEM] * 3,
+        out_specs=[ANY, VMEM],
+        scratch_shapes=[
+            pltpu.VMEM((rows, width), jnp.bfloat16),
+            pltpu.VMEM((steps, depth // steps, width), jnp.float32),
+            pltpu.SemaphoreType.DMA((steps,)),
+        ],
         compiler_params=pltpu.CompilerParams(vmem_limit_bytes=16 << 20),
-        cost_estimate=pl.CostEstimate(flops=2 * rows * depth * width, bytes_accessed=4 * depth * width, transcendentals=0),
+        cost_estimate=pl.CostEstimate(
+            flops=2 * rows * depth * width, bytes_accessed=4 * depth * width, transcendentals=0
+        ),
         name="gradient",
-    )(me, own, arrived, features_t)
+    )(own, arrived, features_t)
 
 
 def small_plan(features, matrix, ids, filled, mask, scale, shift):
@@ -315,15 +337,18 @@
     part = rows // 4
 
     mine = part_unit(ids, filled, features, matrix)
+    mask = jnp.broadcast_to(after(mask, mine)[:, None], (8, 128))
     far = trade(mine, 6, 0)
     near = trade(mine, 1, 0)
     side = trade(mine, 2, 0)
-    unit, unit_bf, length, column = whole_unit(ids, after(features, mine), matrix)
-    others = [swap(after(mask, unit_bf), "group", k) for k in (1, 2, 3)]
+    unit, unit_bf, length, column, numbers = whole_unit(
+        ids, filled, scale, shift, after(features, mine), matrix
+    )
+    others = [swap(mask, "group", k) for k in (1, 2, 3)]
     far_s = trade(after(far, unit_bf, *others), 2, 0)
     far_x = trade(after(far, unit_bf, *others), 1, 0)
     side_x = trade(after(side, unit_bf, near), 1, 0)
-    common = ([scale, shift, filled, mask, *others], column, unit_bf)
+    common = (numbers, [mask, *others], column, unit_bf)
     early = pair_terms(
         *common, [near, side, far], ((1, 0, part, 0), (2, 0, part, 1), (6, 0, part, 2))
     )
@@ -339,8 +364,7 @@
         final=[unit, length],
     )
     own, send = combine(keep, swap(send, "group", 1))
-    me = lax.axis_index("group")
-    return gradient(me.reshape(1), own, swap(send, "group", 2), features.T)
+    return gradient(own, swap(send, "group", 2), features.T)
 
 
 def scatter_sum(block):

time: 63.1 us -> 58.4 us (0.926)
  Pallas kernels: 23.9 us -> 17.3 us
  starting transfers between devices: 16.9 us -> 18 us
  waiting for transfers between devices: 15.7 us -> 16.5 us
    pallas_call x3, Pallas kernels: 12.3 us -> 6.86 us  [pair_terms(): pl.pallas_call(functools.partial(pair_kernel, cuts, old is None, final is...]
    ppermute x7, waiting for transfers between devices: 3.15 us -> 6.34 us  [trade(): return lax.ppermute(block, AXES, route)]
    ppermute x5, waiting for transfers between devices: 12.5 us -> 10.1 us  [swap(): return lax.ppermute(block, axis, [(i, i ^ mask) for i in range(count)])]
    ppermute x7, starting transfers between devices: 12.8 us -> 14.4 us  [trade(): return lax.ppermute(block, AXES, route)]
    pallas_call x1, Pallas kernels: 4.35 us -> 3.71 us  [part_unit(): pl.pallas_call(part_unit_kernel, out_shape=jax.ShapeDtypeStruct((part + F...]
  transfers between devices with their start and end apart: 12 -> 12, of which waited for: 7 -> 5; matrix products, arithmetic and copies ran while one was open for 1% -> 1% of each run, Pallas kernels for 18% -> 13%
where the time goes in v5:
time: 58.4 us; the launch traced here: 58.2 us
  starting transfers between devices  18 us (31%)
  Pallas kernels  17.3 us (30%)
  waiting for transfers between devices  16.5 us (28%)
  between operations  3.35 us (6%)
  local copies, waits for them, and re-layouts  3.07 us (5%)
    ppermute x7, starting transfers between devices, trade(): return lax.ppermute(block, AXES, route)  14.4 us
    ppermute x5, waiting for transfers between devices, swap(): return lax.ppermute(block, axis, [(i, i ^ mask) for i in range(count)])  10.1 us
    pallas_call x3, Pallas kernels, pair_terms(): pl.pallas_call(functools.partial(pair_kernel, cuts, old is None, final is...  6.86 us
    ppermute x7, waiting for transfers between devices, trade(): return lax.ppermute(block, AXES, route)  6.34 us
    pallas_call x1, Pallas kernels, part_unit(): pl.pallas_call(part_unit_kernel, out_shape=jax.ShapeDtypeStruct((part + F...  3.71 us
    pallas_call x1, Pallas kernels, whole_unit(): pl.pallas_call(whole_unit_kernel, out_shape=[jax.ShapeDtypeStruct((rows,...  3.58 us
    ppermute x5, starting transfers between devices, swap(): return lax.ppermute(block, axis, [(i, i ^ mask) for i in range(count)])  3.55 us
    unnamed x7, local copies, waits for them, and re-layouts  3.07 us
  transfers between devices with their start and end apart: 12, of which 5 were waited for; matrix products, arithmetic and copies ran while one was open for 1% of the time, Pallas kernels for 13%

profile of v5, /device:TPU:0, one launch (start us, length us, event | category | flops | bytes accessed | tf_op | source)
XLA Modules:
  0.0 58.2 jit_solution(451766590676171804)
XLA Ops:
  1.3 0.0 copy-start.1
  1.3 0.0 copy-start.2
  1.3 3.7 %part_unit.1 = bf16[104,1536]{1,0:T(8,128)(2,1)} custom-call(s32[384]{0:T(512)} %ids.3, s32[1]{0:T(128)S(6)} %copy.10.filled, bf16[384,1536]{1,0:T(8,128)(2,1)} %features.2, bf16[1536,1536]{1,0:T(8,128)(2,1)} %matrix.3), custom_call_target="tpu_custom_call" | custom-call | flops 905969664 | bytes 4718592 | tf_op jit(solution)/shard_map/part_unit/pallas_call | solution.py:96
  5.0 5.1 %collective-permute-start.6 = (bf16[104,1536]{1,0:T(8,128)(2,1)}, bf16[104,1536]{1,0:T(8,128)(2,1)S(1)}, u32[]{:S(2)}, u32[]{:S(2)}) collective-permute-start(bf16[104,1536]{1,0:T(8,128)(2,1)} %part_unit.1), channel_id=1, source_target_pairs={{0,24},{1,25},{2,26},{3,27},{4,28},{5,29},{6,30},{7,31},{8,16},{9,... | collective-permute-start | bytes 958472 | tf_op jit(solution)/shard_map/ppermute | solution.py:30
  10.8 0.1 collective-permute-start
  10.9 1.6 %collective-permute-start.1 = (s32[8,128]{1,0:T(8,128)S(1)}, s32[8,128]{1,0:T(8,128)S(1)}, u32[]{:S(2)}, u32[]{:S(2)}) collective-permute-start(s32[8,128]{1,0:T(8,128)S(1)} %broadcast_in_dim.9.refs_1_), channel_id=1, source_target_pairs={{0,2},{1,3},{2,0},{3,1},{4,6},{5,7},{6,4},{7,5},{8,10},{9,11},{10,... | collective-permute-start | bytes 12296 | tf_op jit(solution)/shard_map/ppermute | solution.py:20
  12.5 0.3 collective-permute-start.2
  12.7 0.0 collective-permute-start.3
  14.0 0.0 collective-permute-done.refs_2_
  14.0 1.6 %collective-permute-start.4 = (bf16[104,1536]{1,0:T(8,128)(2,1)}, bf16[104,1536]{1,0:T(8,128)(2,1)S(1)}, u32[]{:S(2)}, u32[]{:S(2)}) collective-permute-start(bf16[104,1536]{1,0:T(8,128)(2,1)} %part_unit.1), channel_id=1, source_target_pairs={{0,4},{1,5},{2,6},{3,7},{4,0},{5,1},{6,2},{7,3},{8,12},{9,13},{10,... | collective-permute-start | bytes 958472 | tf_op jit(solution)/shard_map/ppermute | solution.py:30
  15.6 0.0 copy-done.1
  15.6 0.0 copy-done.2
  15.6 0.0 copy-start
  15.6 2.3 %copy-done = bf16[1536,1536]{1,0:T(8,128)(2,1)S(1)} copy-done((bf16[1536,1536]{1,0:T(8,128)(2,1)S(1)}, bf16[1536,1536]{1,0:T(8,128)(2,1)}, u32[]{:S(2)}) %copy-start) | copy-done | bytes 4718616
  17.9 3.6 %whole_unit.1 = (f32[384,1536]{1,0:T(8,128)S(1)}, bf16[384,1536]{1,0:T(8,128)(2,1)S(1)}, f32[384,128]{1,0:T(8,128)S(1)}, f32[384,128]{1,0:T(8,128)S(1)}, f32[8,128]{1,0:T(8,128)S(1)}) custom-call(s32[384]{0:T(512)S(1)} %copy-done.2, s32[1]{0:T(128)S(6)} %copy.10.filled, f32[1]{0:T(128)S(6)} %copy.12.scale, f32[1]{0:T(128)S(6)} %copy.13.shift, ...), custom_call_target="tpu_custom_call" | custom-call | flops 1811939328 | bytes 9437184 | tf_op jit(solution)/shard_map/whole_unit/pallas_call | solution.py:135
  21.5 0.0 collective-permute-done.1.refs_3_
  21.5 0.0 collective-permute-done.2.refs_4_
  21.6 0.0 collective-permute-done.6.refs_9_
  21.6 0.6 %collective-permute-start.7 = (bf16[104,1536]{1,0:T(8,128)(2,1)S(1)}, bf16[104,1536]{1,0:T(8,128)(2,1)S(1)}, u32[]{:S(2)}, u32[]{:S(2)}) collective-permute-start(bf16[104,1536]{1,0:T(8,128)(2,1)S(1)} %collective-permute-done.6.refs_9_), channel_id=1, source_target_pairs={{0,4},{1,5},{2,6},{3,7},{4,0},{5,1},{6,2},{7,3},{8,12},{9,13},{10,... | collective-permute-start | bytes 958472 | tf_op jit(solution)/shard_map/ppermute | solution.py:30
  22.1 3.8 %collective-permute-start.9 = (bf16[104,1536]{1,0:T(8,128)(2,1)S(1)}, bf16[104,1536]{1,0:T(8,128)(2,1)S(1)}, u32[]{:S(2)}, u32[]{:S(2)}) collective-permute-start(bf16[104,1536]{1,0:T(8,128)(2,1)S(1)} %collective-permute-done.6.refs_9_), channel_id=1, source_target_pairs={{0,8},{1,9},{2,10},{3,11},{4,12},{5,13},{6,14},{7,15},{8,0},{9,1},... | collective-permute-start | bytes 958472 | tf_op jit(solution)/shard_map/ppermute | solution.py:30
  25.9 0.0 collective-permute-done.3.refs_8_
  25.9 0.0 collective-permute-done.4.refs_7_
  25.9 0.5 collective-permute-start.5
  26.5 2.3 %pair_terms.3 = (f32[384,1536]{1,0:T(8,128)S(1)}, f32[8,128]{1,0:T(8,128)S(1)}) custom-call(f32[8,128]{1,0:T(8,128)S(1)} %get-tuple-element.21.refs_0_, s32[8,128]{1,0:T(8,128)S(1)} %broadcast_in_dim.9.refs_1_, s32[8,128]{1,0:T(8,128)S(1)} %collective-permute-done.refs_2_, s32[8,128]{1,0:T(8,128)S(1)} %collective-permute-done.1.refs_3_, ...), custom_call_target="tpu_custom_call" | custom-call | flops 679477248 | bytes 4718592 | tf_op jit(solution)/shard_map/pair_terms/pallas_call | solution.py:249
  28.7 3.3 %collective-permute-done.7.refs_8_ = bf16[104,1536]{1,0:T(8,128)(2,1)S(1)} collective-permute-done((bf16[104,1536]{1,0:T(8,128)(2,1)S(1)}, bf16[104,1536]{1,0:T(8,128)(2,1)S(1)}, u32[]{:S(2)}, u32[]{:S(2)}) %collective-permute-start.7) | collective-permute-done | bytes 319520 | tf_op jit(solution)/shard_map/ppermute | solution.py:30
  32.0 2.9 %collective-permute-start.8 = (bf16[104,1536]{1,0:T(8,128)(2,1)S(1)}, bf16[104,1536]{1,0:T(8,128)(2,1)S(1)}, u32[]{:S(2)}, u32[]{:S(2)}) collective-permute-start(bf16[104,1536]{1,0:T(8,128)(2,1)S(1)} %collective-permute-done.7.refs_8_), channel_id=1, source_target_pairs={{0,8},{1,9},{2,10},{3,11},{4,12},{5,13},{6,14},{7,15},{8,0},{9,1},... | collective-permute-start | bytes 958472 | tf_op jit(solution)/shard_map/ppermute | solution.py:30
  34.9 0.0 collective-permute-done.9.refs_7_
  34.9 1.9 %pair_terms.4 = (f32[384,1536]{1,0:T(8,128)S(1)}, f32[8,128]{1,0:T(8,128)S(1)}) custom-call(f32[8,128]{1,0:T(8,128)S(1)} %get-tuple-element.21.refs_0_, s32[8,128]{1,0:T(8,128)S(1)} %broadcast_in_dim.9.refs_1_, s32[8,128]{1,0:T(8,128)S(1)} %collective-permute-done.refs_2_, s32[8,128]{1,0:T(8,128)S(1)} %collective-permute-done.1.refs_3_, ...), custom_call_target="tpu_custom_call" | custom-call | flops 452984832 | bytes 4718592 | tf_op jit(solution)/shard_map/pair_terms/pallas_call | solution.py:249
  36.8 1.2 %collective-permute-done.5.refs_7_ = bf16[104,1536]{1,0:T(8,128)(2,1)S(1)} collective-permute-done((bf16[104,1536]{1,0:T(8,128)(2,1)S(1)}, bf16[104,1536]{1,0:T(8,128)(2,1)S(1)}, u32[]{:S(2)}, u32[]{:S(2)}) %collective-permute-start.5) | collective-permute-done | bytes 319520 | tf_op jit(solution)/shard_map/ppermute | solution.py:30
  38.0 1.9 %collective-permute-done.8.refs_8_ = bf16[104,1536]{1,0:T(8,128)(2,1)S(1)} collective-permute-done((bf16[104,1536]{1,0:T(8,128)(2,1)S(1)}, bf16[104,1536]{1,0:T(8,128)(2,1)S(1)}, u32[]{:S(2)}, u32[]{:S(2)}) %collective-permute-start.8) | collective-permute-done | bytes 319520 | tf_op jit(solution)/shard_map/ppermute | solution.py:30
  39.9 2.7 %pair_terms.5 = (f32[392,768]{1,0:T(8,128)S(1)}, f32[392,768]{1,0:T(8,128)S(1)}) custom-call(f32[8,128]{1,0:T(8,128)S(1)} %get-tuple-element.21.refs_0_, s32[8,128]{1,0:T(8,128)S(1)} %broadcast_in_dim.9.refs_1_, s32[8,128]{1,0:T(8,128)S(1)} %collective-permute-done.refs_2_, s32[8,128]{1,0:T(8,128)S(1)} %collective-permute-done.1.refs_3_, ...), custom_call_target="tpu_custom_call" | custom-call | flops 452984832 | bytes 4718592 | tf_op jit(solution)/shard_map/pair_terms/pallas_call | solution.py:249
  42.6 0.1 collective-permute-start.10
  42.6 2.9 %collective-permute-done.10.arrived = f32[392,768]{1,0:T(8,128)S(1)} collective-permute-done((f32[392,768]{1,0:T(8,128)S(1)}, f32[392,768]{1,0:T(8,128)S(1)}, u32[]{:S(2)}, u32[]{:S(2)}) %collective-permute-start.10) | collective-permute-done | bytes 1204256 | tf_op jit(solution)/shard_map/ppermute | solution.py:20
  45.5 0.9 %combine.1 = (f32[392,384]{1,0:T(8,128)S(1)}, bf16[400,384]{1,0:T(8,128)(2,1)}) custom-call(f32[392,768]{1,0:T(8,128)S(1)} %get-tuple-element.34.keep, f32[392,768]{1,0:T(8,128)S(1)} %collective-permute-done.10.arrived), custom_call_target="tpu_custom_call" | custom-call | flops 294912 | bytes 2359296 | tf_op jit(solution)/shard_map/combine/pallas_call | solution.py:277
  46.4 1.5 %collective-permute-start.11 = (bf16[400,384]{1,0:T(8,128)(2,1)}, bf16[400,384]{1,0:T(8,128)(2,1)S(1)}, u32[]{:S(2)}, u32[]{:S(2)}) collective-permute-start(bf16[400,384]{1,0:T(8,128)(2,1)} %get-tuple-element.37), channel_id=1, source_target_pairs={{0,2},{1,3},{2,0},{3,1},{4,6},{5,7},{6,4},{7,5},{8,10},{9,11},{10,... | collective-permute-start | bytes 921608 | tf_op jit(solution)/shard_map/ppermute | solution.py:20
  47.9 0.7 %copy.9 = bf16[384,1536]{0,1:T(8,128)(2,1)S(1)} copy(bf16[384,1536]{1,0:T(8,128)(2,1)S(1)} %copy-done.1) | data formatting | bytes 2359296 | tf_op args[0]
  48.7 7.2 %collective-permute-done.11.arrived = bf16[400,384]{1,0:T(8,128)(2,1)S(1)} collective-permute-done((bf16[400,384]{1,0:T(8,128)(2,1)}, bf16[400,384]{1,0:T(8,128)(2,1)S(1)}, u32[]{:S(2)}, u32[]{:S(2)}) %collective-permute-start.11) | collective-permute-done | bytes 307232 | tf_op jit(solution)/shard_map/ppermute | solution.py:20
  55.9 2.3 %gradient.1 = (f32[1536,384]{1,0:T(8,128)}, f32[1,1]{1,0:T(1,128)}) custom-call(f32[392,384]{1,0:T(8,128)S(1)} %get-tuple-element.36.own, bf16[400,384]{1,0:T(8,128)(2,1)S(1)} %collective-permute-done.11.arrived, bf16[1536,384]{1,0:T(8,128)(2,1)S(1)} %bitcast.3), custom_call_target="tpu_custom_call" | custom-call | flops 452984832 | bytes 2359296 | tf_op jit(solution)/shard_map/gradient/pallas_call | solution.py:314
  (1 shorter events, 0.0 us)
Async XLA Ops:
  1.3 14.3 %copy-start.1 = (bf16[384,1536]{1,0:T(8,128)(2,1)S(1)}, bf16[384,1536]{1,0:T(8,128)(2,1)}, u32[]{:S(2)}) copy-start(bf16[384,1536]{1,0:T(8,128)(2,1)} %features.2) | copy-start | bytes 3538948
  1.3 14.3 %copy-start.2 = (s32[384]{0:T(512)S(1)}, s32[384]{0:T(512)}, u32[]{:S(2)}) copy-start(s32[384]{0:T(512)} %ids.3) | copy-start | bytes 4612
  5.0 16.5 %collective-permute-start.6 = (bf16[104,1536]{1,0:T(8,128)(2,1)}, bf16[104,1536]{1,0:T(8,128)(2,1)S(1)}, u32[]{:S(2)}, u32[]{:S(2)}) collective-permute-start(bf16[104,1536]{1,0:T(8,128)(2,1)} %part_unit.1), channel_id=1, source_target_pairs={{0,24},{1,25},{2,26},{3,27},{4,28},{5,29},{6,30},{7,31},{8,16},{9,... | collective-permute-start | bytes 958472 | tf_op jit(solution)/shard_map/ppermute | solution.py:30
  10.8 3.2 %collective-permute-start = (s32[8,128]{1,0:T(8,128)S(1)}, s32[8,128]{1,0:T(8,128)S(1)}, u32[]{:S(2)}, u32[]{:S(2)}) collective-permute-start(s32[8,128]{1,0:T(8,128)S(1)} %broadcast_in_dim.9.refs_1_), channel_id=1, source_target_pairs={{0,1},{1,0},{2,3},{3,2},{4,5},{5,4},{6,7},{7,6},{8,9},{9,8},{10,11... | collective-permute-start | bytes 12296 | tf_op jit(solution)/shard_map/ppermute | solution.py:20
  10.9 10.7 %collective-permute-start.1 = (s32[8,128]{1,0:T(8,128)S(1)}, s32[8,128]{1,0:T(8,128)S(1)}, u32[]{:S(2)}, u32[]{:S(2)}) collective-permute-start(s32[8,128]{1,0:T(8,128)S(1)} %broadcast_in_dim.9.refs_1_), channel_id=1, source_target_pairs={{0,2},{1,3},{2,0},{3,1},{4,6},{5,7},{6,4},{7,5},{8,10},{9,11},{10,... | collective-permute-start | bytes 12296 | tf_op jit(solution)/shard_map/ppermute | solution.py:20
  12.5 9.1 %collective-permute-start.2 = (s32[8,128]{1,0:T(8,128)S(1)}, s32[8,128]{1,0:T(8,128)S(1)}, u32[]{:S(2)}, u32[]{:S(2)}) collective-permute-start(s32[8,128]{1,0:T(8,128)S(1)} %broadcast_in_dim.9.refs_1_), channel_id=1, source_target_pairs={{0,3},{1,2},{2,1},{3,0},{4,7},{5,6},{6,5},{7,4},{8,11},{9,10},{10,... | collective-permute-start | bytes 12296 | tf_op jit(solution)/shard_map/ppermute | solution.py:20
  12.7 13.2 %collective-permute-start.3 = (bf16[104,1536]{1,0:T(8,128)(2,1)}, bf16[104,1536]{1,0:T(8,128)(2,1)S(1)}, u32[]{:S(2)}, u32[]{:S(2)}) collective-permute-start(bf16[104,1536]{1,0:T(8,128)(2,1)} %part_unit.1), channel_id=1, source_target_pairs={{0,8},{1,9},{2,10},{3,11},{4,12},{5,13},{6,14},{7,15},{8,0},{9,1},... | collective-permute-start | bytes 958472 | tf_op jit(solution)/shard_map/ppermute | solution.py:30
  14.0 11.9 %collective-permute-start.4 = (bf16[104,1536]{1,0:T(8,128)(2,1)}, bf16[104,1536]{1,0:T(8,128)(2,1)S(1)}, u32[]{:S(2)}, u32[]{:S(2)}) collective-permute-start(bf16[104,1536]{1,0:T(8,128)(2,1)} %part_unit.1), channel_id=1, source_target_pairs={{0,4},{1,5},{2,6},{3,7},{4,0},{5,1},{6,2},{7,3},{8,12},{9,13},{10,... | collective-permute-start | bytes 958472 | tf_op jit(solution)/shard_map/ppermute | solution.py:30
  15.6 2.3 %copy-start = (bf16[1536,1536]{1,0:T(8,128)(2,1)S(1)}, bf16[1536,1536]{1,0:T(8,128)(2,1)}, u32[]{:S(2)}) copy-start(bf16[1536,1536]{1,0:T(8,128)(2,1)} %matrix.3) | copy-start | bytes 14155780
  21.6 10.5 %collective-permute-start.7 = (bf16[104,1536]{1,0:T(8,128)(2,1)S(1)}, bf16[104,1536]{1,0:T(8,128)(2,1)S(1)}, u32[]{:S(2)}, u32[]{:S(2)}) collective-permute-start(bf16[104,1536]{1,0:T(8,128)(2,1)S(1)} %collective-permute-done.6.refs_9_), channel_id=1, source_target_pairs={{0,4},{1,5},{2,6},{3,7},{4,0},{5,1},{6,2},{7,3},{8,12},{9,13},{10,... | collective-permute-start | bytes 958472 | tf_op jit(solution)/shard_map/ppermute | solution.py:30
  22.1 12.8 %collective-permute-start.9 = (bf16[104,1536]{1,0:T(8,128)(2,1)S(1)}, bf16[104,1536]{1,0:T(8,128)(2,1)S(1)}, u32[]{:S(2)}, u32[]{:S(2)}) collective-permute-start(bf16[104,1536]{1,0:T(8,128)(2,1)S(1)} %collective-permute-done.6.refs_9_), channel_id=1, source_target_pairs={{0,8},{1,9},{2,10},{3,11},{4,12},{5,13},{6,14},{7,15},{8,0},{9,1},... | collective-permute-start | bytes 958472 | tf_op jit(solution)/shard_map/ppermute | solution.py:30
  25.9 12.0 %collective-permute-start.5 = (bf16[104,1536]{1,0:T(8,128)(2,1)S(1)}, bf16[104,1536]{1,0:T(8,128)(2,1)S(1)}, u32[]{:S(2)}, u32[]{:S(2)}) collective-permute-start(bf16[104,1536]{1,0:T(8,128)(2,1)S(1)} %collective-permute-done.3.refs_8_), channel_id=1, source_target_pairs={{0,4},{1,5},{2,6},{3,7},{4,0},{5,1},{6,2},{7,3},{8,12},{9,13},{10,... | collective-permute-start | bytes 958472 | tf_op jit(solution)/shard_map/ppermute | solution.py:30
  32.0 7.8 %collective-permute-start.8 = (bf16[104,1536]{1,0:T(8,128)(2,1)S(1)}, bf16[104,1536]{1,0:T(8,128)(2,1)S(1)}, u32[]{:S(2)}, u32[]{:S(2)}) collective-permute-start(bf16[104,1536]{1,0:T(8,128)(2,1)S(1)} %collective-permute-done.7.refs_8_), channel_id=1, source_target_pairs={{0,8},{1,9},{2,10},{3,11},{4,12},{5,13},{6,14},{7,15},{8,0},{9,1},... | collective-permute-start | bytes 958472 | tf_op jit(solution)/shard_map/ppermute | solution.py:30
  42.6 2.9 %collective-permute-start.10 = (f32[392,768]{1,0:T(8,128)S(1)}, f32[392,768]{1,0:T(8,128)S(1)}, u32[]{:S(2)}, u32[]{:S(2)}) collective-permute-start(f32[392,768]{1,0:T(8,128)S(1)} %get-tuple-element.35), channel_id=1, source_target_pairs={{0,1},{1,0},{2,3},{3,2},{4,5},{5,4},{6,7},{7,6},{8,9},{9,8},{10,11... | collective-permute-start | bytes 3612680 | tf_op jit(solution)/shard_map/ppermute | solution.py:20
  46.4 9.5 %collective-permute-start.11 = (bf16[400,384]{1,0:T(8,128)(2,1)}, bf16[400,384]{1,0:T(8,128)(2,1)S(1)}, u32[]{:S(2)}, u32[]{:S(2)}) collective-permute-start(bf16[400,384]{1,0:T(8,128)(2,1)} %get-tuple-element.37), channel_id=1, source_target_pairs={{0,2},{1,3},{2,0},{3,1},{4,6},{5,7},{6,4},{7,5},{8,10},{9,11},{10,... | collective-permute-start | bytes 921608 | tf_op jit(solution)/shard_map/ppermute | solution.py:20

commit v6 on v5

--- a/solution.py
+++ b/solution.py
@@ -8,7 +8,7 @@
 from jax.sharding import PartitionSpec as P
 
 AXES = ("peer", "group")
-STEPS = 6
+STEPS = 3
 FACTS = 8
 SMALL = pl.CostEstimate(flops=1, bytes_accessed=1, transcendentals=0)
 ANY = pl.BlockSpec(memory_space=pl.ANY)
@@ -156,7 +156,7 @@
     )(ids, filled, scale, shift, features, matrix)
 
 
-def pair_kernel(cuts, first, final, *refs):
+def pair_kernel(cuts, first, final, window, *refs):
     refs = list(refs)
     numbers = refs[0]
     masks = [ref[0:1] for ref in refs[1:5]]
@@ -171,20 +171,21 @@
     else:
         total, losses_out, stacked = refs
     me = lax.axis_index("group")
-    rows = unit_bf.shape[0]
-    part = rows // 4
+    here = slice(*window)
+    rows = window[1] - window[0]
+    part = unit_bf.shape[0] // 4
     offset = 0
     values = [block[...] for block in blocks]
     for value, (_, _, count, _) in zip(values, cuts):
         stacked[offset : offset + count] = value[:count]
         offset += count
     scores = lax.dot_general(
-        unit_bf[...], stacked[...], (((1,), (1,)), ((), ())), preferred_element_type=jnp.float32
-    )
-    row = lax.broadcasted_iota(jnp.int32, (rows, 1), 0)
+        unit_bf[here], stacked[...], (((1,), (1,)), ((), ())), preferred_element_type=jnp.float32
+    )
+    row = window[0] + lax.broadcasted_iota(jnp.int32, (rows, 1), 0)
     used_here = row < numbers[2:3, 0:1].astype(jnp.int32)
     lane = lax.broadcasted_iota(jnp.int32, (1, 128), 1)
-    losses = jnp.zeros((1, 128), jnp.float32) if first else old_losses[0:1]
+    losses = jnp.zeros((1, 128), jnp.float32) if first or window[0] else old_losses[0:1]
     slopes = []
     offset = 0
     for mask, begin, count, owner in cuts:
@@ -197,7 +198,7 @@
         place = me * part + begin + lax.broadcasted_iota(jnp.int32, (1, count), 1)
         there = (place < filled.astype(jnp.int32)) & (turn[:, :count] >= 0)
         used = used_here & there
-        signs = jnp.where(ids_here[:, :1] == ids, -1.0, 1.0)
+        signs = jnp.where(ids_here[here, :1] == ids, -1.0, 1.0)
         scale, shift = numbers[0:1, :count], numbers[1:2, :count]
         logits = signs * (scale * scores[:, offset : offset + count] + shift)
         small = jnp.exp(-jnp.abs(logits))
@@ -213,12 +214,12 @@
     for k in range(4):
         at = slice(k * step, (k + 1) * step)
         part = jnp.dot(slopes, stacked[:, at], preferred_element_type=jnp.float32)
-        total[:, at] = part if first else old_dunit[:, at] + part
+        total[:, at] = part if first else old_dunit[here, at] + part
     if not final:
         losses_out[...] = jnp.broadcast_to(losses, losses_out.shape)
         return
-    along = jnp.sum(unit[...] * total[...], axis=1, keepdims=True)
-    total[...] = (total[...] - unit[...] * along) / length[:, :1]
+    along = jnp.sum(unit[here] * total[...], axis=1, keepdims=True)
+    total[...] = (total[...] - unit[here] * along) / length[here, :1]
     for k, other in enumerate((0, 2)):
         at = pl.ds(pl.multiple_of(jnp.bitwise_xor(me, other) * step, 128), step)
         keep[:rows, k * step : (k + 1) * step] = total[:, at]
@@ -230,8 +231,9 @@
     send[rows : rows + 1, 0:128] = losses
 
 
-def pair_terms(numbers, masks, ids_here, unit_bf, blocks, cuts, old=None, final=None):
-    rows, width = unit_bf.shape
+def pair_terms(numbers, masks, ids_here, unit_bf, blocks, cuts, old=None, final=None, window=None):
+    window = window or (0, unit_bf.shape[0])
+    rows, width = window[1] - window[0], unit_bf.shape[1]
     total = sum(count for _, _, count, _ in cuts)
     args = [numbers, *masks, ids_here, unit_bf, *blocks]
     scratch = [pltpu.VMEM((total, width), jnp.bfloat16)]
@@ -247,7 +249,7 @@
             jax.ShapeDtypeStruct((8, 128), jnp.float32),
         ]
     return pl.pallas_call(
-        functools.partial(pair_kernel, cuts, old is None, final is not None),
+        functools.partial(pair_kernel, cuts, old is None, final is not None, window),
         out_shape=shapes,
         in_specs=[VMEM] * len(args),
         out_specs=[VMEM] * len(shapes),
@@ -288,18 +290,21 @@
     )(keep, arrived)
 
 
-def gradient_kernel(own, arrived, features, grad, loss, draw, parts, sems):
+def gradient_kernel(own_a, own_b, arrived_a, arrived_b, features, grad, loss, draw, parts, sems):
     rows = features.shape[1]
+    half = rows // 2
     steps, height = parts.shape[:2]
-    draw[...] = (own[:rows] + arrived[:rows].astype(jnp.float32)).astype(jnp.bfloat16)
+    draw[:half] = (own_a[:half] + arrived_a[:half].astype(jnp.float32)).astype(jnp.bfloat16)
+    draw[half:] = (own_b[:half] + arrived_b[:half].astype(jnp.float32)).astype(jnp.bfloat16)
     copies = []
     for k in range(steps):
         at = pl.ds(k * height, height)
         parts[k] = jnp.dot(features[at], draw[...], preferred_element_type=jnp.float32)
         copies.append(pltpu.make_async_copy(parts.at[k], grad.at[at], sems.at[k]))
         copies[k].start()
-    low = jnp.sum(arrived[rows:, 0:128].astype(jnp.float32), axis=0, keepdims=True)
-    total = own[rows : rows + 1, 0:128] + low
+    total = own_a[half : half + 1, 0:128] + own_b[half : half + 1, 0:128]
+    for arrived in (arrived_a, arrived_b):
+        total += jnp.sum(arrived[half:, 0:128].astype(jnp.float32), axis=0, keepdims=True)
     lane = lax.broadcasted_iota(jnp.int32, (1, 128), 1)
     mine = jnp.where(lane == lax.axis_index("group"), total, 0.0)
     loss[...] = jnp.sum(mine, axis=1, keepdims=True) / (rows * rows)
@@ -309,7 +314,7 @@
 
 def gradient(own, arrived, features_t):
     depth, rows = features_t.shape
-    width = own.shape[1]
+    width = own[0].shape[1]
     steps = 6
     return pl.pallas_call(
         gradient_kernel,
@@ -317,7 +322,7 @@
             jax.ShapeDtypeStruct((depth, width), jnp.float32),
             jax.ShapeDtypeStruct((1, 1), jnp.float32),
         ],
-        in_specs=[VMEM] * 3,
+        in_specs=[VMEM] * 5,
         out_specs=[ANY, VMEM],
         scratch_shapes=[
             pltpu.VMEM((rows, width), jnp.bfloat16),
@@ -329,7 +334,7 @@
             flops=2 * rows * depth * width, bytes_accessed=4 * depth * width, transcendentals=0
         ),
         name="gradient",
-    )(own, arrived, features_t)
+    )(*own, *arrived, features_t)
 
 
 def small_plan(features, matrix, ids, filled, mask, scale, shift):
@@ -356,15 +361,23 @@
     middle = pair_terms(
         *common, [far_s, far_x], ((4, 0, part, 0), (7, 0, part, 1)), old=early
     )
-    keep, send = pair_terms(
-        *common,
-        [side_x, last],
-        ((3, 0, part, 0), (5, 0, part, 1)),
-        old=middle,
-        final=[unit, length],
-    )
-    own, send = combine(keep, swap(send, "group", 1))
-    return gradient(own, swap(send, "group", 2), features.T)
+    own, arrived = [], []
+    sent = []
+    for window in ((0, rows // 2), (rows // 2, rows)):
+        keep, send = pair_terms(
+            *common,
+            [side_x, last],
+            ((3, 0, part, 0), (5, 0, part, 1)),
+            old=middle,
+            final=[unit, length],
+            window=window,
+        )
+        sent.append((keep, swap(send, "group", 1)))
+    for keep, received in sent:
+        kept, send = combine(keep, received)
+        own.append(kept)
+        arrived.append(swap(send, "group", 2))
+    return gradient(own, arrived, features.T)
 
 
 def scatter_sum(block):

time: 58.4 us -> 55.7 us (0.954)
  waiting for transfers between devices: 16.5 us -> 10.9 us
  starting transfers between devices: 18 us -> 21 us
    ppermute x5 -> x7, waiting for transfers between devices: 10.1 us -> 4.97 us  [swap(): return lax.ppermute(block, axis, [(i, i ^ mask) for i in range(count)])]
    ppermute x5 -> x7, starting transfers between devices: 3.55 us -> 5.74 us  [swap(): return lax.ppermute(block, axis, [(i, i ^ mask) for i in range(count)])]
    ppermute x7, starting transfers between devices: 14.4 us -> 15.2 us  [trade(): return lax.ppermute(block, AXES, route)]
    pallas_call x3 -> x4, Pallas kernels: 6.86 us -> 7.07 us  [pair_terms(): pl.pallas_call(functools.partial(pair_kernel, cuts, old is None, final is...]
  transfers between devices with their start and end apart: 12 -> 14, of which waited for: 5 -> 5; matrix products, arithmetic and copies ran while one was open for 1% -> 1% of each run, Pallas kernels for 13% -> 17%
where the time goes in v6:
time: 55.7 us; the launch traced here: 55.5 us
  starting transfers between devices  21 us (38%)
  Pallas kernels  17.2 us (31%)
  waiting for transfers between devices  10.9 us (20%)
  between operations  3.36 us (6%)
  local copies, waits for them, and re-layouts  3.1 us (6%)
    ppermute x7, starting transfers between devices, trade(): return lax.ppermute(block, AXES, route)  15.2 us
    pallas_call x4, Pallas kernels, pair_terms(): pl.pallas_call(functools.partial(pair_kernel, cuts, old is None, final is...  7.07 us
    ppermute x7, waiting for transfers between devices, trade(): return lax.ppermute(block, AXES, route)  5.95 us
    ppermute x7, starting transfers between devices, swap(): return lax.ppermute(block, axis, [(i, i ^ mask) for i in range(count)])  5.74 us
    ppermute x7, waiting for transfers between devices, swap(): return lax.ppermute(block, axis, [(i, i ^ mask) for i in range(count)])  4.97 us
    pallas_call x1, Pallas kernels, part_unit(): pl.pallas_call(part_unit_kernel, out_shape=jax.ShapeDtypeStruct((part + F...  3.84 us
    pallas_call x1, Pallas kernels, whole_unit(): pl.pallas_call(whole_unit_kernel, out_shape=[jax.ShapeDtypeStruct((rows,...  3.19 us
    unnamed x7, local copies, waits for them, and re-layouts  3.1 us
  transfers between devices with their start and end apart: 14, of which 5 were waited for; matrix products, arithmetic and copies ran while one was open for 1% of the time, Pallas kernels for 17%

profile of v6, /device:TPU:0, one launch (start us, length us, event | category | flops | bytes accessed | tf_op | source)
XLA Modules:
  0.0 55.5 jit_solution(15740112774329833042)
XLA Ops:
  1.3 0.0 copy-start.1
  1.3 0.0 copy-start.2
  1.3 3.8 %part_unit.1 = bf16[104,1536]{1,0:T(8,128)(2,1)} custom-call(s32[384]{0:T(512)} %ids.3, s32[1]{0:T(128)S(6)} %copy.10.filled, bf16[384,1536]{1,0:T(8,128)(2,1)} %features.2, bf16[1536,1536]{1,0:T(8,128)(2,1)} %matrix.3), custom_call_target="tpu_custom_call" | custom-call | flops 905969664 | bytes 4718592 | tf_op jit(solution)/shard_map/part_unit/pallas_call | solution.py:96
  5.1 5.1 %collective-permute-start.6 = (bf16[104,1536]{1,0:T(8,128)(2,1)}, bf16[104,1536]{1,0:T(8,128)(2,1)S(1)}, u32[]{:S(2)}, u32[]{:S(2)}) collective-permute-start(bf16[104,1536]{1,0:T(8,128)(2,1)} %part_unit.1), channel_id=1, source_target_pairs={{0,24},{1,25},{2,26},{3,27},{4,28},{5,29},{6,30},{7,31},{8,16},{9,... | collective-permute-start | bytes 958472 | tf_op jit(solution)/shard_map/ppermute | solution.py:30
  10.9 0.1 collective-permute-start
  11.0 1.6 %collective-permute-start.1 = (s32[8,128]{1,0:T(8,128)S(1)}, s32[8,128]{1,0:T(8,128)S(1)}, u32[]{:S(2)}, u32[]{:S(2)}) collective-permute-start(s32[8,128]{1,0:T(8,128)S(1)} %broadcast_in_dim.9.refs_1_), channel_id=1, source_target_pairs={{0,2},{1,3},{2,0},{3,1},{4,6},{5,7},{6,4},{7,5},{8,10},{9,11},{10,... | collective-permute-start | bytes 12296 | tf_op jit(solution)/shard_map/ppermute | solution.py:20
  12.6 0.3 collective-permute-start.2
  12.9 0.0 collective-permute-start.3
  14.2 0.0 collective-permute-done.refs_2_
  14.2 1.6 %collective-permute-start.4 = (bf16[104,1536]{1,0:T(8,128)(2,1)}, bf16[104,1536]{1,0:T(8,128)(2,1)S(1)}, u32[]{:S(2)}, u32[]{:S(2)}) collective-permute-start(bf16[104,1536]{1,0:T(8,128)(2,1)} %part_unit.1), channel_id=1, source_target_pairs={{0,4},{1,5},{2,6},{3,7},{4,0},{5,1},{6,2},{7,3},{8,12},{9,13},{10,... | collective-permute-start | bytes 958472 | tf_op jit(solution)/shard_map/ppermute | solution.py:30
  15.7 0.0 copy-done.1
  15.7 0.0 copy-done.2
  15.7 0.0 copy-start
  15.7 2.3 %copy-done = bf16[1536,1536]{1,0:T(8,128)(2,1)S(1)} copy-done((bf16[1536,1536]{1,0:T(8,128)(2,1)S(1)}, bf16[1536,1536]{1,0:T(8,128)(2,1)}, u32[]{:S(2)}) %copy-start) | copy-done | bytes 4718616
  18.1 3.2 %whole_unit.1 = (f32[384,1536]{1,0:T(8,128)S(1)}, bf16[384,1536]{1,0:T(8,128)(2,1)S(1)}, f32[384,128]{1,0:T(8,128)S(1)}, f32[384,128]{1,0:T(8,128)S(1)}, f32[8,128]{1,0:T(8,128)S(1)}) custom-call(s32[384]{0:T(512)S(1)} %copy-done.2, s32[1]{0:T(128)S(6)} %copy.10.filled, f32[1]{0:T(128)S(6)} %copy.12.scale, f32[1]{0:T(128)S(6)} %copy.13.shift, ...), custom_call_target="tpu_custom_call" | custom-call | flops 1811939328 | bytes 9437184 | tf_op jit(solution)/shard_map/whole_unit/pallas_call | solution.py:135
  21.3 0.0 collective-permute-done.1.refs_3_
  21.3 0.0 collective-permute-done.2.refs_4_
  21.3 0.0 collective-permute-done.6.refs_9_
  21.3 0.6 %collective-permute-start.7 = (bf16[104,1536]{1,0:T(8,128)(2,1)S(1)}, bf16[104,1536]{1,0:T(8,128)(2,1)S(1)}, u32[]{:S(2)}, u32[]{:S(2)}) collective-permute-start(bf16[104,1536]{1,0:T(8,128)(2,1)S(1)} %collective-permute-done.6.refs_9_), channel_id=1, source_target_pairs={{0,4},{1,5},{2,6},{3,7},{4,0},{5,1},{6,2},{7,3},{8,12},{9,13},{10,... | collective-permute-start | bytes 958472 | tf_op jit(solution)/shard_map/ppermute | solution.py:30
  21.9 4.2 %collective-permute-start.9 = (bf16[104,1536]{1,0:T(8,128)(2,1)S(1)}, bf16[104,1536]{1,0:T(8,128)(2,1)S(1)}, u32[]{:S(2)}, u32[]{:S(2)}) collective-permute-start(bf16[104,1536]{1,0:T(8,128)(2,1)S(1)} %collective-permute-done.6.refs_9_), channel_id=1, source_target_pairs={{0,8},{1,9},{2,10},{3,11},{4,12},{5,13},{6,14},{7,15},{8,0},{9,1},... | collective-permute-start | bytes 958472 | tf_op jit(solution)/shard_map/ppermute | solution.py:30
  26.1 0.0 collective-permute-done.3.refs_8_
  26.1 0.0 collective-permute-done.4.refs_7_
  26.1 0.5 collective-permute-start.5
  26.6 2.3 %pair_terms.4 = (f32[384,1536]{1,0:T(8,128)S(1)}, f32[8,128]{1,0:T(8,128)S(1)}) custom-call(f32[8,128]{1,0:T(8,128)S(1)} %get-tuple-element.25.refs_0_, s32[8,128]{1,0:T(8,128)S(1)} %broadcast_in_dim.9.refs_1_, s32[8,128]{1,0:T(8,128)S(1)} %collective-permute-done.refs_2_, s32[8,128]{1,0:T(8,128)S(1)} %collective-permute-done.1.refs_3_, ...), custom_call_target="tpu_custom_call" | custom-call | flops 679477248 | bytes 4718592 | tf_op jit(solution)/shard_map/pair_terms/pallas_call | solution.py:251
  28.9 2.9 %collective-permute-done.7.refs_8_ = bf16[104,1536]{1,0:T(8,128)(2,1)S(1)} collective-permute-done((bf16[104,1536]{1,0:T(8,128)(2,1)S(1)}, bf16[104,1536]{1,0:T(8,128)(2,1)S(1)}, u32[]{:S(2)}, u32[]{:S(2)}) %collective-permute-start.7) | collective-permute-done | bytes 319520 | tf_op jit(solution)/shard_map/ppermute | solution.py:30
  31.8 3.3 %collective-permute-start.8 = (bf16[104,1536]{1,0:T(8,128)(2,1)S(1)}, bf16[104,1536]{1,0:T(8,128)(2,1)S(1)}, u32[]{:S(2)}, u32[]{:S(2)}) collective-permute-start(bf16[104,1536]{1,0:T(8,128)(2,1)S(1)} %collective-permute-done.7.refs_8_), channel_id=1, source_target_pairs={{0,8},{1,9},{2,10},{3,11},{4,12},{5,13},{6,14},{7,15},{8,0},{9,1},... | collective-permute-start | bytes 958472 | tf_op jit(solution)/shard_map/ppermute | solution.py:30
  35.0 0.0 collective-permute-done.9.refs_7_
  35.0 1.9 %pair_terms.5 = (f32[384,1536]{1,0:T(8,128)S(1)}, f32[8,128]{1,0:T(8,128)S(1)}) custom-call(f32[8,128]{1,0:T(8,128)S(1)} %get-tuple-element.25.refs_0_, s32[8,128]{1,0:T(8,128)S(1)} %broadcast_in_dim.9.refs_1_, s32[8,128]{1,0:T(8,128)S(1)} %collective-permute-done.refs_2_, s32[8,128]{1,0:T(8,128)S(1)} %collective-permute-done.1.refs_3_, ...), custom_call_target="tpu_custom_call" | custom-call | flops 452984832 | bytes 4718592 | tf_op jit(solution)/shard_map/pair_terms/pallas_call | solution.py:251
  37.0 1.0 %collective-permute-done.5.refs_7_ = bf16[104,1536]{1,0:T(8,128)(2,1)S(1)} collective-permute-done((bf16[104,1536]{1,0:T(8,128)(2,1)S(1)}, bf16[104,1536]{1,0:T(8,128)(2,1)S(1)}, u32[]{:S(2)}, u32[]{:S(2)}) %collective-permute-start.5) | collective-permute-done | bytes 319520 | tf_op jit(solution)/shard_map/ppermute | solution.py:30
  37.9 2.1 %collective-permute-done.8.refs_8_ = bf16[104,1536]{1,0:T(8,128)(2,1)S(1)} collective-permute-done((bf16[104,1536]{1,0:T(8,128)(2,1)S(1)}, bf16[104,1536]{1,0:T(8,128)(2,1)S(1)}, u32[]{:S(2)}, u32[]{:S(2)}) %collective-permute-start.8) | collective-permute-done | bytes 319520 | tf_op jit(solution)/shard_map/ppermute | solution.py:30
  40.0 1.4 %pair_terms.7 = (f32[200,768]{1,0:T(8,128)S(1)}, f32[200,768]{1,0:T(8,128)S(1)}) custom-call(f32[8,128]{1,0:T(8,128)S(1)} %get-tuple-element.25.refs_0_, s32[8,128]{1,0:T(8,128)S(1)} %broadcast_in_dim.9.refs_1_, s32[8,128]{1,0:T(8,128)S(1)} %collective-permute-done.refs_2_, s32[8,128]{1,0:T(8,128)S(1)} %collective-permute-done.1.refs_3_, ...), custom_call_target="tpu_custom_call" | custom-call | flops 226492416 | bytes 2359296 | tf_op jit(solution)/shard_map/pair_terms/pallas_call | solution.py:251
  41.4 0.1 collective-permute-start.11
  41.5 1.4 %pair_terms.6 = (f32[200,768]{1,0:T(8,128)S(1)}, f32[200,768]{1,0:T(8,128)S(1)}) custom-call(f32[8,128]{1,0:T(8,128)S(1)} %get-tuple-element.25.refs_0_, s32[8,128]{1,0:T(8,128)S(1)} %broadcast_in_dim.9.refs_1_, s32[8,128]{1,0:T(8,128)S(1)} %collective-permute-done.refs_2_, s32[8,128]{1,0:T(8,128)S(1)} %collective-permute-done.1.refs_3_, ...), custom_call_target="tpu_custom_call" | custom-call | flops 226492416 | bytes 2359296 | tf_op jit(solution)/shard_map/pair_terms/pallas_call | solution.py:251
  43.0 0.6 %collective-permute-start.10 = (f32[200,768]{1,0:T(8,128)S(1)}, f32[200,768]{1,0:T(8,128)S(1)}, u32[]{:S(2)}, u32[]{:S(2)}) collective-permute-start(f32[200,768]{1,0:T(8,128)S(1)} %get-tuple-element.39), channel_id=1, source_target_pairs={{0,1},{1,0},{2,3},{3,2},{4,5},{5,4},{6,7},{7,6},{8,9},{9,8},{10,11... | collective-permute-start | bytes 1843208 | tf_op jit(solution)/shard_map/ppermute | solution.py:20
  43.5 0.0 collective-permute-done.11.arrived
  43.6 0.1 combine.3
  43.6 1.6 %collective-permute-start.13 = (bf16[208,384]{1,0:T(8,128)(2,1)S(1)}, bf16[208,384]{1,0:T(8,128)(2,1)S(1)}, u32[]{:S(2)}, u32[]{:S(2)}) collective-permute-start(bf16[208,384]{1,0:T(8,128)(2,1)S(1)} %get-tuple-element.45), channel_id=1, source_target_pairs={{0,2},{1,3},{2,0},{3,1},{4,6},{5,7},{6,4},{7,5},{8,10},{9,11},{10,... | collective-permute-start | bytes 479240 | tf_op jit(solution)/shard_map/ppermute | solution.py:20
  45.3 0.0 collective-permute-done.10.arrived
  45.3 0.8 %combine.2 = (f32[200,384]{1,0:T(8,128)S(1)}, bf16[208,384]{1,0:T(8,128)(2,1)}) custom-call(f32[200,768]{1,0:T(8,128)S(1)} %get-tuple-element.38.keep, f32[200,768]{1,0:T(8,128)S(1)} %collective-permute-done.10.arrived), custom_call_target="tpu_custom_call" | custom-call | flops 147456 | bytes 1179648 | tf_op jit(solution)/shard_map/combine/pallas_call | solution.py:279
  46.0 1.5 %collective-permute-start.12 = (bf16[208,384]{1,0:T(8,128)(2,1)}, bf16[208,384]{1,0:T(8,128)(2,1)S(1)}, u32[]{:S(2)}, u32[]{:S(2)}) collective-permute-start(bf16[208,384]{1,0:T(8,128)(2,1)} %get-tuple-element.44), channel_id=1, source_target_pairs={{0,2},{1,3},{2,0},{3,1},{4,6},{5,7},{6,4},{7,5},{8,10},{9,11},{10,... | collective-permute-start | bytes 479240 | tf_op jit(solution)/shard_map/ppermute | solution.py:20
  47.5 0.8 %copy.9 = bf16[384,1536]{0,1:T(8,128)(2,1)S(1)} copy(bf16[384,1536]{1,0:T(8,128)(2,1)S(1)} %copy-done.1) | data formatting | bytes 2359296 | tf_op args[0]
  48.3 2.2 %collective-permute-done.13.arrived_b = bf16[208,384]{1,0:T(8,128)(2,1)S(1)} collective-permute-done((bf16[208,384]{1,0:T(8,128)(2,1)S(1)}, bf16[208,384]{1,0:T(8,128)(2,1)S(1)}, u32[]{:S(2)}, u32[]{:S(2)}) %collective-permute-start.13) | collective-permute-done | bytes 159776 | tf_op jit(solution)/shard_map/ppermute | solution.py:20
  50.5 2.8 %collective-permute-done.12.arrived_a = bf16[208,384]{1,0:T(8,128)(2,1)S(1)} collective-permute-done((bf16[208,384]{1,0:T(8,128)(2,1)}, bf16[208,384]{1,0:T(8,128)(2,1)S(1)}, u32[]{:S(2)}, u32[]{:S(2)}) %collective-permute-start.12) | collective-permute-done | bytes 159776 | tf_op jit(solution)/shard_map/ppermute | solution.py:20
  53.3 2.3 %gradient.1 = (f32[1536,384]{1,0:T(8,128)}, f32[1,1]{1,0:T(1,128)}) custom-call(f32[200,384]{1,0:T(8,128)S(1)} %get-tuple-element.40.own_a, f32[200,384]{1,0:T(8,128)S(1)} %get-tuple-element.43.own_b, bf16[208,384]{1,0:T(8,128)(2,1)S(1)} %collective-permute-done.12.arrived_a, bf16[208,384]{1,0:T(8,128)(2,1)S(1)} %collective-permute-done.13.arrived_b, ...), custom_call_target="tpu_custom_call" | custom-call | flops 452984832 | bytes 2359296 | tf_op jit(solution)/shard_map/gradient/pallas_call | solution.py:319
  (1 shorter events, 0.0 us)
Async XLA Ops:
  1.3 14.4 %copy-start.1 = (bf16[384,1536]{1,0:T(8,128)(2,1)S(1)}, bf16[384,1536]{1,0:T(8,128)(2,1)}, u32[]{:S(2)}) copy-start(bf16[384,1536]{1,0:T(8,128)(2,1)} %features.2) | copy-start | bytes 3538948
  1.3 14.4 %copy-start.2 = (s32[384]{0:T(512)S(1)}, s32[384]{0:T(512)}, u32[]{:S(2)}) copy-start(s32[384]{0:T(512)} %ids.3) | copy-start | bytes 4612
  5.1 16.1 %collective-permute-start.6 = (bf16[104,1536]{1,0:T(8,128)(2,1)}, bf16[104,1536]{1,0:T(8,128)(2,1)S(1)}, u32[]{:S(2)}, u32[]{:S(2)}) collective-permute-start(bf16[104,1536]{1,0:T(8,128)(2,1)} %part_unit.1), channel_id=1, source_target_pairs={{0,24},{1,25},{2,26},{3,27},{4,28},{5,29},{6,30},{7,31},{8,16},{9,... | collective-permute-start | bytes 958472 | tf_op jit(solution)/shard_map/ppermute | solution.py:30
  10.9 3.2 %collective-permute-start = (s32[8,128]{1,0:T(8,128)S(1)}, s32[8,128]{1,0:T(8,128)S(1)}, u32[]{:S(2)}, u32[]{:S(2)}) collective-permute-start(s32[8,128]{1,0:T(8,128)S(1)} %broadcast_in_dim.9.refs_1_), channel_id=1, source_target_pairs={{0,1},{1,0},{2,3},{3,2},{4,5},{5,4},{6,7},{7,6},{8,9},{9,8},{10,11... | collective-permute-start | bytes 12296 | tf_op jit(solution)/shard_map/ppermute | solution.py:20
  11.0 10.3 %collective-permute-start.1 = (s32[8,128]{1,0:T(8,128)S(1)}, s32[8,128]{1,0:T(8,128)S(1)}, u32[]{:S(2)}, u32[]{:S(2)}) collective-permute-start(s32[8,128]{1,0:T(8,128)S(1)} %broadcast_in_dim.9.refs_1_), channel_id=1, source_target_pairs={{0,2},{1,3},{2,0},{3,1},{4,6},{5,7},{6,4},{7,5},{8,10},{9,11},{10,... | collective-permute-start | bytes 12296 | tf_op jit(solution)/shard_map/ppermute | solution.py:20
  12.6 8.7 %collective-permute-start.2 = (s32[8,128]{1,0:T(8,128)S(1)}, s32[8,128]{1,0:T(8,128)S(1)}, u32[]{:S(2)}, u32[]{:S(2)}) collective-permute-start(s32[8,128]{1,0:T(8,128)S(1)} %broadcast_in_dim.9.refs_1_), channel_id=1, source_target_pairs={{0,3},{1,2},{2,1},{3,0},{4,7},{5,6},{6,5},{7,4},{8,11},{9,10},{10,... | collective-permute-start | bytes 12296 | tf_op jit(solution)/shard_map/ppermute | solution.py:20
  12.9 13.2 %collective-permute-start.3 = (bf16[104,1536]{1,0:T(8,128)(2,1)}, bf16[104,1536]{1,0:T(8,128)(2,1)S(1)}, u32[]{:S(2)}, u32[]{:S(2)}) collective-permute-start(bf16[104,1536]{1,0:T(8,128)(2,1)} %part_unit.1), channel_id=1, source_target_pairs={{0,8},{1,9},{2,10},{3,11},{4,12},{5,13},{6,14},{7,15},{8,0},{9,1},... | collective-permute-start | bytes 958472 | tf_op jit(solution)/shard_map/ppermute | solution.py:30
  14.2 11.9 %collective-permute-start.4 = (bf16[104,1536]{1,0:T(8,128)(2,1)}, bf16[104,1536]{1,0:T(8,128)(2,1)S(1)}, u32[]{:S(2)}, u32[]{:S(2)}) collective-permute-start(bf16[104,1536]{1,0:T(8,128)(2,1)} %part_unit.1), channel_id=1, source_target_pairs={{0,4},{1,5},{2,6},{3,7},{4,0},{5,1},{6,2},{7,3},{8,12},{9,13},{10,... | collective-permute-start | bytes 958472 | tf_op jit(solution)/shard_map/ppermute | solution.py:30
  15.7 2.3 %copy-start = (bf16[1536,1536]{1,0:T(8,128)(2,1)S(1)}, bf16[1536,1536]{1,0:T(8,128)(2,1)}, u32[]{:S(2)}) copy-start(bf16[1536,1536]{1,0:T(8,128)(2,1)} %matrix.3) | copy-start | bytes 14155780
  21.3 10.5 %collective-permute-start.7 = (bf16[104,1536]{1,0:T(8,128)(2,1)S(1)}, bf16[104,1536]{1,0:T(8,128)(2,1)S(1)}, u32[]{:S(2)}, u32[]{:S(2)}) collective-permute-start(bf16[104,1536]{1,0:T(8,128)(2,1)S(1)} %collective-permute-done.6.refs_9_), channel_id=1, source_target_pairs={{0,4},{1,5},{2,6},{3,7},{4,0},{5,1},{6,2},{7,3},{8,12},{9,13},{10,... | collective-permute-start | bytes 958472 | tf_op jit(solution)/shard_map/ppermute | solution.py:30
  21.9 13.1 %collective-permute-start.9 = (bf16[104,1536]{1,0:T(8,128)(2,1)S(1)}, bf16[104,1536]{1,0:T(8,128)(2,1)S(1)}, u32[]{:S(2)}, u32[]{:S(2)}) collective-permute-start(bf16[104,1536]{1,0:T(8,128)(2,1)S(1)} %collective-permute-done.6.refs_9_), channel_id=1, source_target_pairs={{0,8},{1,9},{2,10},{3,11},{4,12},{5,13},{6,14},{7,15},{8,0},{9,1},... | collective-permute-start | bytes 958472 | tf_op jit(solution)/shard_map/ppermute | solution.py:30
  26.1 11.9 %collective-permute-start.5 = (bf16[104,1536]{1,0:T(8,128)(2,1)S(1)}, bf16[104,1536]{1,0:T(8,128)(2,1)S(1)}, u32[]{:S(2)}, u32[]{:S(2)}) collective-permute-start(bf16[104,1536]{1,0:T(8,128)(2,1)S(1)} %collective-permute-done.3.refs_8_), channel_id=1, source_target_pairs={{0,4},{1,5},{2,6},{3,7},{4,0},{5,1},{6,2},{7,3},{8,12},{9,13},{10,... | collective-permute-start | bytes 958472 | tf_op jit(solution)/shard_map/ppermute | solution.py:30
  31.8 8.2 %collective-permute-start.8 = (bf16[104,1536]{1,0:T(8,128)(2,1)S(1)}, bf16[104,1536]{1,0:T(8,128)(2,1)S(1)}, u32[]{:S(2)}, u32[]{:S(2)}) collective-permute-start(bf16[104,1536]{1,0:T(8,128)(2,1)S(1)} %collective-permute-done.7.refs_8_), channel_id=1, source_target_pairs={{0,8},{1,9},{2,10},{3,11},{4,12},{5,13},{6,14},{7,15},{8,0},{9,1},... | collective-permute-start | bytes 958472 | tf_op jit(solution)/shard_map/ppermute | solution.py:30
  41.4 2.1 %collective-permute-start.11 = (f32[200,768]{1,0:T(8,128)S(1)}, f32[200,768]{1,0:T(8,128)S(1)}, u32[]{:S(2)}, u32[]{:S(2)}) collective-permute-start(f32[200,768]{1,0:T(8,128)S(1)} %get-tuple-element.42), channel_id=1, source_target_pairs={{0,1},{1,0},{2,3},{3,2},{4,5},{5,4},{6,7},{7,6},{8,9},{9,8},{10,11... | collective-permute-start | bytes 1843208 | tf_op jit(solution)/shard_map/ppermute | solution.py:20
  43.0 2.3 %collective-permute-start.10 = (f32[200,768]{1,0:T(8,128)S(1)}, f32[200,768]{1,0:T(8,128)S(1)}, u32[]{:S(2)}, u32[]{:S(2)}) collective-permute-start(f32[200,768]{1,0:T(8,128)S(1)} %get-tuple-element.39), channel_id=1, source_target_pairs={{0,1},{1,0},{2,3},{3,2},{4,5},{5,4},{6,7},{7,6},{8,9},{9,8},{10,11... | collective-permute-start | bytes 1843208 | tf_op jit(solution)/shard_map/ppermute | solution.py:20
  43.6 6.8 %collective-permute-start.13 = (bf16[208,384]{1,0:T(8,128)(2,1)S(1)}, bf16[208,384]{1,0:T(8,128)(2,1)S(1)}, u32[]{:S(2)}, u32[]{:S(2)}) collective-permute-start(bf16[208,384]{1,0:T(8,128)(2,1)S(1)} %get-tuple-element.45), channel_id=1, source_target_pairs={{0,2},{1,3},{2,0},{3,1},{4,6},{5,7},{6,4},{7,5},{8,10},{9,11},{10,... | collective-permute-start | bytes 479240 | tf_op jit(solution)/shard_map/ppermute | solution.py:20
  46.0 7.3 %collective-permute-start.12 = (bf16[208,384]{1,0:T(8,128)(2,1)}, bf16[208,384]{1,0:T(8,128)(2,1)S(1)}, u32[]{:S(2)}, u32[]{:S(2)}) collective-permute-start(bf16[208,384]{1,0:T(8,128)(2,1)} %get-tuple-element.44), channel_id=1, source_target_pairs={{0,2},{1,3},{2,0},{3,1},{4,6},{5,7},{6,4},{7,5},{8,10},{9,11},{10,... | collective-permute-start | bytes 479240 | tf_op jit(solution)/shard_map/ppermute | solution.py:20

commit v7 on v6

--- a/solution.py
+++ b/solution.py
@@ -9,7 +9,8 @@
 
 AXES = ("peer", "group")
 STEPS = 3
-FACTS = 8
+FACTS = 16
+LANES = 128
 SMALL = pl.CostEstimate(flops=1, bytes_accessed=1, transcendentals=0)
 ANY = pl.BlockSpec(memory_space=pl.ANY)
 VMEM = pl.BlockSpec(memory_space=pltpu.VMEM)
@@ -78,15 +79,18 @@
     here = all_ids[:, :rows]
     for k in range(1, 4):
         here = jnp.where(me == k, all_ids[:, k * rows : (k + 1) * rows], here)
-    here = jnp.concatenate([here, jnp.zeros((1, 128 - rows), jnp.int32)], axis=1)
-    count = jnp.full((1, 128), filled_s[0], jnp.int32)
-    digits = [here & 255, here >> 8, count & 255, count >> 8]
-    digits.append(jnp.zeros((1, width - 512), jnp.int32))
-    facts = jnp.concatenate(digits, axis=1).astype(jnp.float32)
-    row = lax.broadcasted_iota(jnp.int32, (FACTS, width), 0)
-    facts = jnp.where(row == 0, facts, 0.0)
+    here = jnp.concatenate([here, jnp.zeros((1, LANES - rows), jnp.int32)], axis=1)
+    count = jnp.full((1, LANES), filled_s[0], jnp.int32)
+    row = lax.broadcasted_iota(jnp.int32, (FACTS, LANES), 0)
+    facts = jnp.zeros((FACTS, LANES), jnp.int32)
+    for k, digit in enumerate((here & 255, here >> 8, count & 255, count >> 8)):
+        facts = jnp.where(row == k, digit, facts)
     length = multiply(copies, features_v, matrix_v, raw)
-    unit[...] = jnp.concatenate([raw[...] / length, facts], axis=0).astype(jnp.bfloat16)
+    chunks = width // LANES
+    for k in range(chunks):
+        value = raw[:, k * LANES : (k + 1) * LANES] / length
+        unit[k * rows : (k + 1) * rows] = value.astype(jnp.bfloat16)
+    unit[chunks * rows :] = facts.astype(jnp.float32).astype(jnp.bfloat16)
 
 
 def part_unit(ids, filled, features, matrix):
@@ -95,7 +99,7 @@
     part = rows // 4
     return pl.pallas_call(
         part_unit_kernel,
-        out_shape=jax.ShapeDtypeStruct((part + FACTS, width), jnp.bfloat16),
+        out_shape=jax.ShapeDtypeStruct((part * width // LANES + FACTS, LANES), jnp.bfloat16),
         in_specs=[ANY] * 4,
         out_specs=VMEM,
         scratch_shapes=[
@@ -175,9 +179,10 @@
     rows = window[1] - window[0]
     part = unit_bf.shape[0] // 4
     offset = 0
-    values = [block[...] for block in blocks]
-    for value, (_, _, count, _) in zip(values, cuts):
-        stacked[offset : offset + count] = value[:count]
+    for block, (_, _, count, _) in zip(blocks, cuts):
+        for k in range(stacked.shape[1] // LANES):
+            at = slice(k * LANES, (k + 1) * LANES)
+            stacked[offset : offset + count, at] = block[k * count : (k + 1) * count]
         offset += count
     scores = lax.dot_general(
         unit_bf[here], stacked[...], (((1,), (1,)), ((), ())), preferred_element_type=jnp.float32
@@ -192,9 +197,10 @@
         turn = jnp.full((1, 128), -1, jnp.int32)
         for e, other in enumerate(masks):
             turn = jnp.where(other == mask, jnp.bitwise_xor(me, e), turn)
-        fact = values[owner][-FACTS:].astype(jnp.float32)[0:1]
-        ids = fact[:, begin : begin + count] + 256.0 * fact[:, 128 + begin : 128 + begin + count]
-        filled = fact[:, 256 : 256 + count] + 256.0 * fact[:, 384 : 384 + count]
+        last = blocks[owner].shape[0] - FACTS
+        fact = blocks[owner][last:].astype(jnp.float32)
+        ids = fact[0:1, begin : begin + count] + 256.0 * fact[1:2, begin : begin + count]
+        filled = fact[2:3, :count] + 256.0 * fact[3:4, :count]
         place = me * part + begin + lax.broadcasted_iota(jnp.int32, (1, count), 1)
         there = (place < filled.astype(jnp.int32)) & (turn[:, :count] >= 0)
         used = used_here & there

time: 55.7 us -> 54.4 us (0.977)
  starting transfers between devices: 21 us -> 19.3 us
    ppermute x7, starting transfers between devices: 15.2 us -> 13.6 us  [trade(): return lax.ppermute(block, AXES, route)]
  transfers between devices with their start and end apart: 14 -> 14, of which waited for: 5 -> 5; matrix products, arithmetic and copies ran while one was open for 1% -> 1% of each run, Pallas kernels for 17% -> 18%
where the time goes in v7:
time: 54.4 us; the launch traced here: 54.2 us
  starting transfers between devices  19.3 us (35%)
  Pallas kernels  17.3 us (32%)
  waiting for transfers between devices  11.1 us (20%)
  between operations  3.36 us (6%)
  local copies, waits for them, and re-layouts  3.1 us (6%)
    ppermute x7, starting transfers between devices, trade(): return lax.ppermute(block, AXES, route)  13.6 us
    pallas_call x4, Pallas kernels, pair_terms(): pl.pallas_call(functools.partial(pair_kernel, cuts, old is None, final is...  7.21 us
    ppermute x7, waiting for transfers between devices, trade(): return lax.ppermute(block, AXES, route)  6.14 us
    ppermute x7, starting transfers between devices, swap(): return lax.ppermute(block, axis, [(i, i ^ mask) for i in range(count)])  5.74 us
    ppermute x7, waiting for transfers between devices, swap(): return lax.ppermute(block, axis, [(i, i ^ mask) for i in range(count)])  4.97 us
    pallas_call x1, Pallas kernels, part_unit(): pl.pallas_call(part_unit_kernel, out_shape=jax.ShapeDtypeStruct((part * w...  3.83 us
    pallas_call x1, Pallas kernels, whole_unit(): pl.pallas_call(whole_unit_kernel, out_shape=[jax.ShapeDtypeStruct((rows,...  3.19 us
    unnamed x7, local copies, waits for them, and re-layouts  3.1 us
  transfers between devices with their start and end apart: 14, of which 5 were waited for; matrix products, arithmetic and copies ran while one was open for 1% of the time, Pallas kernels for 18%

profile of v7, /device:TPU:0, one launch (start us, length us, event | category | flops | bytes accessed | tf_op | source)
XLA Modules:
  0.0 54.2 jit_solution(6047521659669737054)
XLA Ops:
  1.3 0.0 copy-start.1
  1.3 0.0 copy-start.2
  1.3 3.8 %part_unit.1 = bf16[1168,128]{1,0:T(8,128)(2,1)} custom-call(s32[384]{0:T(512)} %ids.3, s32[1]{0:T(128)S(6)} %copy.10.filled, bf16[384,1536]{1,0:T(8,128)(2,1)} %features.2, bf16[1536,1536]{1,0:T(8,128)(2,1)} %matrix.3), custom_call_target="tpu_custom_call" | custom-call | flops 905969664 | bytes 4718592 | tf_op jit(solution)/shard_map/part_unit/pallas_call | solution.py:100
  5.1 5.1 %collective-permute-start.6 = (bf16[1168,128]{1,0:T(8,128)(2,1)}, bf16[1168,128]{1,0:T(8,128)(2,1)S(1)}, u32[]{:S(2)}, u32[]{:S(2)}) collective-permute-start(bf16[1168,128]{1,0:T(8,128)(2,1)} %part_unit.1), channel_id=1, source_target_pairs={{0,24},{1,25},{2,26},{3,27},{4,28},{5,29},{6,30},{7,31},{8,16},{9,... | collective-permute-start | bytes 897032 | tf_op jit(solution)/shard_map/ppermute | solution.py:31
  10.9 0.1 collective-permute-start
  11.0 1.6 %collective-permute-start.1 = (s32[8,128]{1,0:T(8,128)S(1)}, s32[8,128]{1,0:T(8,128)S(1)}, u32[]{:S(2)}, u32[]{:S(2)}) collective-permute-start(s32[8,128]{1,0:T(8,128)S(1)} %broadcast_in_dim.9.refs_1_), channel_id=1, source_target_pairs={{0,2},{1,3},{2,0},{3,1},{4,6},{5,7},{6,4},{7,5},{8,10},{9,11},{10,... | collective-permute-start | bytes 12296 | tf_op jit(solution)/shard_map/ppermute | solution.py:21
  12.6 0.3 collective-permute-start.2
  12.9 0.0 collective-permute-start.3
  14.2 0.0 collective-permute-done.refs_2_
  14.2 1.6 %collective-permute-start.4 = (bf16[1168,128]{1,0:T(8,128)(2,1)}, bf16[1168,128]{1,0:T(8,128)(2,1)S(1)}, u32[]{:S(2)}, u32[]{:S(2)}) collective-permute-start(bf16[1168,128]{1,0:T(8,128)(2,1)} %part_unit.1), channel_id=1, source_target_pairs={{0,4},{1,5},{2,6},{3,7},{4,0},{5,1},{6,2},{7,3},{8,12},{9,13},{10,... | collective-permute-start | bytes 897032 | tf_op jit(solution)/shard_map/ppermute | solution.py:31
  15.7 0.0 copy-done.1
  15.7 0.0 copy-done.2
  15.7 0.0 copy-start
  15.7 2.3 %copy-done = bf16[1536,1536]{1,0:T(8,128)(2,1)S(1)} copy-done((bf16[1536,1536]{1,0:T(8,128)(2,1)S(1)}, bf16[1536,1536]{1,0:T(8,128)(2,1)}, u32[]{:S(2)}) %copy-start) | copy-done | bytes 4718616
  18.1 3.2 %whole_unit.1 = (f32[384,1536]{1,0:T(8,128)S(1)}, bf16[384,1536]{1,0:T(8,128)(2,1)S(1)}, f32[384,128]{1,0:T(8,128)S(1)}, f32[384,128]{1,0:T(8,128)S(1)}, f32[8,128]{1,0:T(8,128)S(1)}) custom-call(s32[384]{0:T(512)S(1)} %copy-done.2, s32[1]{0:T(128)S(6)} %copy.10.filled, f32[1]{0:T(128)S(6)} %copy.12.scale, f32[1]{0:T(128)S(6)} %copy.13.shift, ...), custom_call_target="tpu_custom_call" | custom-call | flops 1811939328 | bytes 9437184 | tf_op jit(solution)/shard_map/whole_unit/pallas_call | solution.py:139
  21.3 0.0 collective-permute-done.1.refs_3_
  21.3 0.0 collective-permute-done.2.refs_4_
  21.3 0.0 collective-permute-done.6.refs_9_
  21.3 0.6 %collective-permute-start.7 = (bf16[1168,128]{1,0:T(8,128)(2,1)S(1)}, bf16[1168,128]{1,0:T(8,128)(2,1)S(1)}, u32[]{:S(2)}, u32[]{:S(2)}) collective-permute-start(bf16[1168,128]{1,0:T(8,128)(2,1)S(1)} %collective-permute-done.6.refs_9_), channel_id=1, source_target_pairs={{0,4},{1,5},{2,6},{3,7},{4,0},{5,1},{6,2},{7,3},{8,12},{9,13},{10,... | collective-permute-start | bytes 897032 | tf_op jit(solution)/shard_map/ppermute | solution.py:31
  21.9 3.3 %collective-permute-start.9 = (bf16[1168,128]{1,0:T(8,128)(2,1)S(1)}, bf16[1168,128]{1,0:T(8,128)(2,1)S(1)}, u32[]{:S(2)}, u32[]{:S(2)}) collective-permute-start(bf16[1168,128]{1,0:T(8,128)(2,1)S(1)} %collective-permute-done.6.refs_9_), channel_id=1, source_target_pairs={{0,8},{1,9},{2,10},{3,11},{4,12},{5,13},{6,14},{7,15},{8,0},{9,1},... | collective-permute-start | bytes 897032 | tf_op jit(solution)/shard_map/ppermute | solution.py:31
  25.2 0.0 collective-permute-done.3.refs_8_
  25.2 0.0 collective-permute-done.4.refs_7_
  25.2 0.7 %collective-permute-start.5 = (bf16[1168,128]{1,0:T(8,128)(2,1)S(1)}, bf16[1168,128]{1,0:T(8,128)(2,1)S(1)}, u32[]{:S(2)}, u32[]{:S(2)}) collective-permute-start(bf16[1168,128]{1,0:T(8,128)(2,1)S(1)} %collective-permute-done.3.refs_8_), channel_id=1, source_target_pairs={{0,4},{1,5},{2,6},{3,7},{4,0},{5,1},{6,2},{7,3},{8,12},{9,13},{10,... | collective-permute-start | bytes 897032 | tf_op jit(solution)/shard_map/ppermute | solution.py:31
  25.8 2.3 %pair_terms.4 = (f32[384,1536]{1,0:T(8,128)S(1)}, f32[8,128]{1,0:T(8,128)S(1)}) custom-call(f32[8,128]{1,0:T(8,128)S(1)} %get-tuple-element.25.refs_0_, s32[8,128]{1,0:T(8,128)S(1)} %broadcast_in_dim.9.refs_1_, s32[8,128]{1,0:T(8,128)S(1)} %collective-permute-done.refs_2_, s32[8,128]{1,0:T(8,128)S(1)} %collective-permute-done.1.refs_3_, ...), custom_call_target="tpu_custom_call" | custom-call | flops 679477248 | bytes 4718592 | tf_op jit(solution)/shard_map/pair_terms/pallas_call | solution.py:257
  28.2 3.2 %collective-permute-done.7.refs_8_ = bf16[1168,128]{1,0:T(8,128)(2,1)S(1)} collective-permute-done((bf16[1168,128]{1,0:T(8,128)(2,1)S(1)}, bf16[1168,128]{1,0:T(8,128)(2,1)S(1)}, u32[]{:S(2)}, u32[]{:S(2)}) %collective-permute-start.7) | collective-permute-done | bytes 299040 | tf_op jit(solution)/shard_map/ppermute | solution.py:31
  31.3 2.4 %collective-permute-start.8 = (bf16[1168,128]{1,0:T(8,128)(2,1)S(1)}, bf16[1168,128]{1,0:T(8,128)(2,1)S(1)}, u32[]{:S(2)}, u32[]{:S(2)}) collective-permute-start(bf16[1168,128]{1,0:T(8,128)(2,1)S(1)} %collective-permute-done.7.refs_8_), channel_id=1, source_target_pairs={{0,8},{1,9},{2,10},{3,11},{4,12},{5,13},{6,14},{7,15},{8,0},{9,1},... | collective-permute-start | bytes 897032 | tf_op jit(solution)/shard_map/ppermute | solution.py:31
  33.7 0.0 collective-permute-done.9.refs_7_
  33.7 2.0 %pair_terms.5 = (f32[384,1536]{1,0:T(8,128)S(1)}, f32[8,128]{1,0:T(8,128)S(1)}) custom-call(f32[8,128]{1,0:T(8,128)S(1)} %get-tuple-element.25.refs_0_, s32[8,128]{1,0:T(8,128)S(1)} %broadcast_in_dim.9.refs_1_, s32[8,128]{1,0:T(8,128)S(1)} %collective-permute-done.refs_2_, s32[8,128]{1,0:T(8,128)S(1)} %collective-permute-done.1.refs_3_, ...), custom_call_target="tpu_custom_call" | custom-call | flops 452984832 | bytes 4718592 | tf_op jit(solution)/shard_map/pair_terms/pallas_call | solution.py:257
  35.7 1.2 %collective-permute-done.5.refs_7_ = bf16[1168,128]{1,0:T(8,128)(2,1)S(1)} collective-permute-done((bf16[1168,128]{1,0:T(8,128)(2,1)S(1)}, bf16[1168,128]{1,0:T(8,128)(2,1)S(1)}, u32[]{:S(2)}, u32[]{:S(2)}) %collective-permute-start.5) | collective-permute-done | bytes 299040 | tf_op jit(solution)/shard_map/ppermute | solution.py:31
  36.8 1.8 %collective-permute-done.8.refs_8_ = bf16[1168,128]{1,0:T(8,128)(2,1)S(1)} collective-permute-done((bf16[1168,128]{1,0:T(8,128)(2,1)S(1)}, bf16[1168,128]{1,0:T(8,128)(2,1)S(1)}, u32[]{:S(2)}, u32[]{:S(2)}) %collective-permute-start.8) | collective-permute-done | bytes 299040 | tf_op jit(solution)/shard_map/ppermute | solution.py:31
  38.7 1.5 %pair_terms.7 = (f32[200,768]{1,0:T(8,128)S(1)}, f32[200,768]{1,0:T(8,128)S(1)}) custom-call(f32[8,128]{1,0:T(8,128)S(1)} %get-tuple-element.25.refs_0_, s32[8,128]{1,0:T(8,128)S(1)} %broadcast_in_dim.9.refs_1_, s32[8,128]{1,0:T(8,128)S(1)} %collective-permute-done.refs_2_, s32[8,128]{1,0:T(8,128)S(1)} %collective-permute-done.1.refs_3_, ...), custom_call_target="tpu_custom_call" | custom-call | flops 226492416 | bytes 2359296 | tf_op jit(solution)/shard_map/pair_terms/pallas_call | solution.py:257
  40.1 0.1 collective-permute-start.11
  40.2 1.5 %pair_terms.6 = (f32[200,768]{1,0:T(8,128)S(1)}, f32[200,768]{1,0:T(8,128)S(1)}) custom-call(f32[8,128]{1,0:T(8,128)S(1)} %get-tuple-element.25.refs_0_, s32[8,128]{1,0:T(8,128)S(1)} %broadcast_in_dim.9.refs_1_, s32[8,128]{1,0:T(8,128)S(1)} %collective-permute-done.refs_2_, s32[8,128]{1,0:T(8,128)S(1)} %collective-permute-done.1.refs_3_, ...), custom_call_target="tpu_custom_call" | custom-call | flops 226492416 | bytes 2359296 | tf_op jit(solution)/shard_map/pair_terms/pallas_call | solution.py:257
  41.7 0.6 %collective-permute-start.10 = (f32[200,768]{1,0:T(8,128)S(1)}, f32[200,768]{1,0:T(8,128)S(1)}, u32[]{:S(2)}, u32[]{:S(2)}) collective-permute-start(f32[200,768]{1,0:T(8,128)S(1)} %get-tuple-element.39), channel_id=1, source_target_pairs={{0,1},{1,0},{2,3},{3,2},{4,5},{5,4},{6,7},{7,6},{8,9},{9,8},{10,11... | collective-permute-start | bytes 1843208 | tf_op jit(solution)/shard_map/ppermute | solution.py:21
  42.3 0.0 collective-permute-done.11.arrived
  42.3 0.1 combine.3
  42.3 1.6 %collective-permute-start.13 = (bf16[208,384]{1,0:T(8,128)(2,1)S(1)}, bf16[208,384]{1,0:T(8,128)(2,1)S(1)}, u32[]{:S(2)}, u32[]{:S(2)}) collective-permute-start(bf16[208,384]{1,0:T(8,128)(2,1)S(1)} %get-tuple-element.45), channel_id=1, source_target_pairs={{0,2},{1,3},{2,0},{3,1},{4,6},{5,7},{6,4},{7,5},{8,10},{9,11},{10,... | collective-permute-start | bytes 479240 | tf_op jit(solution)/shard_map/ppermute | solution.py:21
  44.0 0.0 collective-permute-done.10.arrived
  44.0 0.7 %combine.2 = (f32[200,384]{1,0:T(8,128)S(1)}, bf16[208,384]{1,0:T(8,128)(2,1)}) custom-call(f32[200,768]{1,0:T(8,128)S(1)} %get-tuple-element.38.keep, f32[200,768]{1,0:T(8,128)S(1)} %collective-permute-done.10.arrived), custom_call_target="tpu_custom_call" | custom-call | flops 147456 | bytes 1179648 | tf_op jit(solution)/shard_map/combine/pallas_call | solution.py:285
  44.7 1.5 %collective-permute-start.12 = (bf16[208,384]{1,0:T(8,128)(2,1)}, bf16[208,384]{1,0:T(8,128)(2,1)S(1)}, u32[]{:S(2)}, u32[]{:S(2)}) collective-permute-start(bf16[208,384]{1,0:T(8,128)(2,1)} %get-tuple-element.44), channel_id=1, source_target_pairs={{0,2},{1,3},{2,0},{3,1},{4,6},{5,7},{6,4},{7,5},{8,10},{9,11},{10,... | collective-permute-start | bytes 479240 | tf_op jit(solution)/shard_map/ppermute | solution.py:21
  46.2 0.8 %copy.9 = bf16[384,1536]{0,1:T(8,128)(2,1)S(1)} copy(bf16[384,1536]{1,0:T(8,128)(2,1)S(1)} %copy-done.1) | data formatting | bytes 2359296 | tf_op args[0]
  47.0 2.2 %collective-permute-done.13.arrived_b = bf16[208,384]{1,0:T(8,128)(2,1)S(1)} collective-permute-done((bf16[208,384]{1,0:T(8,128)(2,1)S(1)}, bf16[208,384]{1,0:T(8,128)(2,1)S(1)}, u32[]{:S(2)}, u32[]{:S(2)}) %collective-permute-start.13) | collective-permute-done | bytes 159776 | tf_op jit(solution)/shard_map/ppermute | solution.py:21
  49.2 2.8 %collective-permute-done.12.arrived_a = bf16[208,384]{1,0:T(8,128)(2,1)S(1)} collective-permute-done((bf16[208,384]{1,0:T(8,128)(2,1)}, bf16[208,384]{1,0:T(8,128)(2,1)S(1)}, u32[]{:S(2)}, u32[]{:S(2)}) %collective-permute-start.12) | collective-permute-done | bytes 159776 | tf_op jit(solution)/shard_map/ppermute | solution.py:21
  51.9 2.3 %gradient.1 = (f32[1536,384]{1,0:T(8,128)}, f32[1,1]{1,0:T(1,128)}) custom-call(f32[200,384]{1,0:T(8,128)S(1)} %get-tuple-element.40.own_a, f32[200,384]{1,0:T(8,128)S(1)} %get-tuple-element.43.own_b, bf16[208,384]{1,0:T(8,128)(2,1)S(1)} %collective-permute-done.12.arrived_a, bf16[208,384]{1,0:T(8,128)(2,1)S(1)} %collective-permute-done.13.arrived_b, ...), custom_call_target="tpu_custom_call" | custom-call | flops 452984832 | bytes 2359296 | tf_op jit(solution)/shard_map/gradient/pallas_call | solution.py:325
  (1 shorter events, 0.0 us)
Async XLA Ops:
  1.3 14.5 %copy-start.1 = (bf16[384,1536]{1,0:T(8,128)(2,1)S(1)}, bf16[384,1536]{1,0:T(8,128)(2,1)}, u32[]{:S(2)}) copy-start(bf16[384,1536]{1,0:T(8,128)(2,1)} %features.2) | copy-start | bytes 3538948
  1.3 14.4 %copy-start.2 = (s32[384]{0:T(512)S(1)}, s32[384]{0:T(512)}, u32[]{:S(2)}) copy-start(s32[384]{0:T(512)} %ids.3) | copy-start | bytes 4612
  5.1 16.2 %collective-permute-start.6 = (bf16[1168,128]{1,0:T(8,128)(2,1)}, bf16[1168,128]{1,0:T(8,128)(2,1)S(1)}, u32[]{:S(2)}, u32[]{:S(2)}) collective-permute-start(bf16[1168,128]{1,0:T(8,128)(2,1)} %part_unit.1), channel_id=1, source_target_pairs={{0,24},{1,25},{2,26},{3,27},{4,28},{5,29},{6,30},{7,31},{8,16},{9,... | collective-permute-start | bytes 897032 | tf_op jit(solution)/shard_map/ppermute | solution.py:31
  10.9 3.2 %collective-permute-start = (s32[8,128]{1,0:T(8,128)S(1)}, s32[8,128]{1,0:T(8,128)S(1)}, u32[]{:S(2)}, u32[]{:S(2)}) collective-permute-start(s32[8,128]{1,0:T(8,128)S(1)} %broadcast_in_dim.9.refs_1_), channel_id=1, source_target_pairs={{0,1},{1,0},{2,3},{3,2},{4,5},{5,4},{6,7},{7,6},{8,9},{9,8},{10,11... | collective-permute-start | bytes 12296 | tf_op jit(solution)/shard_map/ppermute | solution.py:21
  11.0 10.3 %collective-permute-start.1 = (s32[8,128]{1,0:T(8,128)S(1)}, s32[8,128]{1,0:T(8,128)S(1)}, u32[]{:S(2)}, u32[]{:S(2)}) collective-permute-start(s32[8,128]{1,0:T(8,128)S(1)} %broadcast_in_dim.9.refs_1_), channel_id=1, source_target_pairs={{0,2},{1,3},{2,0},{3,1},{4,6},{5,7},{6,4},{7,5},{8,10},{9,11},{10,... | collective-permute-start | bytes 12296 | tf_op jit(solution)/shard_map/ppermute | solution.py:21
  12.6 8.7 %collective-permute-start.2 = (s32[8,128]{1,0:T(8,128)S(1)}, s32[8,128]{1,0:T(8,128)S(1)}, u32[]{:S(2)}, u32[]{:S(2)}) collective-permute-start(s32[8,128]{1,0:T(8,128)S(1)} %broadcast_in_dim.9.refs_1_), channel_id=1, source_target_pairs={{0,3},{1,2},{2,1},{3,0},{4,7},{5,6},{6,5},{7,4},{8,11},{9,10},{10,... | collective-permute-start | bytes 12296 | tf_op jit(solution)/shard_map/ppermute | solution.py:21
  12.9 12.3 %collective-permute-start.3 = (bf16[1168,128]{1,0:T(8,128)(2,1)}, bf16[1168,128]{1,0:T(8,128)(2,1)S(1)}, u32[]{:S(2)}, u32[]{:S(2)}) collective-permute-start(bf16[1168,128]{1,0:T(8,128)(2,1)} %part_unit.1), channel_id=1, source_target_pairs={{0,8},{1,9},{2,10},{3,11},{4,12},{5,13},{6,14},{7,15},{8,0},{9,1},... | collective-permute-start | bytes 897032 | tf_op jit(solution)/shard_map/ppermute | solution.py:31
  14.2 11.0 %collective-permute-start.4 = (bf16[1168,128]{1,0:T(8,128)(2,1)}, bf16[1168,128]{1,0:T(8,128)(2,1)S(1)}, u32[]{:S(2)}, u32[]{:S(2)}) collective-permute-start(bf16[1168,128]{1,0:T(8,128)(2,1)} %part_unit.1), channel_id=1, source_target_pairs={{0,4},{1,5},{2,6},{3,7},{4,0},{5,1},{6,2},{7,3},{8,12},{9,13},{10,... | collective-permute-start | bytes 897032 | tf_op jit(solution)/shard_map/ppermute | solution.py:31
  15.7 2.3 %copy-start = (bf16[1536,1536]{1,0:T(8,128)(2,1)S(1)}, bf16[1536,1536]{1,0:T(8,128)(2,1)}, u32[]{:S(2)}) copy-start(bf16[1536,1536]{1,0:T(8,128)(2,1)} %matrix.3) | copy-start | bytes 14155780
  21.3 10.0 %collective-permute-start.7 = (bf16[1168,128]{1,0:T(8,128)(2,1)S(1)}, bf16[1168,128]{1,0:T(8,128)(2,1)S(1)}, u32[]{:S(2)}, u32[]{:S(2)}) collective-permute-start(bf16[1168,128]{1,0:T(8,128)(2,1)S(1)} %collective-permute-done.6.refs_9_), channel_id=1, source_target_pairs={{0,4},{1,5},{2,6},{3,7},{4,0},{5,1},{6,2},{7,3},{8,12},{9,13},{10,... | collective-permute-start | bytes 897032 | tf_op jit(solution)/shard_map/ppermute | solution.py:31
  21.9 11.8 %collective-permute-start.9 = (bf16[1168,128]{1,0:T(8,128)(2,1)S(1)}, bf16[1168,128]{1,0:T(8,128)(2,1)S(1)}, u32[]{:S(2)}, u32[]{:S(2)}) collective-permute-start(bf16[1168,128]{1,0:T(8,128)(2,1)S(1)} %collective-permute-done.6.refs_9_), channel_id=1, source_target_pairs={{0,8},{1,9},{2,10},{3,11},{4,12},{5,13},{6,14},{7,15},{8,0},{9,1},... | collective-permute-start | bytes 897032 | tf_op jit(solution)/shard_map/ppermute | solution.py:31
  25.2 11.7 %collective-permute-start.5 = (bf16[1168,128]{1,0:T(8,128)(2,1)S(1)}, bf16[1168,128]{1,0:T(8,128)(2,1)S(1)}, u32[]{:S(2)}, u32[]{:S(2)}) collective-permute-start(bf16[1168,128]{1,0:T(8,128)(2,1)S(1)} %collective-permute-done.3.refs_8_), channel_id=1, source_target_pairs={{0,4},{1,5},{2,6},{3,7},{4,0},{5,1},{6,2},{7,3},{8,12},{9,13},{10,... | collective-permute-start | bytes 897032 | tf_op jit(solution)/shard_map/ppermute | solution.py:31
  31.3 7.3 %collective-permute-start.8 = (bf16[1168,128]{1,0:T(8,128)(2,1)S(1)}, bf16[1168,128]{1,0:T(8,128)(2,1)S(1)}, u32[]{:S(2)}, u32[]{:S(2)}) collective-permute-start(bf16[1168,128]{1,0:T(8,128)(2,1)S(1)} %collective-permute-done.7.refs_8_), channel_id=1, source_target_pairs={{0,8},{1,9},{2,10},{3,11},{4,12},{5,13},{6,14},{7,15},{8,0},{9,1},... | collective-permute-start | bytes 897032 | tf_op jit(solution)/shard_map/ppermute | solution.py:31
  40.1 2.1 %collective-permute-start.11 = (f32[200,768]{1,0:T(8,128)S(1)}, f32[200,768]{1,0:T(8,128)S(1)}, u32[]{:S(2)}, u32[]{:S(2)}) collective-permute-start(f32[200,768]{1,0:T(8,128)S(1)} %get-tuple-element.42), channel_id=1, source_target_pairs={{0,1},{1,0},{2,3},{3,2},{4,5},{5,4},{6,7},{7,6},{8,9},{9,8},{10,11... | collective-permute-start | bytes 1843208 | tf_op jit(solution)/shard_map/ppermute | solution.py:21
  41.7 2.3 %collective-permute-start.10 = (f32[200,768]{1,0:T(8,128)S(1)}, f32[200,768]{1,0:T(8,128)S(1)}, u32[]{:S(2)}, u32[]{:S(2)}) collective-permute-start(f32[200,768]{1,0:T(8,128)S(1)} %get-tuple-element.39), channel_id=1, source_target_pairs={{0,1},{1,0},{2,3},{3,2},{4,5},{5,4},{6,7},{7,6},{8,9},{9,8},{10,11... | collective-permute-start | bytes 1843208 | tf_op jit(solution)/shard_map/ppermute | solution.py:21
  42.3 6.8 %collective-permute-start.13 = (bf16[208,384]{1,0:T(8,128)(2,1)S(1)}, bf16[208,384]{1,0:T(8,128)(2,1)S(1)}, u32[]{:S(2)}, u32[]{:S(2)}) collective-permute-start(bf16[208,384]{1,0:T(8,128)(2,1)S(1)} %get-tuple-element.45), channel_id=1, source_target_pairs={{0,2},{1,3},{2,0},{3,1},{4,6},{5,7},{6,4},{7,5},{8,10},{9,11},{10,... | collective-permute-start | bytes 479240 | tf_op jit(solution)/shard_map/ppermute | solution.py:21
  44.7 7.3 %collective-permute-start.12 = (bf16[208,384]{1,0:T(8,128)(2,1)}, bf16[208,384]{1,0:T(8,128)(2,1)S(1)}, u32[]{:S(2)}, u32[]{:S(2)}) collective-permute-start(bf16[208,384]{1,0:T(8,128)(2,1)} %get-tuple-element.44), channel_id=1, source_target_pairs={{0,2},{1,3},{2,0},{3,1},{4,6},{5,7},{6,4},{7,5},{8,10},{9,11},{10,... | collective-permute-start | bytes 479240 | tf_op jit(solution)/shard_map/ppermute | solution.py:21

commit v8 on v7

--- a/solution.py
+++ b/solution.py
@@ -66,13 +66,13 @@
 def part_unit_kernel(ids, filled, features, matrix, unit, ids_v, filled_s, features_v, matrix_v, raw, sems, small_sems):
     rows, width = raw.shape
     me = lax.axis_index("group")
-    copies = load(features, matrix, features_v, matrix_v, sems, me * rows, rows)
     small = [
         pltpu.make_async_copy(ids, ids_v, small_sems.at[0]),
         pltpu.make_async_copy(filled, filled_s, small_sems.at[1]),
     ]
     for copy in small:
         copy.start()
+    copies = load(features, matrix, features_v, matrix_v, sems, me * rows, rows)
     for copy in small:
         copy.wait()
     all_ids = ids_v[...].reshape(1, 4 * rows)
@@ -269,15 +269,17 @@
 def combine_kernel(keep, arrived, own, send):
     rows, step = own.shape[0] - 8, own.shape[1]
     own[...] = keep[:, :step] + arrived[:, :step]
-    send[:rows] = (keep[:rows, step:] + arrived[:rows, step:]).astype(jnp.bfloat16)
+    for k in range(step // LANES):
+        at = slice(step + k * LANES, step + (k + 1) * LANES)
+        value = keep[:rows, at] + arrived[:rows, at]
+        send[k * rows : (k + 1) * rows] = value.astype(jnp.bfloat16)
     losses = keep[rows : rows + 1, 0:128] + arrived[rows : rows + 1, 0:128]
     high = losses.astype(jnp.bfloat16).astype(jnp.float32)
     middle = (losses - high).astype(jnp.bfloat16).astype(jnp.float32)
     low = losses - high - middle
-    line = lax.broadcasted_iota(jnp.int32, (16, 128), 0)
+    line = lax.broadcasted_iota(jnp.int32, (FACTS, LANES), 0)
     packed = jnp.where(line == 0, high, jnp.where(line == 1, middle, jnp.where(line == 2, low, 0.0)))
-    send[rows:] = jnp.zeros((16, step), jnp.bfloat16)
-    send[rows:, 0:128] = packed.astype(jnp.bfloat16)
+    send[step // LANES * rows :] = packed.astype(jnp.bfloat16)
 
 
 def combine(keep, arrived):
@@ -286,7 +288,7 @@
         combine_kernel,
         out_shape=[
             jax.ShapeDtypeStruct((rows + 8, width // 2), jnp.float32),
-            jax.ShapeDtypeStruct((rows + 16, width // 2), jnp.bfloat16),
+            jax.ShapeDtypeStruct((rows * (width // 2 // LANES) + FACTS, LANES), jnp.bfloat16),
         ],
         in_specs=[VMEM] * 2,
         out_specs=[VMEM] * 2,
@@ -296,24 +298,29 @@
     )(keep, arrived)
 
 
-def gradient_kernel(own_a, own_b, arrived_a, arrived_b, features, grad, loss, draw, parts, sems):
+def gradient_kernel(own_a, own_b, arrived_a, arrived_b, features, grad, loss, draw, parts, value, sems):
     rows = features.shape[1]
     half = rows // 2
     steps, height = parts.shape[:2]
-    draw[:half] = (own_a[:half] + arrived_a[:half].astype(jnp.float32)).astype(jnp.bfloat16)
-    draw[half:] = (own_b[:half] + arrived_b[:half].astype(jnp.float32)).astype(jnp.bfloat16)
-    copies = []
+    total = own_a[half : half + 1, 0:128] + own_b[half : half + 1, 0:128]
+    for arrived in (arrived_a, arrived_b):
+        low = arrived[arrived.shape[0] - FACTS :].astype(jnp.float32)
+        total += jnp.sum(low, axis=0, keepdims=True)
+    lane = lax.broadcasted_iota(jnp.int32, (1, 128), 1)
+    mine = jnp.where(lane == lax.axis_index("group"), total, 0.0)
+    value[...] = jnp.sum(mine, axis=1, keepdims=True) / (rows * rows)
+    copies = [pltpu.make_async_copy(value, loss, sems.at[steps])]
+    copies[0].start()
+    for begin, own, arrived in ((0, own_a, arrived_a), (half, own_b, arrived_b)):
+        for k in range(draw.shape[1] // LANES):
+            at = slice(k * LANES, (k + 1) * LANES)
+            value = own[:half, at] + arrived[k * half : (k + 1) * half].astype(jnp.float32)
+            draw[begin : begin + half, at] = value.astype(jnp.bfloat16)
     for k in range(steps):
         at = pl.ds(k * height, height)
         parts[k] = jnp.dot(features[at], draw[...], preferred_element_type=jnp.float32)
         copies.append(pltpu.make_async_copy(parts.at[k], grad.at[at], sems.at[k]))
-        copies[k].start()
-    total = own_a[half : half + 1, 0:128] + own_b[half : half + 1, 0:128]
-    for arrived in (arrived_a, arrived_b):
-        total += jnp.sum(arrived[half:, 0:128].astype(jnp.float32), axis=0, keepdims=True)
-    lane = lax.broadcasted_iota(jnp.int32, (1, 128), 1)
-    mine = jnp.where(lane == lax.axis_index("group"), total, 0.0)
-    loss[...] = jnp.sum(mine, axis=1, keepdims=True) / (rows * rows)
+        copies[-1].start()
     for copy in copies:
         copy.wait()
 
@@ -329,11 +336,12 @@
             jax.ShapeDtypeStruct((1, 1), jnp.float32),
         ],
         in_specs=[VMEM] * 5,
-        out_specs=[ANY, VMEM],
+        out_specs=[ANY, ANY],
         scratch_shapes=[
             pltpu.VMEM((rows, width), jnp.bfloat16),
             pltpu.VMEM((steps, depth // steps, width), jnp.float32),
-            pltpu.SemaphoreType.DMA((steps,)),
+            pltpu.VMEM((1, 1), jnp.float32),
+            pltpu.SemaphoreType.DMA((steps + 1,)),
         ],
         compiler_params=pltpu.CompilerParams(vmem_limit_bytes=16 << 20),
         cost_estimate=pl.CostEstimate(
@@ -367,13 +375,14 @@
     middle = pair_terms(
         *common, [far_s, far_x], ((4, 0, part, 0), (7, 0, part, 1)), old=early
     )
+    middle = pair_terms(*common, [side_x], ((3, 0, part, 0),), old=middle)
     own, arrived = [], []
     sent = []
     for window in ((0, rows // 2), (rows // 2, rows)):
         keep, send = pair_terms(
             *common,
-            [side_x, last],
-            ((3, 0, part, 0), (5, 0, part, 1)),
+            [last],
+            ((5, 0, part, 0),),
             old=middle,
             final=[unit, length],
             window=window,

time: 54.4 us -> 53.4 us (0.982)
  waiting for transfers between devices: 11.1 us -> 9.43 us
  Pallas kernels: 17.3 us -> 17.9 us
    ppermute x7, waiting for transfers between devices: 6.14 us -> 4.34 us  [trade(): return lax.ppermute(block, AXES, route)]
    pallas_call x4 -> x5, Pallas kernels: 7.21 us -> 8.25 us  [pair_terms(): pl.pallas_call(functools.partial(pair_kernel, cuts, old is None, final is...]
  transfers between devices with their start and end apart: 14 -> 14, of which waited for: 5 -> 6; matrix products, arithmetic and copies ran while one was open for 1% -> 1% of each run, Pallas kernels for 18% -> 21%
where the time goes in v8:
time: 53.4 us; the launch traced here: 53.2 us
  starting transfers between devices  19.4 us (36%)
  Pallas kernels  17.9 us (34%)
  waiting for transfers between devices  9.43 us (18%)
  between operations  3.4 us (6%)
  local copies, waits for them, and re-layouts  3.07 us (6%)
    ppermute x7, starting transfers between devices, trade(): return lax.ppermute(block, AXES, route)  13.9 us
    pallas_call x5, Pallas kernels, pair_terms(): pl.pallas_call(functools.partial(pair_kernel, cuts, old is None, final is...  8.25 us
    ppermute x7, starting transfers between devices, swap(): return lax.ppermute(block, axis, [(i, i ^ mask) for i in range(count)])  5.52 us
    ppermute x7, waiting for transfers between devices, swap(): return lax.ppermute(block, axis, [(i, i ^ mask) for i in range(count)])  5.09 us
    ppermute x7, waiting for transfers between devices, trade(): return lax.ppermute(block, AXES, route)  4.34 us
    pallas_call x1, Pallas kernels, part_unit(): pl.pallas_call(part_unit_kernel, out_shape=jax.ShapeDtypeStruct((part * w...  3.83 us
    pallas_call x1, Pallas kernels, whole_unit(): pl.pallas_call(whole_unit_kernel, out_shape=[jax.ShapeDtypeStruct((rows,...  3.19 us
    unnamed x7, local copies, waits for them, and re-layouts  3.07 us
  transfers between devices with their start and end apart: 14, of which 6 were waited for; matrix products, arithmetic and copies ran while one was open for 1% of the time, Pallas kernels for 21%

profile of v8, /device:TPU:0, one launch (start us, length us, event | category | flops | bytes accessed | tf_op | source)
XLA Modules:
  0.0 53.2 jit_solution(256993262330286030)
XLA Ops:
  1.3 0.0 copy-start.1
  1.3 0.0 copy-start.2
  1.3 3.8 %part_unit.1 = bf16[1168,128]{1,0:T(8,128)(2,1)} custom-call(s32[384]{0:T(512)} %ids.3, s32[1]{0:T(128)S(6)} %copy.10.filled, bf16[384,1536]{1,0:T(8,128)(2,1)} %features.2, bf16[1536,1536]{1,0:T(8,128)(2,1)} %matrix.3), custom_call_target="tpu_custom_call" | custom-call | flops 905969664 | bytes 4718592 | tf_op jit(solution)/shard_map/part_unit/pallas_call | solution.py:100
  5.1 5.1 %collective-permute-start.3 = (bf16[1168,128]{1,0:T(8,128)(2,1)}, bf16[1168,128]{1,0:T(8,128)(2,1)S(1)}, u32[]{:S(2)}, u32[]{:S(2)}) collective-permute-start(bf16[1168,128]{1,0:T(8,128)(2,1)} %part_unit.1), channel_id=1, source_target_pairs={{0,24},{1,25},{2,26},{3,27},{4,28},{5,29},{6,30},{7,31},{8,16},{9,... | collective-permute-start | bytes 897032 | tf_op jit(solution)/shard_map/ppermute | solution.py:31
  10.9 0.1 collective-permute-start
  11.0 1.6 %collective-permute-start.1 = (s32[8,128]{1,0:T(8,128)S(1)}, s32[8,128]{1,0:T(8,128)S(1)}, u32[]{:S(2)}, u32[]{:S(2)}) collective-permute-start(s32[8,128]{1,0:T(8,128)S(1)} %broadcast_in_dim.9.refs_1_), channel_id=1, source_target_pairs={{0,2},{1,3},{2,0},{3,1},{4,6},{5,7},{6,4},{7,5},{8,10},{9,11},{10,... | collective-permute-start | bytes 12296 | tf_op jit(solution)/shard_map/ppermute | solution.py:21
  12.6 0.3 collective-permute-start.2
  12.9 1.5 %collective-permute-start.5 = (bf16[1168,128]{1,0:T(8,128)(2,1)}, bf16[1168,128]{1,0:T(8,128)(2,1)S(1)}, u32[]{:S(2)}, u32[]{:S(2)}) collective-permute-start(bf16[1168,128]{1,0:T(8,128)(2,1)} %part_unit.1), channel_id=1, source_target_pairs={{0,4},{1,5},{2,6},{3,7},{4,0},{5,1},{6,2},{7,3},{8,12},{9,13},{10,... | collective-permute-start | bytes 897032 | tf_op jit(solution)/shard_map/ppermute | solution.py:31
  15.6 0.0 collective-permute-done.refs_2_
  15.7 0.1 collective-permute-start.6
  15.7 0.0 copy-done.1
  15.7 0.0 copy-done.2
  15.8 0.0 copy-start
  15.8 2.3 %copy-done = bf16[1536,1536]{1,0:T(8,128)(2,1)S(1)} copy-done((bf16[1536,1536]{1,0:T(8,128)(2,1)S(1)}, bf16[1536,1536]{1,0:T(8,128)(2,1)}, u32[]{:S(2)}) %copy-start) | copy-done | bytes 4718616
  18.1 3.2 %whole_unit.1 = (f32[384,1536]{1,0:T(8,128)S(1)}, bf16[384,1536]{1,0:T(8,128)(2,1)S(1)}, f32[384,128]{1,0:T(8,128)S(1)}, f32[384,128]{1,0:T(8,128)S(1)}, f32[8,128]{1,0:T(8,128)S(1)}) custom-call(s32[384]{0:T(512)S(1)} %copy-done.2, s32[1]{0:T(128)S(6)} %copy.10.filled, f32[1]{0:T(128)S(6)} %copy.12.scale, f32[1]{0:T(128)S(6)} %copy.13.shift, ...), custom_call_target="tpu_custom_call" | custom-call | flops 1811939328 | bytes 9437184 | tf_op jit(solution)/shard_map/whole_unit/pallas_call | solution.py:139
  21.3 0.0 collective-permute-done.1.refs_3_
  21.3 0.0 collective-permute-done.2.refs_4_
  21.3 0.0 collective-permute-done.3.refs_9_
  21.3 0.6 %collective-permute-start.4 = (bf16[1168,128]{1,0:T(8,128)(2,1)S(1)}, bf16[1168,128]{1,0:T(8,128)(2,1)S(1)}, u32[]{:S(2)}, u32[]{:S(2)}) collective-permute-start(bf16[1168,128]{1,0:T(8,128)(2,1)S(1)} %collective-permute-done.3.refs_9_), channel_id=1, source_target_pairs={{0,4},{1,5},{2,6},{3,7},{4,0},{5,1},{6,2},{7,3},{8,12},{9,13},{10,... | collective-permute-start | bytes 897032 | tf_op jit(solution)/shard_map/ppermute | solution.py:31
  21.9 3.3 %collective-permute-start.9 = (bf16[1168,128]{1,0:T(8,128)(2,1)S(1)}, bf16[1168,128]{1,0:T(8,128)(2,1)S(1)}, u32[]{:S(2)}, u32[]{:S(2)}) collective-permute-start(bf16[1168,128]{1,0:T(8,128)(2,1)S(1)} %collective-permute-done.3.refs_9_), channel_id=1, source_target_pairs={{0,8},{1,9},{2,10},{3,11},{4,12},{5,13},{6,14},{7,15},{8,0},{9,1},... | collective-permute-start | bytes 897032 | tf_op jit(solution)/shard_map/ppermute | solution.py:31
  25.2 0.0 collective-permute-done.5.refs_7_
  25.2 0.0 collective-permute-done.6.refs_8_
  25.2 1.0 %collective-permute-start.8 = (bf16[1168,128]{1,0:T(8,128)(2,1)S(1)}, bf16[1168,128]{1,0:T(8,128)(2,1)S(1)}, u32[]{:S(2)}, u32[]{:S(2)}) collective-permute-start(bf16[1168,128]{1,0:T(8,128)(2,1)S(1)} %collective-permute-done.6.refs_8_), channel_id=1, source_target_pairs={{0,4},{1,5},{2,6},{3,7},{4,0},{5,1},{6,2},{7,3},{8,12},{9,13},{10,... | collective-permute-start | bytes 897032 | tf_op jit(solution)/shard_map/ppermute | solution.py:31
  26.2 2.3 %pair_terms.5 = (f32[384,1536]{1,0:T(8,128)S(1)}, f32[8,128]{1,0:T(8,128)S(1)}) custom-call(f32[8,128]{1,0:T(8,128)S(1)} %get-tuple-element.27.refs_0_, s32[8,128]{1,0:T(8,128)S(1)} %broadcast_in_dim.9.refs_1_, s32[8,128]{1,0:T(8,128)S(1)} %collective-permute-done.refs_2_, s32[8,128]{1,0:T(8,128)S(1)} %collective-permute-done.1.refs_3_, ...), custom_call_target="tpu_custom_call" | custom-call | flops 679477248 | bytes 4718592 | tf_op jit(solution)/shard_map/pair_terms/pallas_call | solution.py:257
  28.5 2.8 %collective-permute-done.4.refs_8_ = bf16[1168,128]{1,0:T(8,128)(2,1)S(1)} collective-permute-done((bf16[1168,128]{1,0:T(8,128)(2,1)S(1)}, bf16[1168,128]{1,0:T(8,128)(2,1)S(1)}, u32[]{:S(2)}, u32[]{:S(2)}) %collective-permute-start.4) | collective-permute-done | bytes 299040 | tf_op jit(solution)/shard_map/ppermute | solution.py:31
  31.3 2.4 %collective-permute-start.7 = (bf16[1168,128]{1,0:T(8,128)(2,1)S(1)}, bf16[1168,128]{1,0:T(8,128)(2,1)S(1)}, u32[]{:S(2)}, u32[]{:S(2)}) collective-permute-start(bf16[1168,128]{1,0:T(8,128)(2,1)S(1)} %collective-permute-done.4.refs_8_), channel_id=1, source_target_pairs={{0,8},{1,9},{2,10},{3,11},{4,12},{5,13},{6,14},{7,15},{8,0},{9,1},... | collective-permute-start | bytes 897032 | tf_op jit(solution)/shard_map/ppermute | solution.py:31
  33.7 0.0 collective-permute-done.9.refs_7_
  33.7 1.9 %pair_terms.6 = (f32[384,1536]{1,0:T(8,128)S(1)}, f32[8,128]{1,0:T(8,128)S(1)}) custom-call(f32[8,128]{1,0:T(8,128)S(1)} %get-tuple-element.27.refs_0_, s32[8,128]{1,0:T(8,128)S(1)} %broadcast_in_dim.9.refs_1_, s32[8,128]{1,0:T(8,128)S(1)} %collective-permute-done.refs_2_, s32[8,128]{1,0:T(8,128)S(1)} %collective-permute-done.1.refs_3_, ...), custom_call_target="tpu_custom_call" | custom-call | flops 452984832 | bytes 4718592 | tf_op jit(solution)/shard_map/pair_terms/pallas_call | solution.py:257
  35.7 1.2 %collective-permute-done.8.refs_7_ = bf16[1168,128]{1,0:T(8,128)(2,1)S(1)} collective-permute-done((bf16[1168,128]{1,0:T(8,128)(2,1)S(1)}, bf16[1168,128]{1,0:T(8,128)(2,1)S(1)}, u32[]{:S(2)}, u32[]{:S(2)}) %collective-permute-start.8) | collective-permute-done | bytes 299040 | tf_op jit(solution)/shard_map/ppermute | solution.py:31
  36.9 1.5 %pair_terms.7 = (f32[384,1536]{1,0:T(8,128)S(1)}, f32[8,128]{1,0:T(8,128)S(1)}) custom-call(f32[8,128]{1,0:T(8,128)S(1)} %get-tuple-element.27.refs_0_, s32[8,128]{1,0:T(8,128)S(1)} %broadcast_in_dim.9.refs_1_, s32[8,128]{1,0:T(8,128)S(1)} %collective-permute-done.refs_2_, s32[8,128]{1,0:T(8,128)S(1)} %collective-permute-done.1.refs_3_, ...), custom_call_target="tpu_custom_call" | custom-call | flops 226492416 | bytes 4718592 | tf_op jit(solution)/shard_map/pair_terms/pallas_call | solution.py:257
  38.4 0.3 collective-permute-done.7.refs_7_
  38.7 1.2 %pair_terms.9 = (f32[200,768]{1,0:T(8,128)S(1)}, f32[200,768]{1,0:T(8,128)S(1)}) custom-call(f32[8,128]{1,0:T(8,128)S(1)} %get-tuple-element.27.refs_0_, s32[8,128]{1,0:T(8,128)S(1)} %broadcast_in_dim.9.refs_1_, s32[8,128]{1,0:T(8,128)S(1)} %collective-permute-done.refs_2_, s32[8,128]{1,0:T(8,128)S(1)} %collective-permute-done.1.refs_3_, ...), custom_call_target="tpu_custom_call" | custom-call | flops 113246208 | bytes 2359296 | tf_op jit(solution)/shard_map/pair_terms/pallas_call | solution.py:257
  39.9 0.1 collective-permute-start.11
  40.0 1.2 %pair_terms.8 = (f32[200,768]{1,0:T(8,128)S(1)}, f32[200,768]{1,0:T(8,128)S(1)}) custom-call(f32[8,128]{1,0:T(8,128)S(1)} %get-tuple-element.27.refs_0_, s32[8,128]{1,0:T(8,128)S(1)} %broadcast_in_dim.9.refs_1_, s32[8,128]{1,0:T(8,128)S(1)} %collective-permute-done.refs_2_, s32[8,128]{1,0:T(8,128)S(1)} %collective-permute-done.1.refs_3_, ...), custom_call_target="tpu_custom_call" | custom-call | flops 113246208 | bytes 2359296 | tf_op jit(solution)/shard_map/pair_terms/pallas_call | solution.py:257
  41.3 0.6 %collective-permute-start.10 = (f32[200,768]{1,0:T(8,128)S(1)}, f32[200,768]{1,0:T(8,128)S(1)}, u32[]{:S(2)}, u32[]{:S(2)}) collective-permute-start(f32[200,768]{1,0:T(8,128)S(1)} %get-tuple-element.43), channel_id=1, source_target_pairs={{0,1},{1,0},{2,3},{3,2},{4,5},{5,4},{6,7},{7,6},{8,9},{9,8},{10,11... | collective-permute-start | bytes 1843208 | tf_op jit(solution)/shard_map/ppermute | solution.py:21
  41.8 0.2 collective-permute-done.11.arrived
  42.0 0.1 combine.3
  42.1 1.6 %collective-permute-start.13 = (bf16[592,128]{1,0:T(8,128)(2,1)S(1)}, bf16[592,128]{1,0:T(8,128)(2,1)S(1)}, u32[]{:S(2)}, u32[]{:S(2)}) collective-permute-start(bf16[592,128]{1,0:T(8,128)(2,1)S(1)} %get-tuple-element.49), channel_id=1, source_target_pairs={{0,2},{1,3},{2,0},{3,1},{4,6},{5,7},{6,4},{7,5},{8,10},{9,11},{10,... | collective-permute-start | bytes 454664 | tf_op jit(solution)/shard_map/ppermute | solution.py:21
  43.7 0.0 collective-permute-done.10.arrived
  43.7 0.7 %combine.2 = (f32[200,384]{1,0:T(8,128)S(1)}, bf16[592,128]{1,0:T(8,128)(2,1)}) custom-call(f32[200,768]{1,0:T(8,128)S(1)} %get-tuple-element.42.keep, f32[200,768]{1,0:T(8,128)S(1)} %collective-permute-done.10.arrived), custom_call_target="tpu_custom_call" | custom-call | flops 147456 | bytes 1179648 | tf_op jit(solution)/shard_map/combine/pallas_call | solution.py:287
  44.4 1.4 %collective-permute-start.12 = (bf16[592,128]{1,0:T(8,128)(2,1)}, bf16[592,128]{1,0:T(8,128)(2,1)S(1)}, u32[]{:S(2)}, u32[]{:S(2)}) collective-permute-start(bf16[592,128]{1,0:T(8,128)(2,1)} %get-tuple-element.48), channel_id=1, source_target_pairs={{0,2},{1,3},{2,0},{3,1},{4,6},{5,7},{6,4},{7,5},{8,10},{9,11},{10,... | collective-permute-start | bytes 454664 | tf_op jit(solution)/shard_map/ppermute | solution.py:21
  45.8 0.7 %copy.9 = bf16[384,1536]{0,1:T(8,128)(2,1)S(1)} copy(bf16[384,1536]{1,0:T(8,128)(2,1)S(1)} %copy-done.1) | data formatting | bytes 2359296 | tf_op args[0]
  46.5 2.3 %collective-permute-done.13.arrived_b = bf16[592,128]{1,0:T(8,128)(2,1)S(1)} collective-permute-done((bf16[592,128]{1,0:T(8,128)(2,1)S(1)}, bf16[592,128]{1,0:T(8,128)(2,1)S(1)}, u32[]{:S(2)}, u32[]{:S(2)}) %collective-permute-start.13) | collective-permute-done | bytes 151584 | tf_op jit(solution)/shard_map/ppermute | solution.py:21
  48.8 2.6 %collective-permute-done.12.arrived_a = bf16[592,128]{1,0:T(8,128)(2,1)S(1)} collective-permute-done((bf16[592,128]{1,0:T(8,128)(2,1)}, bf16[592,128]{1,0:T(8,128)(2,1)S(1)}, u32[]{:S(2)}, u32[]{:S(2)}) %collective-permute-start.12) | collective-permute-done | bytes 151584 | tf_op jit(solution)/shard_map/ppermute | solution.py:21
  51.4 1.8 %gradient.1 = (f32[1536,384]{1,0:T(8,128)}, f32[1,1]{1,0:T(1,128)}) custom-call(f32[200,384]{1,0:T(8,128)S(1)} %get-tuple-element.44.own_a, f32[200,384]{1,0:T(8,128)S(1)} %get-tuple-element.47.own_b, bf16[592,128]{1,0:T(8,128)(2,1)S(1)} %collective-permute-done.12.arrived_a, bf16[592,128]{1,0:T(8,128)(2,1)S(1)} %collective-permute-done.13.arrived_b, ...), custom_call_target="tpu_custom_call" | custom-call | flops 452984832 | bytes 2359296 | tf_op jit(solution)/shard_map/gradient/pallas_call | solution.py:332
  (1 shorter events, 0.0 us)
Async XLA Ops:
  1.3 14.5 %copy-start.1 = (bf16[384,1536]{1,0:T(8,128)(2,1)S(1)}, bf16[384,1536]{1,0:T(8,128)(2,1)}, u32[]{:S(2)}) copy-start(bf16[384,1536]{1,0:T(8,128)(2,1)} %features.2) | copy-start | bytes 3538948
  1.3 14.5 %copy-start.2 = (s32[384]{0:T(512)S(1)}, s32[384]{0:T(512)}, u32[]{:S(2)}) copy-start(s32[384]{0:T(512)} %ids.3) | copy-start | bytes 4612
  5.1 16.2 %collective-permute-start.3 = (bf16[1168,128]{1,0:T(8,128)(2,1)}, bf16[1168,128]{1,0:T(8,128)(2,1)S(1)}, u32[]{:S(2)}, u32[]{:S(2)}) collective-permute-start(bf16[1168,128]{1,0:T(8,128)(2,1)} %part_unit.1), channel_id=1, source_target_pairs={{0,24},{1,25},{2,26},{3,27},{4,28},{5,29},{6,30},{7,31},{8,16},{9,... | collective-permute-start | bytes 897032 | tf_op jit(solution)/shard_map/ppermute | solution.py:31
  10.9 4.7 %collective-permute-start = (s32[8,128]{1,0:T(8,128)S(1)}, s32[8,128]{1,0:T(8,128)S(1)}, u32[]{:S(2)}, u32[]{:S(2)}) collective-permute-start(s32[8,128]{1,0:T(8,128)S(1)} %broadcast_in_dim.9.refs_1_), channel_id=1, source_target_pairs={{0,1},{1,0},{2,3},{3,2},{4,5},{5,4},{6,7},{7,6},{8,9},{9,8},{10,11... | collective-permute-start | bytes 12296 | tf_op jit(solution)/shard_map/ppermute | solution.py:21
  11.0 10.3 %collective-permute-start.1 = (s32[8,128]{1,0:T(8,128)S(1)}, s32[8,128]{1,0:T(8,128)S(1)}, u32[]{:S(2)}, u32[]{:S(2)}) collective-permute-start(s32[8,128]{1,0:T(8,128)S(1)} %broadcast_in_dim.9.refs_1_), channel_id=1, source_target_pairs={{0,2},{1,3},{2,0},{3,1},{4,6},{5,7},{6,4},{7,5},{8,10},{9,11},{10,... | collective-permute-start | bytes 12296 | tf_op jit(solution)/shard_map/ppermute | solution.py:21
  12.6 8.7 %collective-permute-start.2 = (s32[8,128]{1,0:T(8,128)S(1)}, s32[8,128]{1,0:T(8,128)S(1)}, u32[]{:S(2)}, u32[]{:S(2)}) collective-permute-start(s32[8,128]{1,0:T(8,128)S(1)} %broadcast_in_dim.9.refs_1_), channel_id=1, source_target_pairs={{0,3},{1,2},{2,1},{3,0},{4,7},{5,6},{6,5},{7,4},{8,11},{9,10},{10,... | collective-permute-start | bytes 12296 | tf_op jit(solution)/shard_map/ppermute | solution.py:21
  12.9 12.3 %collective-permute-start.5 = (bf16[1168,128]{1,0:T(8,128)(2,1)}, bf16[1168,128]{1,0:T(8,128)(2,1)S(1)}, u32[]{:S(2)}, u32[]{:S(2)}) collective-permute-start(bf16[1168,128]{1,0:T(8,128)(2,1)} %part_unit.1), channel_id=1, source_target_pairs={{0,4},{1,5},{2,6},{3,7},{4,0},{5,1},{6,2},{7,3},{8,12},{9,13},{10,... | collective-permute-start | bytes 897032 | tf_op jit(solution)/shard_map/ppermute | solution.py:31
  15.7 9.5 %collective-permute-start.6 = (bf16[1168,128]{1,0:T(8,128)(2,1)}, bf16[1168,128]{1,0:T(8,128)(2,1)S(1)}, u32[]{:S(2)}, u32[]{:S(2)}) collective-permute-start(bf16[1168,128]{1,0:T(8,128)(2,1)} %part_unit.1), channel_id=1, source_target_pairs={{0,8},{1,9},{2,10},{3,11},{4,12},{5,13},{6,14},{7,15},{8,0},{9,1},... | collective-permute-start | bytes 897032 | tf_op jit(solution)/shard_map/ppermute | solution.py:31
  15.8 2.3 %copy-start = (bf16[1536,1536]{1,0:T(8,128)(2,1)S(1)}, bf16[1536,1536]{1,0:T(8,128)(2,1)}, u32[]{:S(2)}) copy-start(bf16[1536,1536]{1,0:T(8,128)(2,1)} %matrix.3) | copy-start | bytes 14155780
  21.3 10.0 %collective-permute-start.4 = (bf16[1168,128]{1,0:T(8,128)(2,1)S(1)}, bf16[1168,128]{1,0:T(8,128)(2,1)S(1)}, u32[]{:S(2)}, u32[]{:S(2)}) collective-permute-start(bf16[1168,128]{1,0:T(8,128)(2,1)S(1)} %collective-permute-done.3.refs_9_), channel_id=1, source_target_pairs={{0,4},{1,5},{2,6},{3,7},{4,0},{5,1},{6,2},{7,3},{8,12},{9,13},{10,... | collective-permute-start | bytes 897032 | tf_op jit(solution)/shard_map/ppermute | solution.py:31
  21.9 11.8 %collective-permute-start.9 = (bf16[1168,128]{1,0:T(8,128)(2,1)S(1)}, bf16[1168,128]{1,0:T(8,128)(2,1)S(1)}, u32[]{:S(2)}, u32[]{:S(2)}) collective-permute-start(bf16[1168,128]{1,0:T(8,128)(2,1)S(1)} %collective-permute-done.3.refs_9_), channel_id=1, source_target_pairs={{0,8},{1,9},{2,10},{3,11},{4,12},{5,13},{6,14},{7,15},{8,0},{9,1},... | collective-permute-start | bytes 897032 | tf_op jit(solution)/shard_map/ppermute | solution.py:31
  25.2 11.7 %collective-permute-start.8 = (bf16[1168,128]{1,0:T(8,128)(2,1)S(1)}, bf16[1168,128]{1,0:T(8,128)(2,1)S(1)}, u32[]{:S(2)}, u32[]{:S(2)}) collective-permute-start(bf16[1168,128]{1,0:T(8,128)(2,1)S(1)} %collective-permute-done.6.refs_8_), channel_id=1, source_target_pairs={{0,4},{1,5},{2,6},{3,7},{4,0},{5,1},{6,2},{7,3},{8,12},{9,13},{10,... | collective-permute-start | bytes 897032 | tf_op jit(solution)/shard_map/ppermute | solution.py:31
  31.3 7.3 %collective-permute-start.7 = (bf16[1168,128]{1,0:T(8,128)(2,1)S(1)}, bf16[1168,128]{1,0:T(8,128)(2,1)S(1)}, u32[]{:S(2)}, u32[]{:S(2)}) collective-permute-start(bf16[1168,128]{1,0:T(8,128)(2,1)S(1)} %collective-permute-done.4.refs_8_), channel_id=1, source_target_pairs={{0,8},{1,9},{2,10},{3,11},{4,12},{5,13},{6,14},{7,15},{8,0},{9,1},... | collective-permute-start | bytes 897032 | tf_op jit(solution)/shard_map/ppermute | solution.py:31
  39.9 2.1 %collective-permute-start.11 = (f32[200,768]{1,0:T(8,128)S(1)}, f32[200,768]{1,0:T(8,128)S(1)}, u32[]{:S(2)}, u32[]{:S(2)}) collective-permute-start(f32[200,768]{1,0:T(8,128)S(1)} %get-tuple-element.46), channel_id=1, source_target_pairs={{0,1},{1,0},{2,3},{3,2},{4,5},{5,4},{6,7},{7,6},{8,9},{9,8},{10,11... | collective-permute-start | bytes 1843208 | tf_op jit(solution)/shard_map/ppermute | solution.py:21
  41.3 2.4 %collective-permute-start.10 = (f32[200,768]{1,0:T(8,128)S(1)}, f32[200,768]{1,0:T(8,128)S(1)}, u32[]{:S(2)}, u32[]{:S(2)}) collective-permute-start(f32[200,768]{1,0:T(8,128)S(1)} %get-tuple-element.43), channel_id=1, source_target_pairs={{0,1},{1,0},{2,3},{3,2},{4,5},{5,4},{6,7},{7,6},{8,9},{9,8},{10,11... | collective-permute-start | bytes 1843208 | tf_op jit(solution)/shard_map/ppermute | solution.py:21
  42.1 6.7 %collective-permute-start.13 = (bf16[592,128]{1,0:T(8,128)(2,1)S(1)}, bf16[592,128]{1,0:T(8,128)(2,1)S(1)}, u32[]{:S(2)}, u32[]{:S(2)}) collective-permute-start(bf16[592,128]{1,0:T(8,128)(2,1)S(1)} %get-tuple-element.49), channel_id=1, source_target_pairs={{0,2},{1,3},{2,0},{3,1},{4,6},{5,7},{6,4},{7,5},{8,10},{9,11},{10,... | collective-permute-start | bytes 454664 | tf_op jit(solution)/shard_map/ppermute | solution.py:21
  44.4 7.0 %collective-permute-start.12 = (bf16[592,128]{1,0:T(8,128)(2,1)}, bf16[592,128]{1,0:T(8,128)(2,1)S(1)}, u32[]{:S(2)}, u32[]{:S(2)}) collective-permute-start(bf16[592,128]{1,0:T(8,128)(2,1)} %get-tuple-element.48), channel_id=1, source_target_pairs={{0,2},{1,3},{2,0},{3,1},{4,6},{5,7},{6,4},{7,5},{8,10},{9,11},{10,... | collective-permute-start | bytes 454664 | tf_op jit(solution)/shard_map/ppermute | solution.py:21

commit v9 on v8

--- a/solution.py
+++ b/solution.py
@@ -85,10 +85,10 @@
     facts = jnp.zeros((FACTS, LANES), jnp.int32)
     for k, digit in enumerate((here & 255, here >> 8, count & 255, count >> 8)):
         facts = jnp.where(row == k, digit, facts)
-    length = multiply(copies, features_v, matrix_v, raw)
+    inverse = 1.0 / multiply(copies, features_v, matrix_v, raw)
     chunks = width // LANES
     for k in range(chunks):
-        value = raw[:, k * LANES : (k + 1) * LANES] / length
+        value = raw[:, k * LANES : (k + 1) * LANES] * inverse
         unit[k * rows : (k + 1) * rows] = value.astype(jnp.bfloat16)
     unit[chunks * rows :] = facts.astype(jnp.float32).astype(jnp.bfloat16)
 
@@ -119,7 +119,7 @@
     )(ids, filled, features, matrix)
 
 
-def whole_unit_kernel(ids, filled, scale, shift, features, matrix, unit, unit_bf, length, column, numbers, features_v, matrix_v, sems):
+def whole_unit_kernel(ids, filled, scale, shift, features, matrix, unit, unit_bf, inverse, column, numbers, features_v, matrix_v, sems):
     rows = unit.shape[0]
     copies = load(features, matrix, features_v, matrix_v, sems, 0, rows)
     column[...] = jnp.broadcast_to(ids[...].reshape(1, rows).astype(jnp.float32), (128, rows)).T
@@ -127,10 +127,11 @@
     numbers[1:2] = jnp.broadcast_to(shift[...].reshape(1, 1), (1, 128))
     numbers[2:3] = jnp.broadcast_to(filled[...].reshape(1, 1), (1, 128)).astype(jnp.float32)
     numbers[3:] = jnp.zeros((5, 128), jnp.float32)
-    norm = multiply(copies, features_v, matrix_v, unit)
-    length[...] = jnp.broadcast_to(norm, length.shape)
-    unit[...] = unit[...] / norm
-    unit_bf[...] = unit[...].astype(jnp.bfloat16)
+    factor = 1.0 / multiply(copies, features_v, matrix_v, unit)
+    inverse[...] = jnp.broadcast_to(factor, inverse.shape)
+    value = unit[...] * factor
+    unit[...] = value
+    unit_bf[...] = value.astype(jnp.bfloat16)
 
 
 def whole_unit(ids, filled, scale, shift, features, matrix):
@@ -170,7 +171,7 @@
     if not first:
         old_dunit, old_losses = refs.pop(0), refs.pop(0)
     if final:
-        unit, length = refs.pop(0), refs.pop(0)
+        unit, inverse = refs.pop(0), refs.pop(0)
         keep, send, stacked, total = refs
     else:
         total, losses_out, stacked = refs
@@ -225,12 +226,11 @@
         losses_out[...] = jnp.broadcast_to(losses, losses_out.shape)
         return
     along = jnp.sum(unit[here] * total[...], axis=1, keepdims=True)
-    total[...] = (total[...] - unit[here] * along) / length[here, :1]
     for k, other in enumerate((0, 2)):
-        at = pl.ds(pl.multiple_of(jnp.bitwise_xor(me, other) * step, 128), step)
-        keep[:rows, k * step : (k + 1) * step] = total[:, at]
-        at = pl.ds(pl.multiple_of(jnp.bitwise_xor(me, other + 1) * step, 128), step)
-        send[:rows, k * step : (k + 1) * step] = total[:, at]
+        for out, member in ((keep, other), (send, other + 1)):
+            at = pl.ds(pl.multiple_of(jnp.bitwise_xor(me, member) * step, 128), step)
+            value = (total[:, at] - unit[here, at] * along) * inverse[here, :1]
+            out[:rows, k * step : (k + 1) * step] = value
     keep[rows:, :] = jnp.zeros((8, 2 * step), jnp.float32)
     keep[rows : rows + 1, 0:128] = losses
     send[rows:, :] = jnp.zeros((8, 2 * step), jnp.float32)
@@ -360,7 +360,7 @@
     far = trade(mine, 6, 0)
     near = trade(mine, 1, 0)
     side = trade(mine, 2, 0)
-    unit, unit_bf, length, column, numbers = whole_unit(
+    unit, unit_bf, inverse, column, numbers = whole_unit(
         ids, filled, scale, shift, after(features, mine), matrix
     )
     others = [swap(mask, "group", k) for k in (1, 2, 3)]
@@ -384,7 +384,7 @@
             [last],
             ((5, 0, part, 0),),
             old=middle,
-            final=[unit, length],
+            final=[unit, inverse],
             window=window,
         )
         sent.append((keep, swap(send, "group", 1)))

time: 53.4 us -> 53.3 us (level)
  no operation moved by 1% of the time
where the time goes in v9:
time: 53.3 us; the launch traced here: 53.1 us
  starting transfers between devices  19.2 us (36%)
  Pallas kernels  17.8 us (33%)
  waiting for transfers between devices  9.68 us (18%)
  between operations  3.4 us (6%)
  local copies, waits for them, and re-layouts  3.07 us (6%)
    ppermute x7, starting transfers between devices, trade(): return lax.ppermute(block, AXES, route)  13.9 us
    pallas_call x5, Pallas kernels, pair_terms(): pl.pallas_call(functools.partial(pair_kernel, cuts, old is None, final is...  8.12 us
    ppermute x7, starting transfers between devices, swap(): return lax.ppermute(block, axis, [(i, i ^ mask) for i in range(count)])  5.37 us
    ppermute x7, waiting for transfers between devices, swap(): return lax.ppermute(block, axis, [(i, i ^ mask) for i in range(count)])  5.3 us
    ppermute x7, waiting for transfers between devices, trade(): return lax.ppermute(block, AXES, route)  4.38 us
    pallas_call x1, Pallas kernels, part_unit(): pl.pallas_call(part_unit_kernel, out_shape=jax.ShapeDtypeStruct((part * w...  3.83 us
    pallas_call x1, Pallas kernels, whole_unit(): pl.pallas_call(whole_unit_kernel, out_shape=[jax.ShapeDtypeStruct((rows,...  3.2 us
    unnamed x7, local copies, waits for them, and re-layouts  3.07 us
  transfers between devices with their start and end apart: 14, of which 6 were waited for; matrix products, arithmetic and copies ran while one was open for 1% of the time, Pallas kernels for 21%

profile of v9, /device:TPU:0, one launch (start us, length us, event | category | flops | bytes accessed | tf_op | source)
XLA Modules:
  0.0 53.1 jit_solution(7805711340571759730)
XLA Ops:
  1.3 0.0 copy-start.1
  1.3 0.0 copy-start.2
  1.3 3.8 %part_unit.1 = bf16[1168,128]{1,0:T(8,128)(2,1)} custom-call(s32[384]{0:T(512)} %ids.3, s32[1]{0:T(128)S(6)} %copy.10.filled, bf16[384,1536]{1,0:T(8,128)(2,1)} %features.2, bf16[1536,1536]{1,0:T(8,128)(2,1)} %matrix.3), custom_call_target="tpu_custom_call" | custom-call | flops 905969664 | bytes 4718592 | tf_op jit(solution)/shard_map/part_unit/pallas_call | solution.py:100
  5.1 5.1 %collective-permute-start.3 = (bf16[1168,128]{1,0:T(8,128)(2,1)}, bf16[1168,128]{1,0:T(8,128)(2,1)S(1)}, u32[]{:S(2)}, u32[]{:S(2)}) collective-permute-start(bf16[1168,128]{1,0:T(8,128)(2,1)} %part_unit.1), channel_id=1, source_target_pairs={{0,24},{1,25},{2,26},{3,27},{4,28},{5,29},{6,30},{7,31},{8,16},{9,... | collective-permute-start | bytes 897032 | tf_op jit(solution)/shard_map/ppermute | solution.py:31
  10.9 0.1 collective-permute-start
  11.0 1.6 %collective-permute-start.1 = (s32[8,128]{1,0:T(8,128)S(1)}, s32[8,128]{1,0:T(8,128)S(1)}, u32[]{:S(2)}, u32[]{:S(2)}) collective-permute-start(s32[8,128]{1,0:T(8,128)S(1)} %broadcast_in_dim.9.refs_1_), channel_id=1, source_target_pairs={{0,2},{1,3},{2,0},{3,1},{4,6},{5,7},{6,4},{7,5},{8,10},{9,11},{10,... | collective-permute-start | bytes 12296 | tf_op jit(solution)/shard_map/ppermute | solution.py:21
  12.6 0.3 collective-permute-start.2
  12.9 1.5 %collective-permute-start.5 = (bf16[1168,128]{1,0:T(8,128)(2,1)}, bf16[1168,128]{1,0:T(8,128)(2,1)S(1)}, u32[]{:S(2)}, u32[]{:S(2)}) collective-permute-start(bf16[1168,128]{1,0:T(8,128)(2,1)} %part_unit.1), channel_id=1, source_target_pairs={{0,4},{1,5},{2,6},{3,7},{4,0},{5,1},{6,2},{7,3},{8,12},{9,13},{10,... | collective-permute-start | bytes 897032 | tf_op jit(solution)/shard_map/ppermute | solution.py:31
  15.6 0.0 collective-permute-done.refs_2_
  15.7 0.1 collective-permute-start.6
  15.7 0.0 copy-done.1
  15.7 0.0 copy-done.2
  15.8 0.0 copy-start
  15.8 2.3 %copy-done = bf16[1536,1536]{1,0:T(8,128)(2,1)S(1)} copy-done((bf16[1536,1536]{1,0:T(8,128)(2,1)S(1)}, bf16[1536,1536]{1,0:T(8,128)(2,1)}, u32[]{:S(2)}) %copy-start) | copy-done | bytes 4718616
  18.1 3.2 %whole_unit.1 = (f32[384,1536]{1,0:T(8,128)S(1)}, bf16[384,1536]{1,0:T(8,128)(2,1)S(1)}, f32[384,128]{1,0:T(8,128)S(1)}, f32[384,128]{1,0:T(8,128)S(1)}, f32[8,128]{1,0:T(8,128)S(1)}) custom-call(s32[384]{0:T(512)S(1)} %copy-done.2, s32[1]{0:T(128)S(6)} %copy.10.filled, f32[1]{0:T(128)S(6)} %copy.12.scale, f32[1]{0:T(128)S(6)} %copy.13.shift, ...), custom_call_target="tpu_custom_call" | custom-call | flops 1811939328 | bytes 9437184 | tf_op jit(solution)/shard_map/whole_unit/pallas_call | solution.py:140
  21.3 0.0 collective-permute-done.1.refs_3_
  21.3 0.0 collective-permute-done.2.refs_4_
  21.3 0.0 collective-permute-done.3.refs_9_
  21.3 0.6 %collective-permute-start.4 = (bf16[1168,128]{1,0:T(8,128)(2,1)S(1)}, bf16[1168,128]{1,0:T(8,128)(2,1)S(1)}, u32[]{:S(2)}, u32[]{:S(2)}) collective-permute-start(bf16[1168,128]{1,0:T(8,128)(2,1)S(1)} %collective-permute-done.3.refs_9_), channel_id=1, source_target_pairs={{0,4},{1,5},{2,6},{3,7},{4,0},{5,1},{6,2},{7,3},{8,12},{9,13},{10,... | collective-permute-start | bytes 897032 | tf_op jit(solution)/shard_map/ppermute | solution.py:31
  21.9 3.2 %collective-permute-start.9 = (bf16[1168,128]{1,0:T(8,128)(2,1)S(1)}, bf16[1168,128]{1,0:T(8,128)(2,1)S(1)}, u32[]{:S(2)}, u32[]{:S(2)}) collective-permute-start(bf16[1168,128]{1,0:T(8,128)(2,1)S(1)} %collective-permute-done.3.refs_9_), channel_id=1, source_target_pairs={{0,8},{1,9},{2,10},{3,11},{4,12},{5,13},{6,14},{7,15},{8,0},{9,1},... | collective-permute-start | bytes 897032 | tf_op jit(solution)/shard_map/ppermute | solution.py:31
  25.2 0.0 collective-permute-done.5.refs_7_
  25.2 0.0 collective-permute-done.6.refs_8_
  25.2 1.0 %collective-permute-start.8 = (bf16[1168,128]{1,0:T(8,128)(2,1)S(1)}, bf16[1168,128]{1,0:T(8,128)(2,1)S(1)}, u32[]{:S(2)}, u32[]{:S(2)}) collective-permute-start(bf16[1168,128]{1,0:T(8,128)(2,1)S(1)} %collective-permute-done.6.refs_8_), channel_id=1, source_target_pairs={{0,4},{1,5},{2,6},{3,7},{4,0},{5,1},{6,2},{7,3},{8,12},{9,13},{10,... | collective-permute-start | bytes 897032 | tf_op jit(solution)/shard_map/ppermute | solution.py:31
  26.2 2.3 %pair_terms.5 = (f32[384,1536]{1,0:T(8,128)S(1)}, f32[8,128]{1,0:T(8,128)S(1)}) custom-call(f32[8,128]{1,0:T(8,128)S(1)} %get-tuple-element.27.refs_0_, s32[8,128]{1,0:T(8,128)S(1)} %broadcast_in_dim.9.refs_1_, s32[8,128]{1,0:T(8,128)S(1)} %collective-permute-done.refs_2_, s32[8,128]{1,0:T(8,128)S(1)} %collective-permute-done.1.refs_3_, ...), custom_call_target="tpu_custom_call" | custom-call | flops 679477248 | bytes 4718592 | tf_op jit(solution)/shard_map/pair_terms/pallas_call | solution.py:257
  28.5 2.9 %collective-permute-done.4.refs_8_ = bf16[1168,128]{1,0:T(8,128)(2,1)S(1)} collective-permute-done((bf16[1168,128]{1,0:T(8,128)(2,1)S(1)}, bf16[1168,128]{1,0:T(8,128)(2,1)S(1)}, u32[]{:S(2)}, u32[]{:S(2)}) %collective-permute-start.4) | collective-permute-done | bytes 299040 | tf_op jit(solution)/shard_map/ppermute | solution.py:31
  31.4 2.4 %collective-permute-start.7 = (bf16[1168,128]{1,0:T(8,128)(2,1)S(1)}, bf16[1168,128]{1,0:T(8,128)(2,1)S(1)}, u32[]{:S(2)}, u32[]{:S(2)}) collective-permute-start(bf16[1168,128]{1,0:T(8,128)(2,1)S(1)} %collective-permute-done.4.refs_8_), channel_id=1, source_target_pairs={{0,8},{1,9},{2,10},{3,11},{4,12},{5,13},{6,14},{7,15},{8,0},{9,1},... | collective-permute-start | bytes 897032 | tf_op jit(solution)/shard_map/ppermute | solution.py:31
  33.7 0.0 collective-permute-done.9.refs_7_
  33.7 1.9 %pair_terms.6 = (f32[384,1536]{1,0:T(8,128)S(1)}, f32[8,128]{1,0:T(8,128)S(1)}) custom-call(f32[8,128]{1,0:T(8,128)S(1)} %get-tuple-element.27.refs_0_, s32[8,128]{1,0:T(8,128)S(1)} %broadcast_in_dim.9.refs_1_, s32[8,128]{1,0:T(8,128)S(1)} %collective-permute-done.refs_2_, s32[8,128]{1,0:T(8,128)S(1)} %collective-permute-done.1.refs_3_, ...), custom_call_target="tpu_custom_call" | custom-call | flops 452984832 | bytes 4718592 | tf_op jit(solution)/shard_map/pair_terms/pallas_call | solution.py:257
  35.7 1.2 %collective-permute-done.8.refs_7_ = bf16[1168,128]{1,0:T(8,128)(2,1)S(1)} collective-permute-done((bf16[1168,128]{1,0:T(8,128)(2,1)S(1)}, bf16[1168,128]{1,0:T(8,128)(2,1)S(1)}, u32[]{:S(2)}, u32[]{:S(2)}) %collective-permute-start.8) | collective-permute-done | bytes 299040 | tf_op jit(solution)/shard_map/ppermute | solution.py:31
  36.9 1.5 %pair_terms.7 = (f32[384,1536]{1,0:T(8,128)S(1)}, f32[8,128]{1,0:T(8,128)S(1)}) custom-call(f32[8,128]{1,0:T(8,128)S(1)} %get-tuple-element.27.refs_0_, s32[8,128]{1,0:T(8,128)S(1)} %broadcast_in_dim.9.refs_1_, s32[8,128]{1,0:T(8,128)S(1)} %collective-permute-done.refs_2_, s32[8,128]{1,0:T(8,128)S(1)} %collective-permute-done.1.refs_3_, ...), custom_call_target="tpu_custom_call" | custom-call | flops 226492416 | bytes 4718592 | tf_op jit(solution)/shard_map/pair_terms/pallas_call | solution.py:257
  38.4 0.3 collective-permute-done.7.refs_7_
  38.7 1.2 %pair_terms.9 = (f32[200,768]{1,0:T(8,128)S(1)}, f32[200,768]{1,0:T(8,128)S(1)}) custom-call(f32[8,128]{1,0:T(8,128)S(1)} %get-tuple-element.27.refs_0_, s32[8,128]{1,0:T(8,128)S(1)} %broadcast_in_dim.9.refs_1_, s32[8,128]{1,0:T(8,128)S(1)} %collective-permute-done.refs_2_, s32[8,128]{1,0:T(8,128)S(1)} %collective-permute-done.1.refs_3_, ...), custom_call_target="tpu_custom_call" | custom-call | flops 113246208 | bytes 2359296 | tf_op jit(solution)/shard_map/pair_terms/pallas_call | solution.py:257
  39.9 0.1 collective-permute-start.11
  40.0 1.2 %pair_terms.8 = (f32[200,768]{1,0:T(8,128)S(1)}, f32[200,768]{1,0:T(8,128)S(1)}) custom-call(f32[8,128]{1,0:T(8,128)S(1)} %get-tuple-element.27.refs_0_, s32[8,128]{1,0:T(8,128)S(1)} %broadcast_in_dim.9.refs_1_, s32[8,128]{1,0:T(8,128)S(1)} %collective-permute-done.refs_2_, s32[8,128]{1,0:T(8,128)S(1)} %collective-permute-done.1.refs_3_, ...), custom_call_target="tpu_custom_call" | custom-call | flops 113246208 | bytes 2359296 | tf_op jit(solution)/shard_map/pair_terms/pallas_call | solution.py:257
  41.1 0.5 %collective-permute-start.10 = (f32[200,768]{1,0:T(8,128)S(1)}, f32[200,768]{1,0:T(8,128)S(1)}, u32[]{:S(2)}, u32[]{:S(2)}) collective-permute-start(f32[200,768]{1,0:T(8,128)S(1)} %get-tuple-element.43), channel_id=1, source_target_pairs={{0,1},{1,0},{2,3},{3,2},{4,5},{5,4},{6,7},{7,6},{8,9},{9,8},{10,11... | collective-permute-start | bytes 1843208 | tf_op jit(solution)/shard_map/ppermute | solution.py:21
  41.7 0.3 collective-permute-done.11.arrived
  42.0 0.1 combine.3
  42.1 1.6 %collective-permute-start.13 = (bf16[592,128]{1,0:T(8,128)(2,1)S(1)}, bf16[592,128]{1,0:T(8,128)(2,1)S(1)}, u32[]{:S(2)}, u32[]{:S(2)}) collective-permute-start(bf16[592,128]{1,0:T(8,128)(2,1)S(1)} %get-tuple-element.49), channel_id=1, source_target_pairs={{0,2},{1,3},{2,0},{3,1},{4,6},{5,7},{6,4},{7,5},{8,10},{9,11},{10,... | collective-permute-start | bytes 454664 | tf_op jit(solution)/shard_map/ppermute | solution.py:21
  43.6 0.0 collective-permute-done.10.arrived
  43.6 0.7 %combine.2 = (f32[200,384]{1,0:T(8,128)S(1)}, bf16[592,128]{1,0:T(8,128)(2,1)}) custom-call(f32[200,768]{1,0:T(8,128)S(1)} %get-tuple-element.42.keep, f32[200,768]{1,0:T(8,128)S(1)} %collective-permute-done.10.arrived), custom_call_target="tpu_custom_call" | custom-call | flops 147456 | bytes 1179648 | tf_op jit(solution)/shard_map/combine/pallas_call | solution.py:287
  44.4 1.2 %collective-permute-start.12 = (bf16[592,128]{1,0:T(8,128)(2,1)}, bf16[592,128]{1,0:T(8,128)(2,1)S(1)}, u32[]{:S(2)}, u32[]{:S(2)}) collective-permute-start(bf16[592,128]{1,0:T(8,128)(2,1)} %get-tuple-element.48), channel_id=1, source_target_pairs={{0,2},{1,3},{2,0},{3,1},{4,6},{5,7},{6,4},{7,5},{8,10},{9,11},{10,... | collective-permute-start | bytes 454664 | tf_op jit(solution)/shard_map/ppermute | solution.py:21
  45.6 0.7 %copy.9 = bf16[384,1536]{0,1:T(8,128)(2,1)S(1)} copy(bf16[384,1536]{1,0:T(8,128)(2,1)S(1)} %copy-done.1) | data formatting | bytes 2359296 | tf_op args[0]
  46.4 2.5 %collective-permute-done.13.arrived_b = bf16[592,128]{1,0:T(8,128)(2,1)S(1)} collective-permute-done((bf16[592,128]{1,0:T(8,128)(2,1)S(1)}, bf16[592,128]{1,0:T(8,128)(2,1)S(1)}, u32[]{:S(2)}, u32[]{:S(2)}) %collective-permute-start.13) | collective-permute-done | bytes 151584 | tf_op jit(solution)/shard_map/ppermute | solution.py:21
  48.9 2.4 %collective-permute-done.12.arrived_a = bf16[592,128]{1,0:T(8,128)(2,1)S(1)} collective-permute-done((bf16[592,128]{1,0:T(8,128)(2,1)}, bf16[592,128]{1,0:T(8,128)(2,1)S(1)}, u32[]{:S(2)}, u32[]{:S(2)}) %collective-permute-start.12) | collective-permute-done | bytes 151584 | tf_op jit(solution)/shard_map/ppermute | solution.py:21
  51.3 1.8 %gradient.1 = (f32[1536,384]{1,0:T(8,128)}, f32[1,1]{1,0:T(1,128)}) custom-call(f32[200,384]{1,0:T(8,128)S(1)} %get-tuple-element.44.own_a, f32[200,384]{1,0:T(8,128)S(1)} %get-tuple-element.47.own_b, bf16[592,128]{1,0:T(8,128)(2,1)S(1)} %collective-permute-done.12.arrived_a, bf16[592,128]{1,0:T(8,128)(2,1)S(1)} %collective-permute-done.13.arrived_b, ...), custom_call_target="tpu_custom_call" | custom-call | flops 452984832 | bytes 2359296 | tf_op jit(solution)/shard_map/gradient/pallas_call | solution.py:332
  (1 shorter events, 0.0 us)
Async XLA Ops:
  1.3 14.5 %copy-start.1 = (bf16[384,1536]{1,0:T(8,128)(2,1)S(1)}, bf16[384,1536]{1,0:T(8,128)(2,1)}, u32[]{:S(2)}) copy-start(bf16[384,1536]{1,0:T(8,128)(2,1)} %features.2) | copy-start | bytes 3538948
  1.3 14.5 %copy-start.2 = (s32[384]{0:T(512)S(1)}, s32[384]{0:T(512)}, u32[]{:S(2)}) copy-start(s32[384]{0:T(512)} %ids.3) | copy-start | bytes 4612
  5.1 16.2 %collective-permute-start.3 = (bf16[1168,128]{1,0:T(8,128)(2,1)}, bf16[1168,128]{1,0:T(8,128)(2,1)S(1)}, u32[]{:S(2)}, u32[]{:S(2)}) collective-permute-start(bf16[1168,128]{1,0:T(8,128)(2,1)} %part_unit.1), channel_id=1, source_target_pairs={{0,24},{1,25},{2,26},{3,27},{4,28},{5,29},{6,30},{7,31},{8,16},{9,... | collective-permute-start | bytes 897032 | tf_op jit(solution)/shard_map/ppermute | solution.py:31
  10.9 4.7 %collective-permute-start = (s32[8,128]{1,0:T(8,128)S(1)}, s32[8,128]{1,0:T(8,128)S(1)}, u32[]{:S(2)}, u32[]{:S(2)}) collective-permute-start(s32[8,128]{1,0:T(8,128)S(1)} %broadcast_in_dim.9.refs_1_), channel_id=1, source_target_pairs={{0,1},{1,0},{2,3},{3,2},{4,5},{5,4},{6,7},{7,6},{8,9},{9,8},{10,11... | collective-permute-start | bytes 12296 | tf_op jit(solution)/shard_map/ppermute | solution.py:21
  11.0 10.3 %collective-permute-start.1 = (s32[8,128]{1,0:T(8,128)S(1)}, s32[8,128]{1,0:T(8,128)S(1)}, u32[]{:S(2)}, u32[]{:S(2)}) collective-permute-start(s32[8,128]{1,0:T(8,128)S(1)} %broadcast_in_dim.9.refs_1_), channel_id=1, source_target_pairs={{0,2},{1,3},{2,0},{3,1},{4,6},{5,7},{6,4},{7,5},{8,10},{9,11},{10,... | collective-permute-start | bytes 12296 | tf_op jit(solution)/shard_map/ppermute | solution.py:21
  12.6 8.7 %collective-permute-start.2 = (s32[8,128]{1,0:T(8,128)S(1)}, s32[8,128]{1,0:T(8,128)S(1)}, u32[]{:S(2)}, u32[]{:S(2)}) collective-permute-start(s32[8,128]{1,0:T(8,128)S(1)} %broadcast_in_dim.9.refs_1_), channel_id=1, source_target_pairs={{0,3},{1,2},{2,1},{3,0},{4,7},{5,6},{6,5},{7,4},{8,11},{9,10},{10,... | collective-permute-start | bytes 12296 | tf_op jit(solution)/shard_map/ppermute | solution.py:21
  12.9 12.3 %collective-permute-start.5 = (bf16[1168,128]{1,0:T(8,128)(2,1)}, bf16[1168,128]{1,0:T(8,128)(2,1)S(1)}, u32[]{:S(2)}, u32[]{:S(2)}) collective-permute-start(bf16[1168,128]{1,0:T(8,128)(2,1)} %part_unit.1), channel_id=1, source_target_pairs={{0,4},{1,5},{2,6},{3,7},{4,0},{5,1},{6,2},{7,3},{8,12},{9,13},{10,... | collective-permute-start | bytes 897032 | tf_op jit(solution)/shard_map/ppermute | solution.py:31
  15.7 9.5 %collective-permute-start.6 = (bf16[1168,128]{1,0:T(8,128)(2,1)}, bf16[1168,128]{1,0:T(8,128)(2,1)S(1)}, u32[]{:S(2)}, u32[]{:S(2)}) collective-permute-start(bf16[1168,128]{1,0:T(8,128)(2,1)} %part_unit.1), channel_id=1, source_target_pairs={{0,8},{1,9},{2,10},{3,11},{4,12},{5,13},{6,14},{7,15},{8,0},{9,1},... | collective-permute-start | bytes 897032 | tf_op jit(solution)/shard_map/ppermute | solution.py:31
  15.8 2.3 %copy-start = (bf16[1536,1536]{1,0:T(8,128)(2,1)S(1)}, bf16[1536,1536]{1,0:T(8,128)(2,1)}, u32[]{:S(2)}) copy-start(bf16[1536,1536]{1,0:T(8,128)(2,1)} %matrix.3) | copy-start | bytes 14155780
  21.3 10.0 %collective-permute-start.4 = (bf16[1168,128]{1,0:T(8,128)(2,1)S(1)}, bf16[1168,128]{1,0:T(8,128)(2,1)S(1)}, u32[]{:S(2)}, u32[]{:S(2)}) collective-permute-start(bf16[1168,128]{1,0:T(8,128)(2,1)S(1)} %collective-permute-done.3.refs_9_), channel_id=1, source_target_pairs={{0,4},{1,5},{2,6},{3,7},{4,0},{5,1},{6,2},{7,3},{8,12},{9,13},{10,... | collective-permute-start | bytes 897032 | tf_op jit(solution)/shard_map/ppermute | solution.py:31
  21.9 11.8 %collective-permute-start.9 = (bf16[1168,128]{1,0:T(8,128)(2,1)S(1)}, bf16[1168,128]{1,0:T(8,128)(2,1)S(1)}, u32[]{:S(2)}, u32[]{:S(2)}) collective-permute-start(bf16[1168,128]{1,0:T(8,128)(2,1)S(1)} %collective-permute-done.3.refs_9_), channel_id=1, source_target_pairs={{0,8},{1,9},{2,10},{3,11},{4,12},{5,13},{6,14},{7,15},{8,0},{9,1},... | collective-permute-start | bytes 897032 | tf_op jit(solution)/shard_map/ppermute | solution.py:31
  25.2 11.7 %collective-permute-start.8 = (bf16[1168,128]{1,0:T(8,128)(2,1)S(1)}, bf16[1168,128]{1,0:T(8,128)(2,1)S(1)}, u32[]{:S(2)}, u32[]{:S(2)}) collective-permute-start(bf16[1168,128]{1,0:T(8,128)(2,1)S(1)} %collective-permute-done.6.refs_8_), channel_id=1, source_target_pairs={{0,4},{1,5},{2,6},{3,7},{4,0},{5,1},{6,2},{7,3},{8,12},{9,13},{10,... | collective-permute-start | bytes 897032 | tf_op jit(solution)/shard_map/ppermute | solution.py:31
  31.4 7.3 %collective-permute-start.7 = (bf16[1168,128]{1,0:T(8,128)(2,1)S(1)}, bf16[1168,128]{1,0:T(8,128)(2,1)S(1)}, u32[]{:S(2)}, u32[]{:S(2)}) collective-permute-start(bf16[1168,128]{1,0:T(8,128)(2,1)S(1)} %collective-permute-done.4.refs_8_), channel_id=1, source_target_pairs={{0,8},{1,9},{2,10},{3,11},{4,12},{5,13},{6,14},{7,15},{8,0},{9,1},... | collective-permute-start | bytes 897032 | tf_op jit(solution)/shard_map/ppermute | solution.py:31
  39.9 2.1 %collective-permute-start.11 = (f32[200,768]{1,0:T(8,128)S(1)}, f32[200,768]{1,0:T(8,128)S(1)}, u32[]{:S(2)}, u32[]{:S(2)}) collective-permute-start(f32[200,768]{1,0:T(8,128)S(1)} %get-tuple-element.46), channel_id=1, source_target_pairs={{0,1},{1,0},{2,3},{3,2},{4,5},{5,4},{6,7},{7,6},{8,9},{9,8},{10,11... | collective-permute-start | bytes 1843208 | tf_op jit(solution)/shard_map/ppermute | solution.py:21
  41.1 2.5 %collective-permute-start.10 = (f32[200,768]{1,0:T(8,128)S(1)}, f32[200,768]{1,0:T(8,128)S(1)}, u32[]{:S(2)}, u32[]{:S(2)}) collective-permute-start(f32[200,768]{1,0:T(8,128)S(1)} %get-tuple-element.43), channel_id=1, source_target_pairs={{0,1},{1,0},{2,3},{3,2},{4,5},{5,4},{6,7},{7,6},{8,9},{9,8},{10,11... | collective-permute-start | bytes 1843208 | tf_op jit(solution)/shard_map/ppermute | solution.py:21
  42.1 6.8 %collective-permute-start.13 = (bf16[592,128]{1,0:T(8,128)(2,1)S(1)}, bf16[592,128]{1,0:T(8,128)(2,1)S(1)}, u32[]{:S(2)}, u32[]{:S(2)}) collective-permute-start(bf16[592,128]{1,0:T(8,128)(2,1)S(1)} %get-tuple-element.49), channel_id=1, source_target_pairs={{0,2},{1,3},{2,0},{3,1},{4,6},{5,7},{6,4},{7,5},{8,10},{9,11},{10,... | collective-permute-start | bytes 454664 | tf_op jit(solution)/shard_map/ppermute | solution.py:21
  44.4 7.0 %collective-permute-start.12 = (bf16[592,128]{1,0:T(8,128)(2,1)}, bf16[592,128]{1,0:T(8,128)(2,1)S(1)}, u32[]{:S(2)}, u32[]{:S(2)}) collective-permute-start(bf16[592,128]{1,0:T(8,128)(2,1)} %get-tuple-element.48), channel_id=1, source_target_pairs={{0,2},{1,3},{2,0},{3,1},{4,6},{5,7},{6,4},{7,5},{8,10},{9,11},{10,... | collective-permute-start | bytes 454664 | tf_op jit(solution)/shard_map/ppermute | solution.py:21
